TPU v7x, 32 devices: a whole 2x2x4 slice. The times are simulated.
32 devices in a mesh: blk: 4 (over y, x), dp: 8 (over z, core).
Axes of the slice: x: 2, y: 2, z: 4, core: 2. Of those that a mesh axis runs over, the one named last changes fastest.
Arguments:
- inputs: bfloat16 [8, 1024, 768], P('dp', 'blk'), may hold values from -6 to 6
- condition: float32 [8, 128], P('dp'), may hold values from -6 to 6
- prefix: int32 [8], P('dp'), may hold values from 1 to 1023
- mask_embed: bfloat16 [768], replicated, may hold values from -6 to 6
- adaptive_weight: bfloat16 [2, 128, 4608], replicated, may hold values from -0.25 to 0.25
- adaptive_bias: bfloat16 [2, 4608], replicated, may hold values from -3 to 3
- triple_weight: bfloat16 [2, 768, 2304], replicated, may hold values from -0.21875 to 0.21875
- triple_bias: bfloat16 [2, 2304], replicated, may hold values from -3 to 3
- output_weight: bfloat16 [2, 768, 768], replicated, may hold values from -3.5 to 3.5
- output_bias: bfloat16 [2, 768], replicated, may hold values from -3 to 3
- expand_weight: bfloat16 [2, 768, 3072], replicated, may hold values from -0.21875 to 0.21875
- expand_bias: bfloat16 [2, 3072], replicated, may hold values from -3 to 3
- shrink_weight: bfloat16 [2, 3072, 768], replicated, may hold values from -0.109375 to 0.109375
- shrink_bias: bfloat16 [2, 768], replicated, may hold values from -3 to 3
- cotangent: bfloat16 [8, 1024, 768], P('dp', 'blk'), may hold values from -6 to 6
Outputs:
- outputs: bfloat16 [8, 1024, 768], P('dp', 'blk')
- input_gradient: float32 [8, 1024, 768], P('dp', 'blk')
- condition_gradient: float32 [8, 128], P('dp')
- mask_gradient: float32 [768], P(('blk', 'dp'))
- adaptive_weight_gradient: float32 [2, 128, 4608], P(None, ('blk', 'dp'))
- adaptive_bias_gradient: float32 [2, 4608], P(None, ('blk', 'dp'))
- triple_weight_gradient: float32 [2, 768, 2304], P(None, ('blk', 'dp'))
- triple_bias_gradient: float32 [2, 2304], P(None, ('blk', 'dp'))
- output_weight_gradient: float32 [2, 768, 768], P(None, ('blk', 'dp'))
- output_bias_gradient: float32 [2, 768], P(None, ('blk', 'dp'))
- expand_weight_gradient: float32 [2, 768, 3072], P(None, ('blk', 'dp'))
- expand_bias_gradient: float32 [2, 3072], P(None, ('blk', 'dp'))
- shrink_weight_gradient: float32 [2, 3072, 768], P(None, ('blk', 'dp'))
- shrink_bias_gradient: float32 [2, 768], P(None, ('blk', 'dp'))
All inputs are finite; a program needn't handle non-finite values.
Results may differ from a plain program's by a relative error of at most 0.025.
Values may be sent and summed in bfloat16 or wider, within the bound.
No kernel may reach another device: no remote copies, remote signals or barrier semaphores. Data moves between devices by JAX's collectives and lax.ppermute only.
A program may use at most 256 MiB of HBM per device.

v0:
```python
import math

import jax
import jax.numpy as jnp
from jax import lax
from jax.sharding import PartitionSpec as P

HEADS = 12
HEAD_DIM = 64
LAYERS = 2


HIGHEST = lax.Precision.HIGHEST
EPSILON = 1e-06


def modulate(residual, shift, scaling):
    average = jnp.mean(residual, -1, keepdims=True)
    centered = residual - average
    variance = jnp.mean(centered * centered, -1, keepdims=True)
    return centered * lax.rsqrt(variance + EPSILON) * (1.0 + scaling) + shift


def gelu_tanh(values):
    return jax.nn.gelu(values, approximate=True)


def tables(offset, row_count, head_dim):
    half_dim = head_dim // 2
    position = (offset + jnp.arange(row_count, dtype=jnp.int32)).astype(jnp.float32)
    frequency = jnp.exp(
        jnp.arange(half_dim, dtype=jnp.float32) * (-2.0 * math.log(10000.0) / head_dim)
    )
    angles = position[:, None] * frequency[None, :]
    return (jnp.cos(angles)[:, None, :], jnp.sin(angles)[:, None, :])


def rotate(vectors, cosine, sine_table):
    half_dim = vectors.shape[-1] // 2
    front_half = vectors[..., :half_dim]
    back_half = vectors[..., half_dim:]
    return jnp.concatenate(
        [
            front_half * cosine - back_half * sine_table,
            back_half * cosine + front_half * sine_table,
        ],
        -1,
    )


def unrotate(gradient, cosine, sine_table):
    half_dim = gradient.shape[-1] // 2
    front_half = gradient[..., :half_dim]
    back_half = gradient[..., half_dim:]
    return jnp.concatenate(
        [
            front_half * cosine + back_half * sine_table,
            back_half * cosine - front_half * sine_table,
        ],
        -1,
    )


def split_einsum(form, float_left, low_right):
    upper = float_left.astype(jnp.bfloat16)
    lower = (float_left - upper.astype(jnp.float32)).astype(jnp.bfloat16)
    first = jnp.einsum(form, upper, low_right, preferred_element_type=jnp.float32)
    return first + jnp.einsum(form, lower, low_right, preferred_element_type=jnp.float32)


def fold_keys(queries, scaling):

    def absorb(carried, key_piece, offset):
        key_flat, value_flat = key_piece
        piece_rows = key_flat.shape[0]
        block_rows = math.gcd(piece_rows, 512)
        key_blocks = key_flat.reshape(piece_rows // block_rows, block_rows, HEADS, HEAD_DIM)
        value_blocks = value_flat.reshape(piece_rows // block_rows, block_rows, HEADS, HEAD_DIM)

        def absorb_inner(running, block_pair):
            running_max, running_sum, weighted = running
            key_block, value_block = block_pair
            scores = (
                jnp.einsum("qhd,khd->hqk", queries, key_block, preferred_element_type=jnp.float32)
                * scaling
            )
            new_max = jnp.maximum(running_max, jnp.max(scores, -1))
            weights = jnp.exp(scores - new_max[..., None])
            factor = jnp.exp(running_max - new_max)
            running_sum = running_sum * factor + jnp.sum(weights, -1)
            weighted = weighted * factor[..., None] + split_einsum(
                "hqk,khd->hqd", weights, value_block
            )
            return ((new_max, running_sum, weighted), None)

        carried, _ = lax.scan(absorb_inner, carried, (key_blocks, value_blocks))
        return carried

    return absorb


def attend_back(queries, key_all, value_all, out_gradient, attended_f, log_total, scaling):
    row_count = queries.shape[0]
    all_rows = key_all.shape[0]
    block_rows = math.gcd(all_rows, 512)
    key_blocks = key_all.reshape(all_rows // block_rows, block_rows, HEADS, HEAD_DIM)
    value_blocks = value_all.reshape(all_rows // block_rows, block_rows, HEADS, HEAD_DIM)
    out_float = out_gradient.astype(jnp.float32)
    row_delta = jnp.transpose(jnp.sum(out_float * attended_f, -1), (1, 0))

    def attend_inner(query_grad, block_pair):
        key_block, value_block = block_pair
        scores = (
            jnp.einsum("qhd,khd->hqk", queries, key_block, preferred_element_type=jnp.float32)
            * scaling
        )
        probs = jnp.exp(scores - log_total[..., None])
        prob_grad = jnp.einsum(
            "qhd,khd->hqk", out_gradient, value_block, preferred_element_type=jnp.float32
        )
        score_grad = (probs * (prob_grad - row_delta[..., None])).astype(jnp.bfloat16)
        query_grad = query_grad + jnp.einsum(
            "hqk,khd->qhd", score_grad, key_block, preferred_element_type=jnp.float32
        )
        key_grad = (
            jnp.einsum("hqk,qhd->khd", score_grad, queries, preferred_element_type=jnp.float32)
            * scaling
        )
        value_grad = split_einsum("hqk,qhd->khd", probs, out_gradient)
        return (query_grad, (key_grad, value_grad))

    start_grad = jnp.zeros((row_count, HEADS, HEAD_DIM), jnp.float32)
    query_grad, (key_grads, value_grads) = lax.scan(
        attend_inner, start_grad, (key_blocks, value_blocks)
    )
    width = HEADS * HEAD_DIM
    return (
        query_grad * scaling,
        key_grads.reshape(all_rows, width),
        value_grads.reshape(all_rows, width),
    )


def forward_layer(residual, modulation, layer_index, weights, cosine, sine_table, scaling):
    (
        adaptive_weight,
        adaptive_bias,
        triple_weight,
        triple_bias,
        output_weight,
        output_bias,
        expand_weight,
        expand_bias,
        shrink_weight,
        shrink_bias,
    ) = weights
    row_count, width = residual.shape
    pieces = [modulation[number * width : (number + 1) * width] for number in range(6)]
    shift_attn, scale_attn, gate_attn, shift_mlp, scale_mlp, gate_mlp = pieces
    normed = modulate(residual, shift_attn, scale_attn).astype(jnp.bfloat16)
    mixed = jnp.dot(
        normed, triple_weight[layer_index], preferred_element_type=jnp.float32
    ) + triple_bias[layer_index].astype(jnp.float32)
    head_shape = (row_count, HEADS, HEAD_DIM)
    queries = rotate(mixed[:, :width].reshape(head_shape), cosine, sine_table).astype(jnp.bfloat16)
    key_flat = (
        rotate(mixed[:, width : 2 * width].reshape(head_shape), cosine, sine_table)
        .astype(jnp.bfloat16)
        .reshape(row_count, width)
    )
    value_flat = mixed[:, 2 * width :].astype(jnp.bfloat16)
    start_state = (
        jnp.full((HEADS, row_count), -1e30, jnp.float32),
        jnp.zeros((HEADS, row_count), jnp.float32),
        jnp.zeros((HEADS, row_count, HEAD_DIM), jnp.float32),
    )
    absorb = fold_keys(queries, scaling)
    final_state = absorb(
        start_state,
        (
            lax.all_gather(key_flat, "blk", axis=0, tiled=True),
            lax.all_gather(value_flat, "blk", axis=0, tiled=True),
        ),
        jnp.int32(0),
    )
    running_max, running_sum, weighted = final_state
    log_total = running_max + jnp.log(running_sum)
    attended_f = jnp.transpose(weighted / running_sum[..., None], (1, 0, 2))
    attended = attended_f.reshape(row_count, width).astype(jnp.bfloat16)
    branch = jnp.dot(
        attended, output_weight[layer_index], preferred_element_type=jnp.float32
    ) + output_bias[layer_index].astype(jnp.float32)
    middle = residual + gate_attn * branch
    normed_mlp = modulate(middle, shift_mlp, scale_mlp).astype(jnp.bfloat16)
    up_proj = jnp.dot(
        normed_mlp, expand_weight[layer_index], preferred_element_type=jnp.float32
    ) + expand_bias[layer_index].astype(jnp.float32)
    active = gelu_tanh(up_proj).astype(jnp.bfloat16)
    lowered = jnp.dot(
        active, shrink_weight[layer_index], preferred_element_type=jnp.float32
    ) + shrink_bias[layer_index].astype(jnp.float32)
    result = middle + gate_mlp * lowered
    saved = (
        residual,
        normed,
        queries,
        key_flat,
        value_flat,
        None,
        attended_f,
        attended,
        log_total,
        branch,
        middle,
        normed_mlp,
        up_proj,
        active,
        lowered,
    )
    return (result, saved)


def backward_layer(
    gradient, modulation, layer_index, weights, saved, cosine, sine_table, scaling, condition
):
    (
        adaptive_weight,
        adaptive_bias,
        triple_weight,
        triple_bias,
        output_weight,
        output_bias,
        expand_weight,
        expand_bias,
        shrink_weight,
        shrink_bias,
    ) = weights
    (
        residual,
        normed,
        queries,
        key_flat,
        value_flat,
        gathered,
        attended_f,
        attended,
        log_total,
        branch,
        middle,
        normed_mlp,
        up_proj,
        active,
        lowered,
    ) = saved
    row_count, width = residual.shape
    pieces = [modulation[number * width : (number + 1) * width] for number in range(6)]
    shift_attn, scale_attn, gate_attn, shift_mlp, scale_mlp, gate_mlp = pieces
    gate_mlp_grad = jnp.sum(gradient * lowered, 0)
    lowered_grad = (gradient * gate_mlp).astype(jnp.bfloat16)
    shrink_w_grad = jnp.einsum(
        "tf,td->fd", active, lowered_grad, preferred_element_type=jnp.float32
    )
    shrink_b_grad = jnp.sum(lowered_grad.astype(jnp.float32), 0)
    active_grad = jnp.einsum(
        "td,fd->tf", lowered_grad, shrink_weight[layer_index], preferred_element_type=jnp.float32
    )
    _, gelu_pull = jax.vjp(gelu_tanh, up_proj)
    up_grad = gelu_pull(active_grad)[0].astype(jnp.bfloat16)
    expand_w_grad = jnp.einsum("td,tf->df", normed_mlp, up_grad, preferred_element_type=jnp.float32)
    expand_b_grad = jnp.sum(up_grad.astype(jnp.float32), 0)
    normed_mlp_grad = jnp.einsum(
        "tf,df->td", up_grad, expand_weight[layer_index], preferred_element_type=jnp.float32
    )
    _, mlp_pull = jax.vjp(modulate, middle, shift_mlp, scale_mlp)
    middle_grad, shift_mlp_grad, scale_mlp_grad = mlp_pull(normed_mlp_grad)
    middle_grad = middle_grad + gradient
    gate_attn_grad = jnp.sum(middle_grad * branch, 0)
    branch_grad = (middle_grad * gate_attn).astype(jnp.bfloat16)
    output_w_grad = jnp.einsum(
        "tc,td->cd", attended, branch_grad, preferred_element_type=jnp.float32
    )
    output_b_grad = jnp.sum(branch_grad.astype(jnp.float32), 0)
    attended_grad = jnp.einsum(
        "td,cd->tc", branch_grad, output_weight[layer_index], preferred_element_type=jnp.float32
    )
    attended_grad = attended_grad.astype(jnp.bfloat16).reshape(row_count, HEADS, HEAD_DIM)
    key_all, value_all = (
        lax.all_gather(key_flat, "blk", axis=0, tiled=True),
        lax.all_gather(value_flat, "blk", axis=0, tiled=True),
    )
    query_grad, key_all_grad, value_all_grad = attend_back(
        queries, key_all, value_all, attended_grad, attended_f, log_total, scaling
    )
    key_grad, value_grad = (
        lax.psum_scatter(
            key_all_grad.astype(jnp.bfloat16), "blk", scatter_dimension=0, tiled=True
        ).astype(jnp.float32),
        lax.psum_scatter(
            value_all_grad.astype(jnp.bfloat16), "blk", scatter_dimension=0, tiled=True
        ).astype(jnp.float32),
    )
    mixed_grad = jnp.concatenate(
        [
            unrotate(query_grad, cosine, sine_table).reshape(row_count, width),
            unrotate(key_grad.reshape(row_count, HEADS, HEAD_DIM), cosine, sine_table).reshape(
                row_count, width
            ),
            value_grad,
        ],
        -1,
    ).astype(jnp.bfloat16)
    triple_w_grad = jnp.einsum("td,tc->dc", normed, mixed_grad, preferred_element_type=jnp.float32)
    triple_b_grad = jnp.sum(mixed_grad.astype(jnp.float32), 0)
    normed_grad = jnp.einsum(
        "tc,dc->td", mixed_grad, triple_weight[layer_index], preferred_element_type=jnp.float32
    )
    _, attn_pull = jax.vjp(modulate, residual, shift_attn, scale_attn)
    residual_grad, shift_attn_grad, scale_attn_grad = attn_pull(normed_grad)
    residual_grad = residual_grad + middle_grad
    modulation_grad = jnp.concatenate(
        [
            shift_attn_grad,
            scale_attn_grad,
            gate_attn_grad,
            shift_mlp_grad,
            scale_mlp_grad,
            gate_mlp_grad,
        ],
        0,
    )
    adaptive_w_grad = condition[0][:, None] * modulation_grad[None, :]
    condition_term = jnp.dot(
        adaptive_weight[layer_index].astype(jnp.float32), modulation_grad, precision=HIGHEST
    )
    grad_terms = (
        adaptive_w_grad,
        modulation_grad,
        triple_w_grad,
        triple_b_grad,
        output_w_grad,
        output_b_grad,
        expand_w_grad,
        expand_b_grad,
        shrink_w_grad,
        shrink_b_grad,
    )
    return (residual_grad, grad_terms, condition_term)


def local(
    inputs,
    condition,
    prefix,
    mask_embed,
    adaptive_weight,
    adaptive_bias,
    triple_weight,
    triple_bias,
    output_weight,
    output_bias,
    expand_weight,
    expand_bias,
    shrink_weight,
    shrink_bias,
    cotangent,
):
    weights = (
        adaptive_weight,
        adaptive_bias,
        triple_weight,
        triple_bias,
        output_weight,
        output_bias,
        expand_weight,
        expand_bias,
        shrink_weight,
        shrink_bias,
    )
    row_count = inputs.shape[1]
    offset = lax.axis_index("blk") * row_count
    position = offset + jnp.arange(row_count, dtype=jnp.int32)
    masked = position >= prefix[0]
    residual = jnp.where(
        masked[:, None], mask_embed.astype(jnp.float32)[None, :], inputs[0].astype(jnp.float32)
    )
    cosine, sine_table = tables(offset, row_count, HEAD_DIM)
    scaling = 1.0 / math.sqrt(HEAD_DIM)
    modulations = []
    saved_layers = []
    for layer_index in range(LAYERS):
        modulation = jnp.dot(
            condition, adaptive_weight[layer_index].astype(jnp.float32), precision=HIGHEST
        )[0] + adaptive_bias[layer_index].astype(jnp.float32)
        residual, saved = forward_layer(
            residual, modulation, layer_index, weights, cosine, sine_table, scaling
        )
        modulations.append(modulation)
        saved_layers.append(saved)
    outputs = residual.astype(jnp.bfloat16)[None]
    gradient = cotangent[0].astype(jnp.float32)
    condition_total = jnp.zeros((condition.shape[1],), jnp.float32)
    collected = [None] * LAYERS
    mask_sum = None
    for layer_index in reversed(range(LAYERS)):
        gradient, grad_terms, condition_term = backward_layer(
            gradient,
            modulations[layer_index],
            layer_index,
            weights,
            saved_layers[layer_index],
            cosine,
            sine_table,
            scaling,
            condition,
        )
        condition_total = condition_total + condition_term
        collected[layer_index] = grad_terms
    mask_term = jnp.sum(jnp.where(masked[:, None], gradient, 0.0), 0)
    flat_terms = ()
    for layer_index in range(LAYERS):
        flat_terms = flat_terms + tuple(collected[layer_index])
    summed = lax.psum_scatter(
        flat_terms + (mask_term,), ("blk", "dp"), scatter_dimension=0, tiled=True
    )
    collected = [summed[layer_index * 10 : (layer_index + 1) * 10] for layer_index in range(LAYERS)]
    mask_sum = summed[LAYERS * 10]
    condition_grad = lax.psum(condition_total, "blk")[None, :]
    input_grad = jnp.where(masked[:, None], 0.0, gradient)[None]
    stacked = [
        jnp.stack([collected[layer_index][number] for layer_index in range(LAYERS)], 0)
        for number in range(10)
    ]
    return (
        outputs,
        input_grad,
        condition_grad,
        mask_sum,
        stacked[0],
        stacked[1],
        stacked[2],
        stacked[3],
        stacked[4],
        stacked[5],
        stacked[6],
        stacked[7],
        stacked[8],
        stacked[9],
    )


def solution(mesh):
    in_specs = (
        P("dp", "blk", None),
        P("dp", None),
        P("dp"),
        P(),
        P(),
        P(),
        P(),
        P(),
        P(),
        P(),
        P(),
        P(),
        P(),
        P(),
        P("dp", "blk", None),
    )
    out_specs = (
        P("dp", "blk", None),
        P("dp", "blk", None),
        P("dp", None),
        P(("blk", "dp")),
        P(None, ("blk", "dp"), None),
        P(None, ("blk", "dp")),
        P(None, ("blk", "dp"), None),
        P(None, ("blk", "dp")),
        P(None, ("blk", "dp"), None),
        P(None, ("blk", "dp")),
        P(None, ("blk", "dp"), None),
        P(None, ("blk", "dp")),
        P(None, ("blk", "dp"), None),
        P(None, ("blk", "dp")),
    )
    return jax.shard_map(local, mesh=mesh, in_specs=in_specs, out_specs=out_specs, check_vma=False)
```

profile of v0, /device:TPU:0, one launch (start us, length us, event | category | flops | bytes accessed | tf_op | source)
XLA Modules:
  0.0 1786.5 jit_solution(14609906756589600221)
XLA Ops:
  15.4 3.4 convolution_add_fusion.1
  27.5 28.2 %all-gather.5.cloned.1.call-done = bf16[1024,768]{0,1:T(8,128)(2,1)} async-done(((bf16[256,768]{0,1:T(8,128)(2,1)}), bf16[1024,768]{0,1:T(8,128)(2,1)}) %all-gather.5.cloned.1.call-update) | async-done | bytes 1572880 | tf_op jit(solution)/shard_map/all_gather | solution.py:181
  60.2 29.0 %all-gather.7.cloned.1.call-done = bf16[1024,768]{1,0:T(8,128)(2,1)} async-done(((bf16[256,768]{1,0:T(8,128)(2,1)}), bf16[1024,768]{1,0:T(8,128)(2,1)}) %all-gather.7.cloned.1.call-update) | async-done | bytes 1572880 | tf_op jit(solution)/shard_map/all_gather | solution.py:182
  95.0 24.3 %while.60 = (s32[]{:T(128)}, f32[12,256]{1,0:T(8,128)S(1)}, f32[12,256]{1,0:T(8,128)S(1)}, f32[12,256,64]{1,2,0:T(8,128)S(1)}, bf16[2,512,12,64]{1,3,2,0:T(8,128...) while((s32[]{:T(128)}, f32[12,256]{1,0:T(8,128)S(1)}, ...), condition=%wide.region_5.6_spmd.clone, body=%wide.region_2.5_spmd.clone.sunk | while | flops 626801664 | bytes 56451720 | solution.py:96
  95.0 5.0 bitcast_reduce_fusion.4
  100.0 4.3 fusion.362
  107.1 4.9 bitcast_reduce_fusion.4
  112.1 4.3 fusion.362
  119.5 3.5 fusion.268
  123.4 4.0 fusion.122
  140.5 27.2 %all-gather.9.cloned.1.call-done = bf16[1024,768]{0,1:T(8,128)(2,1)} async-done(((bf16[256,768]{0,1:T(8,128)(2,1)}), bf16[1024,768]{0,1:T(8,128)(2,1)}) %all-gather.9.cloned.1.call-update) | async-done | bytes 1572880 | tf_op jit(solution)/shard_map/all_gather | solution.py:181
  167.7 3.1 reshape.383
  172.3 28.7 %all-gather.11.cloned.1.call-done = bf16[1024,768]{1,0:T(8,128)(2,1)} async-done(((bf16[256,768]{1,0:T(8,128)(2,1)}), bf16[1024,768]{1,0:T(8,128)(2,1)}) %all-gather.11.cloned.1.call-update) | async-done | bytes 1572880 | tf_op jit(solution)/shard_map/all_gather | solution.py:182
  206.8 24.5 %while.61 = (s32[]{:T(128)}, f32[12,256]{1,0:T(8,128)S(1)}, f32[12,256]{1,0:T(8,128)S(1)}, f32[12,256,64]{1,2,0:T(8,128)S(1)}, bf16[2,512,12,64]{1,3,2,0:T(8,128...) while((s32[]{:T(128)}, f32[12,256]{1,0:T(8,128)S(1)}, ...), condition=%wide.region_13.14_spmd.clone, body=%wide.region_10.13_spmd.clone.sunk | while | flops 626801664 | bytes 56451720 | solution.py:96
  206.9 4.9 bitcast_reduce_fusion.5
  211.8 4.3 fusion.370
  218.9 4.9 bitcast_reduce_fusion.5
  223.8 4.3 fusion.370
  231.5 3.3 fusion.266
  235.1 4.0 fusion.125
  239.1 7.0 convert_reduce_fusion
  254.3 26.9 %while.62 = (s32[]{:T(128)}, f32[256,12,64]{0,2,1:T(8,128)}, bf16[2,512,12,64]{1,3,2,0:T(8,128)(2,1)}, bf16[2,512,12,64]{1,3,2,0:T(8,128)(2,1)}, bf16[2,512,12,6...) while((s32[]{:T(128)}, f32[256,12,64]{0,2,1:T(8,128)}, ...), condition=%wide.region_20.21_spmd.clone, body=%wide.region_19.20_spmd.clone.sunk | while | flops 1231159296 | bytes 53192888 | solution.py:133
  290.8 26.1 %reduce-scatter.13.cloned.1.call-done = bf16[256,768]{0,1:T(8,128)(2,1)} async-done(((bf16[1024,768]{0,1:T(8,128)(2,1)}), bf16[256,768]{0,1:T(8,128)(2,1)}) %reduce-scatter.13.cloned.1.call-update) | async-done | bytes 393232 | tf_op jit(solution)/shard_map/reduce_scatter | solution.py:295
  318.4 32.4 %reduce-scatter.15.cloned.1.call-done = bf16[256,768]{0,1:T(8,128)(2,1)} async-done(((bf16[1024,768]{0,1:T(8,128)(2,1)}), bf16[256,768]{0,1:T(8,128)(2,1)}) %reduce-scatter.15.cloned.1.call-update) | async-done | bytes 393232 | tf_op jit(solution)/shard_map/reduce_scatter | solution.py:298
  350.8 4.2 multiply_reduce_fusion.5
  355.5 6.6 convert_reduce_fusion.4
  362.2 4.1 convert_reduce_fusion.1
  374.9 26.7 %while.63 = (s32[]{:T(128)}, f32[256,12,64]{0,2,1:T(8,128)}, bf16[2,512,12,64]{1,3,2,0:T(8,128)(2,1)}, bf16[2,512,12,64]{1,3,2,0:T(8,128)(2,1)}, bf16[2,512,12,6...) while((s32[]{:T(128)}, f32[256,12,64]{0,2,1:T(8,128)}, ...), condition=%wide.region_29.30_spmd.clone, body=%wide.region_28.29_spmd.clone.sunk | while | flops 1231159296 | bytes 53192888 | solution.py:133
  418.0 19.3 %reduce-scatter.17.cloned.1.call-done = bf16[256,768]{0,1:T(8,128)(2,1)} async-done(((bf16[1024,768]{0,1:T(8,128)(2,1)}), bf16[256,768]{0,1:T(8,128)(2,1)}) %reduce-scatter.17.cloned.1.call-update) | async-done | bytes 393232 | tf_op jit(solution)/shard_map/reduce_scatter | solution.py:295
  438.7 32.5 %reduce-scatter.19.cloned.1.call-done = bf16[256,768]{0,1:T(8,128)(2,1)} async-done(((bf16[1024,768]{0,1:T(8,128)(2,1)}), bf16[256,768]{0,1:T(8,128)(2,1)}) %reduce-scatter.19.cloned.1.call-update) | async-done | bytes 393232 | tf_op jit(solution)/shard_map/reduce_scatter | solution.py:298
  471.3 3.6 fusion.216
  482.9 7.9 fusion.248
  491.8 7.8 fusion.261
  500.7 6.6 fusion.260
  508.5 6.7 fusion.259
  516.4 4.8 fusion.258
  521.9 4.2 fusion.231
  529.8 9.4 psum.7
  539.2 36.4 %reduce-scatter.27.cloned.1.call-done = f32[24,768]{1,0:T(8,128)} async-done(((f32[768,768]{1,0:T(8,128)}), f32[24,768]{1,0:T(8,128)}) %reduce-scatter.27.cloned.1.call-update) | async-done | bytes 73744 | tf_op jit(solution)/shard_map/reduce_scatter | solution.py:422
  575.6 104.0 %reduce-scatter.25.cloned.1.call-done = f32[24,768]{1,0:T(8,128)} async-done(((f32[768,768]{1,0:T(8,128)}), f32[24,768]{1,0:T(8,128)}) %reduce-scatter.25.cloned.1.call-update) | async-done | bytes 73744 | tf_op jit(solution)/shard_map/reduce_scatter | solution.py:422
  681.1 131.9 %all-reduce.18.cloned.1.call-done = (f32[768]{0:T(1024)}, f32[4608]{0:T(1024)}, f32[4608]{0:T(1024)}, f32[2304]{0:T(1024)}, f32[2304]{0:T(1024)}, /*index=5*/f32...) async-done(((f32[768]{0:T(1024)}, f32[4608]{0:T(1024)}, f32[4608]{0:T(1024)}, f32[2304]{0:T(1024)}, ...) | async-done | bytes 95248
  824.8 140.8 %all-reduce.20.cloned.1.call-done = (f32[128,4608]{1,0:T(8,128)}, f32[128,4608]{1,0:T(8,128)}) async-done(((f32[128,4608]{1,0:T(8,128)}, f32[128,4608]{1,0:T(8,128)}), (f32[128,4608]{1,0:T(8,128)}, f32[128,4608]{1,0:T(8,128)})) %all-reduce.20.cloned.1.call-update) | async-done | bytes 4718608
  968.1 137.8 %reduce-scatter.35.cloned.1.call-done = f32[96,768]{1,0:T(8,128)} async-done(((f32[3072,768]{1,0:T(8,128)}), f32[96,768]{1,0:T(8,128)}) %reduce-scatter.35.cloned.1.call-update) | async-done | bytes 294928 | tf_op jit(solution)/shard_map/reduce_scatter | solution.py:422
  1105.9 141.3 %reduce-scatter.33.cloned.1.call-done = f32[96,768]{1,0:T(8,128)} async-done(((f32[3072,768]{1,0:T(8,128)}), f32[96,768]{1,0:T(8,128)}) %reduce-scatter.33.cloned.1.call-update) | async-done | bytes 294928 | tf_op jit(solution)/shard_map/reduce_scatter | solution.py:422
  1249.1 138.5 %reduce-scatter.31.cloned.1.call-done = f32[24,3072]{1,0:T(8,128)} async-done(((f32[768,3072]{1,0:T(8,128)}), f32[24,3072]{1,0:T(8,128)}) %reduce-scatter.31.cloned.1.call-update) | async-done | bytes 294928 | tf_op jit(solution)/shard_map/reduce_scatter | solution.py:422
  1387.6 141.3 %reduce-scatter.29.cloned.1.call-done = f32[24,3072]{1,0:T(8,128)} async-done(((f32[768,3072]{1,0:T(8,128)}), f32[24,3072]{1,0:T(8,128)}) %reduce-scatter.29.cloned.1.call-update) | async-done | bytes 294928 | tf_op jit(solution)/shard_map/reduce_scatter | solution.py:422
  1530.7 122.0 %reduce-scatter.23.cloned.1.call-done = f32[24,2304]{1,0:T(8,128)} async-done(((f32[768,2304]{1,0:T(8,128)}), f32[24,2304]{1,0:T(8,128)}) %reduce-scatter.23.cloned.1.call-update) | async-done | bytes 221200 | tf_op jit(solution)/shard_map/reduce_scatter | solution.py:422
  1652.7 124.9 %reduce-scatter.21.cloned.1.call-done = f32[24,2304]{1,0:T(8,128)} async-done(((f32[768,2304]{1,0:T(8,128)}), f32[24,2304]{1,0:T(8,128)}) %reduce-scatter.21.cloned.1.call-update) | async-done | bytes 221200 | tf_op jit(solution)/shard_map/reduce_scatter | solution.py:422
  (562 shorter events, 194.5 us)
Async XLA Ops:
  7.2 48.6 %all-gather.5.cloned.1.call-start = ((), (), s32[]{:S(2)}) async-start(), calls=%async_computation.12 | async-start | bytes 1966080 | tf_op jit(solution)/shard_map/all_gather | solution.py:181
  7.9 111.6 %copy-start.103 = (pred[256]{0:T(512)(128)(4,1)}, pred[256]{0:T(512)(128)(4,1)S(1)}, u32[]{:S(2)}) copy-start(pred[256]{0:T(512)(128)(4,1)S(1)} %fusion.251) | copy-start | bytes 772
  8.6 110.9 %copy-start.68 = (f32[768]{0:T(1024)}, f32[768]{0:T(1024)S(1)}, u32[]{:S(2)}) copy-start(f32[768]{0:T(1024)S(1)} %convert_element_type.245) | copy-start | bytes 9220
  14.5 105.0 %copy-start.109 = (f32[768]{0:T(1024)}, f32[768]{0:T(1024)S(1)}, u32[]{:S(2)}) copy-start(f32[768]{0:T(1024)S(1)} %get-tuple-element.609) | copy-start | bytes 9220
  14.5 108.8 %copy-start.76 = (f32[768]{0:T(1024)}, f32[768]{0:T(1024)S(1)}, u32[]{:S(2)}) copy-start(f32[768]{0:T(1024)S(1)} %get-tuple-element.606) | copy-start | bytes 9220
  14.5 108.8 %copy-start.86 = (f32[768]{0:T(1024)}, f32[768]{0:T(1024)S(1)}, u32[]{:S(2)}) copy-start(f32[768]{0:T(1024)S(1)} %get-tuple-element.605) | copy-start | bytes 9220
  14.6 112.9 %copy-start.130 = (f32[768]{0:T(1024)}, f32[768]{0:T(1024)S(1)}, u32[]{:S(2)}) copy-start(f32[768]{0:T(1024)S(1)} %get-tuple-element.604) | copy-start | bytes 9220
  21.0 114.0 %copy-start.53 = (f32[256,32]{0,1:T(8,128)}, f32[256,32]{0,1:T(8,128)S(1)}, u32[]{:S(2)}) copy-start(f32[256,32]{0,1:T(8,128)S(1)} %get-tuple-element.612) | copy-start | bytes 98308
  21.0 114.0 %copy-start.56 = (f32[256,32]{0,1:T(8,128)}, f32[256,32]{0,1:T(8,128)S(1)}, u32[]{:S(2)}) copy-start(f32[256,32]{0,1:T(8,128)S(1)} %get-tuple-element.613) | copy-start | bytes 98308
  22.1 67.1 %all-gather.7.cloned.1.call-start = ((), (), s32[]{:S(2)}) async-start(), calls=%async_computation.13 | async-start | bytes 1966080 | tf_op jit(solution)/shard_map/all_gather | solution.py:182
  24.1 143.7 %all-gather.9.cloned.1.call-start = ((), (), s32[]{:S(2)}) async-start(), calls=%async_computation.14 | async-start | bytes 1966080 | tf_op jit(solution)/shard_map/all_gather | solution.py:181
  27.5 104.2 %copy-start.79 = (f32[768]{0:T(1024)}, f32[768]{0:T(1024)S(1)}, u32[]{:S(2)}) copy-start(f32[768]{0:T(1024)S(1)} %get-tuple-element.602) | copy-start | bytes 9220
  27.5 104.2 %copy-start.88 = (f32[768]{0:T(1024)}, f32[768]{0:T(1024)S(1)}, u32[]{:S(2)}) copy-start(f32[768]{0:T(1024)S(1)} %get-tuple-element.601) | copy-start | bytes 9220
  27.5 207.6 %copy-start.90 = (f32[768]{0:T(1024)}, f32[768]{0:T(1024)S(1)}, u32[]{:S(2)}) copy-start(f32[768]{0:T(1024)S(1)} %get-tuple-element.599) | copy-start | bytes 9220
  27.5 211.6 %copy-start.106 = (f32[768]{0:T(1024)}, f32[768]{0:T(1024)S(1)}, u32[]{:S(2)}) copy-start(f32[768]{0:T(1024)S(1)} %get-tuple-element.598) | copy-start | bytes 9220
  27.5 220.8 %copy-start.82 = (f32[768]{0:T(1024)}, f32[768]{0:T(1024)S(1)}, u32[]{:S(2)}) copy-start(f32[768]{0:T(1024)S(1)} %get-tuple-element.600) | copy-start | bytes 9220
  95.0 24.5 %copy-start.20 = (bf16[1,256,768]{2,1,0:T(8,128)(2,1)S(1)}, bf16[1,256,768]{2,1,0:T(8,128)(2,1)}, u32[]{:S(2)}) copy-start(bf16[1,256,768]{2,1,0:T(8,128)(2,1)} %param.23) | copy-start | bytes 1179652
  131.4 100.1 %copy-start.10 = (f32[256,768]{1,0:T(8,128)}, f32[256,768]{1,0:T(8,128)S(1)}, u32[]{:S(2)}) copy-start(f32[256,768]{1,0:T(8,128)S(1)} %get-tuple-element.557) | copy-start | bytes 2359300
  136.7 64.3 %all-gather.11.cloned.1.call-start = ((), (), s32[]{:S(2)}) async-start(), calls=%async_computation.15 | async-start | bytes 1966080 | tf_op jit(solution)/shard_map/all_gather | solution.py:182
  138.7 178.2 %reduce-scatter.13.cloned.1.call-start = ((), (), s32[]{:S(2)}) async-start(), calls=%async_computation.16 | async-start | bytes 1966080 | tf_op jit(solution)/shard_map/reduce_scatter | solution.py:295
  285.9 64.8 %reduce-scatter.15.cloned.1.call-start = ((), (), s32[]{:S(2)}) async-start(), calls=%async_computation.17 | async-start | bytes 1966080 | tf_op jit(solution)/shard_map/reduce_scatter | solution.py:298
  289.0 29.0 %copy-start.54 = (f32[256,32]{0,1:T(8,128)S(1)}, f32[256,32]{0,1:T(8,128)}, u32[]{:S(2)}) copy-start(f32[256,32]{0,1:T(8,128)} %copy-done.53) | copy-start | bytes 98308
  289.0 29.0 %copy-start.57 = (f32[256,32]{0,1:T(8,128)S(1)}, f32[256,32]{0,1:T(8,128)}, u32[]{:S(2)}) copy-start(f32[256,32]{0,1:T(8,128)} %copy-done.56) | copy-start | bytes 98308
  290.6 146.7 %reduce-scatter.17.cloned.1.call-start = ((), (), s32[]{:S(2)}) async-start(), calls=%async_computation.18 | async-start | bytes 1966080 | tf_op jit(solution)/shard_map/reduce_scatter | solution.py:295
  290.7 60.0 %copy-start.11 = (f32[256,768]{1,0:T(8,128)S(1)}, f32[256,768]{1,0:T(8,128)}, u32[]{:S(2)}) copy-start(f32[256,768]{1,0:T(8,128)} %copy-done.10) | copy-start | bytes 2359300
  290.7 60.0 %copy-start.80 = (f32[768]{0:T(1024)S(1)}, f32[768]{0:T(1024)}, u32[]{:S(2)}) copy-start(f32[768]{0:T(1024)} %copy-done.79) | copy-start | bytes 9220
  290.7 60.0 %copy-start.99 = (f32[256]{0:T(256)S(1)}, f32[256]{0:T(256)}, u32[]{:S(2)}) copy-start(f32[256]{0:T(256)} %copy-done.98) | copy-start | bytes 3076
  290.7 60.0 %copy-start.116 = (f32[256]{0:T(256)S(1)}, f32[256]{0:T(256)}, u32[]{:S(2)}) copy-start(f32[256]{0:T(256)} %copy-done.115) | copy-start | bytes 3076
  318.3 36.7 %copy-start.26 = (bf16[256,12,64]{0,2,1:T(8,128)(2,1)}, bf16[256,12,64]{0,2,1:T(8,128)(2,1)S(1)}, u32[]{:S(2)}) copy-start(bf16[256,12,64]{0,2,1:T(8,128)(2,1)S(1)} %get-tuple-element.627) | copy-start | bytes 1179652
  318.3 36.7 %copy-start.28 = (bf16[256,12,64]{0,2,1:T(8,128)(2,1)}, bf16[256,12,64]{0,2,1:T(8,128)(2,1)S(1)}, u32[]{:S(2)}) copy-start(bf16[256,12,64]{0,2,1:T(8,128)(2,1)S(1)} %get-tuple-element.628) | copy-start | bytes 1179652
  406.2 65.0 %reduce-scatter.19.cloned.1.call-start = ((), (), s32[]{:S(2)}) async-start(), calls=%async_computation.19 | async-start | bytes 1966080 | tf_op jit(solution)/shard_map/reduce_scatter | solution.py:298
  411.0 164.6 %reduce-scatter.27.cloned.1.call-start = ((), (), s32[]{:S(2)}) async-start(), calls=%async_computation.23 | async-start | bytes 2433024 | tf_op jit(solution)/shard_map/reduce_scatter | solution.py:422
  413.0 266.5 %reduce-scatter.25.cloned.1.call-start = ((), (), s32[]{:S(2)}) async-start(), calls=%async_computation.22 | async-start | bytes 2433024 | tf_op jit(solution)/shard_map/reduce_scatter | solution.py:422
  416.9 21.5 %copy-start.58 = (f32[256,32]{0,1:T(8,128)S(1)}, f32[256,32]{0,1:T(8,128)}, u32[]{:S(2)}) copy-start(f32[256,32]{0,1:T(8,128)} %copy-done.56) | copy-start | bytes 98308
  416.9 54.3 %copy-start.21 = (bf16[1,256,768]{2,1,0:T(8,128)(2,1)S(1)}, bf16[1,256,768]{2,1,0:T(8,128)(2,1)}, u32[]{:S(2)}) copy-start(bf16[1,256,768]{2,1,0:T(8,128)(2,1)} %param.23) | copy-start | bytes 1179652
  417.0 54.3 %copy-start.69 = (f32[768]{0:T(1024)S(1)}, f32[768]{0:T(1024)}, u32[]{:S(2)}) copy-start(f32[768]{0:T(1024)} %copy-done.68) | copy-start | bytes 9220
  417.0 54.2 %copy-start.75 = (f32[768]{0:T(1024)S(1)}, f32[768]{0:T(1024)}, u32[]{:S(2)}) copy-start(f32[768]{0:T(1024)} %copy-done.74) | copy-start | bytes 9220
  417.0 54.2 %copy-start.96 = (f32[256]{0:T(256)S(1)}, f32[256]{0:T(256)}, u32[]{:S(2)}) copy-start(f32[256]{0:T(256)} %copy-done.95) | copy-start | bytes 3076
  417.0 54.2 %copy-start.104 = (pred[256]{0:T(512)(128)(4,1)S(1)}, pred[256]{0:T(512)(128)(4,1)}, u32[]{:S(2)}) copy-start(pred[256]{0:T(512)(128)(4,1)} %copy-done.103) | copy-start | bytes 772
  417.0 54.2 %copy-start.113 = (f32[256]{0:T(256)S(1)}, f32[256]{0:T(256)}, u32[]{:S(2)}) copy-start(f32[256]{0:T(256)} %copy-done.112) | copy-start | bytes 3076
  481.5 331.5 %all-reduce.18.cloned.1.call-start = ((), (), s32[]{:S(2)}) async-start(), calls=%async_computation.28 | async-start | bytes 221184
  482.3 483.3 %all-reduce.20.cloned.1.call-start = ((), (), s32[]{:S(2)}) async-start(), calls=%async_computation.29 | async-start | bytes 9437184
  482.8 623.0 %reduce-scatter.35.cloned.1.call-start = ((), (), s32[]{:S(2)}) async-start(), calls=%async_computation.27 | async-start | bytes 9732096 | tf_op jit(solution)/shard_map/reduce_scatter | solution.py:422
  490.8 756.3 %reduce-scatter.33.cloned.1.call-start = ((), (), s32[]{:S(2)}) async-start(), calls=%async_computation.26 | async-start | bytes 9732096 | tf_op jit(solution)/shard_map/reduce_scatter | solution.py:422
  499.6 887.9 %reduce-scatter.31.cloned.1.call-start = ((), (), s32[]{:S(2)}) async-start(), calls=%async_computation.25 | async-start | bytes 9732096 | tf_op jit(solution)/shard_map/reduce_scatter | solution.py:422
  507.4 1021.4 %reduce-scatter.29.cloned.1.call-start = ((), (), s32[]{:S(2)}) async-start(), calls=%async_computation.24 | async-start | bytes 9732096 | tf_op jit(solution)/shard_map/reduce_scatter | solution.py:422
  515.3 1137.4 %reduce-scatter.23.cloned.1.call-start = ((), (), s32[]{:S(2)}) async-start(), calls=%async_computation.21 | async-start | bytes 7299072 | tf_op jit(solution)/shard_map/reduce_scatter | solution.py:422
  521.2 1256.4 %reduce-scatter.21.cloned.1.call-start = ((), (), s32[]{:S(2)}) async-start(), calls=%async_computation.20 | async-start | bytes 7299072 | tf_op jit(solution)/shard_map/reduce_scatter | solution.py:422
  (131 other events, 534.7 us)
Sparse Core Ops, SparseCore 0:
  22.2 33.5 all-gather.4
  58.2 30.9 all-gather.6
  136.9 30.8 all-gather.8
  170.0 30.9 all-gather.10
  286.0 30.8 reduce-scatter.12
  319.8 30.8 reduce-scatter.14
  406.3 30.8 reduce-scatter.16
  440.3 30.8 reduce-scatter.18
  476.5 99.0 reduce-scatter.26
  581.6 97.9 reduce-scatter.24
  687.1 125.8 all-reduce.17
  819.7 145.7 all-reduce.19
  971.5 134.3 reduce-scatter.34
  1112.6 134.4 reduce-scatter.32
  1252.9 134.6 reduce-scatter.30
  1394.3 134.4 reduce-scatter.28
  1534.3 118.2 reduce-scatter.22
  1659.1 118.3 reduce-scatter.20
where the time goes:
time: 1800 us; the launch traced here: 1790 us
  waiting for transfers between devices  1440 us (80%)
  matrix products  197 us (11%)
  local copies, waits for them, and re-layouts  74.8 us (4%)
  other arithmetic  41.7 us (2%)
    reduce_scatter x8, waiting for transfers between devices, local(): lax.psum_scatter(flat_terms + (mask_term,), ('blk', 'dp'), scatter_dimens...  946 us
    unnamed x20, waiting for transfers between devices  274 us
    reduce_scatter x2, waiting for transfers between devices, backward_layer(): lax.psum_scatter(value_all_grad.astype(jnp.bfloat16), 'blk', scatter_dime...  64.9 us
    all_gather x2, waiting for transfers between devices, forward_layer(): lax.all_gather(value_flat, 'blk', axis=0, tiled=True)  57.7 us
    all_gather x2, waiting for transfers between devices, forward_layer(): lax.all_gather(key_flat, 'blk', axis=0, tiled=True)  55.4 us
    reduce_scatter x2, waiting for transfers between devices, backward_layer(): lax.psum_scatter(key_all_grad.astype(jnp.bfloat16), 'blk', scatter_dimens...  45.4 us
  transfers between devices with their start and end apart: 18, of which 18 were waited for; matrix products, arithmetic and copies ran while one was open for 6% of the time, Pallas kernels for 0%

commit v1 on v0

--- a/solution.py
+++ b/solution.py
@@ -1,8 +1,11 @@
+import functools
 import math
 
 import jax
 import jax.numpy as jnp
 from jax import lax
+from jax.experimental import pallas as pl
+from jax.experimental.pallas import tpu as pltpu
 from jax.sharding import PartitionSpec as P
 
 HEADS = 12
@@ -448,6 +451,779 @@
     )
 
 
+BF = jnp.bfloat16
+F32 = jnp.float32
+WIDTH = HEADS * HEAD_DIM
+GROUP = WIDTH // 4
+VM = pl.BlockSpec(memory_space=pltpu.VMEM)
+ANY = pl.BlockSpec(memory_space=pl.ANY)
+SM = pl.BlockSpec(memory_space=pltpu.SMEM)
+VMEM_LIMIT = 58 * 1024 * 1024
+ROOT_TWO_PI = math.sqrt(2.0 / math.pi)
+CUBIC = 0.044715
+
+
+def dot_nn(left, right):
+    return jnp.dot(left, right, preferred_element_type=F32)
+
+
+def dot_nt(left, right):
+    return lax.dot_general(left, right, (((1,), (1,)), ((), ())), preferred_element_type=F32)
+
+
+def dot_tn(left, right):
+    return lax.dot_general(left, right, (((0,), (0,)), ((), ())), preferred_element_type=F32)
+
+
+def normalise(values):
+    centered = values - jnp.mean(values, -1, keepdims=True)
+    rstd = lax.rsqrt(jnp.mean(centered * centered, -1, keepdims=True) + EPSILON)
+    return centered * rstd, rstd
+
+
+def normalise_back(upstream, unit, rstd):
+    first = jnp.mean(upstream, -1, keepdims=True)
+    second = jnp.mean(upstream * unit, -1, keepdims=True)
+    return rstd * (upstream - first - unit * second)
+
+
+def column_sum(values):
+    return jnp.sum(values, 0, keepdims=True)
+
+
+def turn(values, cosine, signed_sine):
+    lane = lax.broadcasted_iota(jnp.int32, (values.shape[0], 128), 1)
+    front = (lane % HEAD_DIM) < HEAD_DIM // 2
+    pieces = []
+    for start in range(0, values.shape[1], 128):
+        piece = values[:, start : start + 128]
+        swapped = jnp.where(front, pltpu.roll(piece, 96, 1), pltpu.roll(piece, 32, 1))
+        pieces.append(piece * cosine + swapped * signed_sine)
+    return jnp.concatenate(pieces, 1)
+
+
+def piece_of(row, number):
+    return row[:, number * WIDTH : (number + 1) * WIDTH]
+
+
+BIAS_AT = {"triple": (0, 2304), "output": (2304, 3072), "expand": (3072, 6144), "shrink": (6144, 6912)}
+
+
+def bias_of(bias_ref, layer, name):
+    low, high = BIAS_AT[name]
+    return bias_ref[layer][:, low:high]
+
+
+def pack_rows(values):
+    half = values.shape[0] // 2
+    return jnp.concatenate([values[:half], values[half:]], 1)
+
+
+def qkv_stage(x, layer, mod_row, bias_ref, triple, cos_ref, sin_ref, me, h_ref, chunk_refs, hold):
+    unit, _ = normalise(x)
+    h = (unit * (1.0 + piece_of(mod_row, 1)) + piece_of(mod_row, 0)).astype(BF)
+    h_ref[...] = h
+    bias = bias_of(bias_ref, layer, "triple")
+    cosine, sine = cos_ref[0], sin_ref[0]
+    parts = []
+    for number in range(3):
+        columns = slice(number * WIDTH, (number + 1) * WIDTH)
+        mixed = dot_nn(h, triple[:, columns]) + bias[:, columns]
+        if number < 2:
+            mixed = turn(mixed, cosine, sine)
+        if number == 0:
+            mixed = mixed * HEAD_DIM**-0.5
+        parts.append(mixed)
+    rows = x.shape[0]
+    for group in range(4):
+        columns = slice(group * GROUP, (group + 1) * GROUP)
+        pair = jnp.concatenate([parts[0][:, columns], parts[1][:, columns]], 1)
+        hold[group, 0:rows, :] = pair.astype(BF)
+        hold[group, rows : rows + rows // 2, :] = pack_rows(parts[2][:, columns]).astype(BF)
+    for place in range(4):
+        chunk_refs[place][...] = hold[place ^ me]
+
+
+def first_kernel(
+    scal, inputs, mask_embed, condition, adaptive_weight, adaptive_bias, bias_ref, cos_ref, sin_ref, triple_any,
+    x_ref, mod_ref, h_ref, c0, c1, c2, c3,
+    triple, hold, sems,
+):
+    copy = pltpu.make_async_copy(triple_any.at[0], triple, sems.at[0])
+    copy.start()
+    me = scal[0]
+    cond = condition[...]
+    upper = cond.astype(BF).astype(F32)
+    rest = cond - upper
+    mid = rest.astype(BF).astype(F32)
+    low = rest - mid
+    row = lax.broadcasted_iota(jnp.int32, (8, cond.shape[1]), 0)
+    stack = jnp.where(row == 0, upper, jnp.where(row == 1, mid, jnp.where(row == 2, low, 0.0))).astype(BF)
+    for layer in range(LAYERS):
+        total = column_sum(dot_nn(stack, adaptive_weight[layer]))
+        mod_ref[layer] = total + adaptive_bias[layer].astype(F32)
+    rows = inputs.shape[1]
+    position = me * rows + lax.broadcasted_iota(jnp.int32, (rows, WIDTH), 0)
+    x = jnp.where(position >= scal[3], mask_embed[...].astype(F32), inputs[0].astype(F32))
+    x_ref[...] = x
+    copy.wait()
+    qkv_stage(x, 0, mod_ref[0], bias_ref, triple, cos_ref, sin_ref, me, h_ref, (c0, c1, c2, c3), hold)
+
+
+def attend_kernel(
+    c0, c1, c2, c3,
+    o0, o1, o2, o3, lse_ref, ot_ref,
+    q_all, k_all, v_turned,
+):
+    rows = c0.shape[1] * 2 // 3
+    rows = 256
+    for place, chunk in enumerate((c0, c1, c2, c3)):
+        span = slice(place * rows, (place + 1) * rows)
+        q_all[place] = chunk[0:rows, 0:GROUP]
+        k_all[span, :] = chunk[0:rows, GROUP : 2 * GROUP]
+        tail = chunk[rows : rows + rows // 2, :]
+        v_block = jnp.concatenate([tail[:, 0:GROUP], tail[:, GROUP : 2 * GROUP]], 0)
+        v_turned[:, span] = v_block.T
+    head = lax.broadcasted_iota(jnp.int32, (rows, GROUP), 1) // HEAD_DIM
+
+    def step(block, carry):
+        q = q_all[block]
+        for number in range(3):
+            masked = jnp.where(head == number, q, jnp.zeros_like(q))
+            scores = dot_nt(k_all[...], masked)
+            peak = jnp.max(scores, 0, keepdims=True)
+            weights = jnp.exp(scores - peak)
+            total = jnp.sum(weights, 0, keepdims=True)
+            span = slice(number * HEAD_DIM, (number + 1) * HEAD_DIM)
+            ot_ref[block, span, :] = dot_nn(v_turned[span, :], weights.astype(BF)) / total
+            lse_ref[block, number : number + 1, :] = peak + jnp.log(total)
+        return carry
+
+    lax.fori_loop(0, 4, step, 0)
+    for place, out in enumerate((o0, o1, o2, o3)):
+        out[...] = pack_rows(ot_ref[place].T).astype(BF)
+
+
+def gather_chunks(refs, hold):
+    for place in range(4):
+        hold[place] = refs[place][...]
+
+
+def mlp_forward(
+    layer, x, mod_row, bias_ref, me, o_refs, output, expand, shrink, waits, hold, o_ref, aout_ref, m_ref, h2_ref,
+    z_ref, slope_ref, f_ref,
+):
+    gather_chunks(o_refs, hold)
+    rows = x.shape[0]
+    half = rows // 2
+    for group in range(4):
+        chunk = hold[group ^ me]
+        columns = slice(group * GROUP, (group + 1) * GROUP)
+        o_ref[0:half, columns] = chunk[:, 0:GROUP]
+        o_ref[half:rows, columns] = chunk[:, GROUP : 2 * GROUP]
+    waits[0].wait()
+    a_out = dot_nn(o_ref[...], output[...]) + bias_of(bias_ref, layer, "output")
+    aout_ref[...] = a_out.astype(BF)
+    m = x + piece_of(mod_row, 2) * a_out
+    m_ref[...] = m
+    unit, _ = normalise(m)
+    h2 = (unit * (1.0 + piece_of(mod_row, 4)) + piece_of(mod_row, 3)).astype(BF)
+    h2_ref[...] = h2
+    waits[1].wait()
+    bias = bias_of(bias_ref, layer, "expand")
+    f = bias_of(bias_ref, layer, "shrink")
+    hidden = expand.shape[1]
+    for start in range(0, hidden, 768):
+        if start == 0:
+            waited = False
+        columns = slice(start, start + 768)
+        u = dot_nn(h2, expand[:, columns]) + bias[:, columns]
+        square = u * u
+        gate = 0.5 + 0.5 * jnp.tanh(u * (ROOT_TWO_PI + ROOT_TWO_PI * CUBIC * square))
+        active = u * gate
+        slope = gate + 2.0 * active * (1.0 - gate) * (ROOT_TWO_PI + 3.0 * ROOT_TWO_PI * CUBIC * square)
+        z = active.astype(BF)
+        z_ref[:, columns] = z
+        slope_ref[:, columns] = slope.astype(BF)
+        if not waited:
+            waits[2].wait()
+            waited = True
+        f = f + dot_nn(z, shrink[columns, :])
+    f_ref[...] = f.astype(BF)
+    return m + piece_of(mod_row, 5) * f
+
+
+def share(values, hold, core, mine_ref, theirs_ref):
+    half = values.shape[1] // 2
+    hold[0] = values[:, 0:half]
+    hold[1] = values[:, half : 2 * half]
+    mine_ref[...] = hold[core]
+    theirs_ref[...] = hold[1 - core]
+
+
+def mlp_backward(
+    dy, mod_row, me, core, m_ref, f_ref, slope_ref, aout_ref, output, expand, shrink, waits, hold, holds,
+    df_refs, du_refs, da_refs, do_refs, dm_ref, vec_ref,
+):
+    def put(place, row):
+        vec_ref[:, place : place + row.shape[1]] = row
+
+    put(0, column_sum(dy * f_ref[...].astype(F32)))
+    df = (dy * piece_of(mod_row, 5)).astype(BF)
+    put(3072, column_sum(df.astype(F32)))
+    share(df, holds[0], core, *df_refs)
+    hidden = expand.shape[1]
+    dh2 = jnp.zeros(dy.shape, F32)
+    waits[2].wait()
+    for start in range(0, hidden, 768):
+        columns = slice(start, start + 768)
+        dz = dot_nt(df, shrink[columns, :])
+        du = (slope_ref[:, columns].astype(F32) * dz).astype(BF)
+        put(3840 + start, column_sum(du.astype(F32)))
+        half = hidden // 2
+        holds[1][start // half, :, start % half : start % half + 768] = du
+        if start == 0:
+            waits[1].wait()
+        dh2 = dh2 + dot_nt(du, expand[:, columns])
+    du_refs[0][...] = holds[1][core]
+    du_refs[1][...] = holds[1][1 - core]
+    unit, rstd = normalise(m_ref[...])
+    put(768, column_sum(dh2))
+    put(1536, column_sum(dh2 * unit))
+    dm = dy + normalise_back(dh2 * (1.0 + piece_of(mod_row, 4)), unit, rstd)
+    dm_ref[...] = dm
+    put(2304, column_sum(dm * aout_ref[...].astype(F32)))
+    da = (dm * piece_of(mod_row, 2)).astype(BF)
+    put(6912, column_sum(da.astype(F32)))
+    share(da, holds[2], core, *da_refs)
+    waits[0].wait()
+    do = dot_nt(da, output[...])
+    for group in range(4):
+        hold[group] = pack_rows(do[:, group * GROUP : (group + 1) * GROUP]).astype(BF)
+    for place in range(4):
+        do_refs[place][...] = hold[place ^ me]
+
+
+def attend_back_kernel(
+    c0, c1, c2, c3, d0, d1, d2, d3, lse_ref, ot_ref, cos_ref, sin_ref,
+    g0, g1, g2, g3,
+    q_masked, do_masked, k_all, v_all, k_turned, lse_rows, delta_rows, dq_turned, dk_all, dv_all,
+):
+    rows = 256
+    head = lax.broadcasted_iota(jnp.int32, (rows, GROUP), 1) // HEAD_DIM
+    for place in range(4):
+        chunk = (c0, c1, c2, c3)[place]
+        given = (d0, d1, d2, d3)[place][...]
+        span = slice(place * rows, (place + 1) * rows)
+        q = chunk[0:rows, 0:GROUP]
+        k = chunk[0:rows, GROUP : 2 * GROUP]
+        tail = chunk[rows : rows + rows // 2, :]
+        v_all[place] = jnp.concatenate([tail[:, 0:GROUP], tail[:, GROUP : 2 * GROUP]], 0)
+        k_all[place] = k
+        k_turned[place] = k.T
+        do = jnp.concatenate([given[:, 0:GROUP], given[:, GROUP : 2 * GROUP]], 0)
+        product = do.astype(F32).T * ot_ref[place]
+        for number in range(3):
+            q_masked[number, span, :] = jnp.where(head == number, q, jnp.zeros_like(q))
+            do_masked[number, span, :] = jnp.where(head == number, do, jnp.zeros_like(do))
+            part = product[number * HEAD_DIM : (number + 1) * HEAD_DIM, :]
+            delta_rows[number : number + 1, span] = jnp.sum(part, 0, keepdims=True)
+            lse_rows[number : number + 1, span] = lse_ref[place, number : number + 1, :]
+    dq_turned[...] = jnp.zeros(dq_turned.shape, F32)
+
+    def step(block, carry):
+        k = k_all[block]
+        v = v_all[block]
+        dk = jnp.zeros((rows, GROUP), F32)
+        dv = jnp.zeros((rows, GROUP), F32)
+        for number in range(3):
+            span = slice(number * HEAD_DIM, (number + 1) * HEAD_DIM)
+            scores = dot_nt(k, q_masked[number])
+            probs = jnp.exp(scores - lse_rows[number : number + 1, :])
+            prob_grad = dot_nt(v, do_masked[number])
+            score_grad = (probs * (prob_grad - delta_rows[number : number + 1, :])).astype(BF)
+            dv = dv + dot_nn(probs.astype(BF), do_masked[number])
+            dk = dk + dot_nn(score_grad, q_masked[number])
+            dq_turned[span, :] += dot_nn(k_turned[block, span, :], score_grad)
+        dk_all[block] = dk
+        dv_all[block] = dv
+        return carry
+
+    lax.fori_loop(0, 4, step, 0)
+    for place, out in enumerate((g0, g1, g2, g3)):
+        span = slice(place * rows, (place + 1) * rows)
+        dq = dq_turned[:, span].T * HEAD_DIM**-0.5
+        pair = jnp.concatenate([dq, dk_all[place]], 1)
+        out[0:rows, :] = turn(pair, cos_ref[place], -sin_ref[place]).astype(BF)
+        out[rows : rows + rows // 2, :] = pack_rows(dv_all[place]).astype(BF)
+
+
+def qkv_backward(x, dm, mod_row, me, core, g_refs, triple, wait, hold, share_hold, full, dqkv_refs, vec_ref):
+    gather_chunks(g_refs, hold)
+    rows = x.shape[0]
+    half = rows // 2
+    for group in range(4):
+        chunk = hold[group ^ me]
+        low = group * GROUP
+        full[:, low : low + GROUP] = chunk[0:rows, 0:GROUP]
+        full[:, WIDTH + low : WIDTH + low + GROUP] = chunk[0:rows, GROUP : 2 * GROUP]
+        full[0:half, 2 * WIDTH + low : 2 * WIDTH + low + GROUP] = chunk[rows : rows + half, 0:GROUP]
+        full[half:rows, 2 * WIDTH + low : 2 * WIDTH + low + GROUP] = chunk[rows : rows + half, GROUP : 2 * GROUP]
+    dqkv = full[...]
+    share(dqkv, share_hold, core, *dqkv_refs)
+    vec_ref[:, 1536:3840] = column_sum(dqkv.astype(F32))
+    wait.wait()
+    dh = dot_nt(dqkv, triple[...])
+    unit, rstd = normalise(x)
+    vec_ref[:, 0:768] = column_sum(dh)
+    vec_ref[:, 768:1536] = column_sum(dh * unit)
+    return dm + normalise_back(dh * (1.0 + piece_of(mod_row, 1)), unit, rstd)
+
+
+def fetch(pairs, sems):
+    copies = []
+    for number, (source, target) in enumerate(pairs):
+        copy = pltpu.make_async_copy(source, target, sems.at[number])
+        copy.start()
+        copies.append(copy)
+    return copies
+
+
+class Done:
+    def wait(self):
+        pass
+
+
+def middle_kernel(
+    scal, x_ref, mod_ref, bias_ref, cos_ref, sin_ref, o0, o1, o2, o3, output_any, expand_any, shrink_any, triple_any,
+    o_ref, aout_ref, m_ref, h2_ref, z_ref, slope_ref, f_ref, y_ref, h_ref, c0, c1, c2, c3,
+    output, expand, shrink, triple, o_hold, c_hold, sems,
+):
+    copies = fetch(
+        [(output_any.at[0], output), (expand_any.at[0], expand), (shrink_any.at[0], shrink), (triple_any.at[1], triple)],
+        sems,
+    )
+    me = scal[0]
+    y = mlp_forward(
+        0, x_ref[...], mod_ref[0], bias_ref, me, (o0, o1, o2, o3), output, expand, shrink, copies, o_hold, o_ref,
+        aout_ref, m_ref, h2_ref, z_ref, slope_ref, f_ref,
+    )
+    y_ref[...] = y
+    copies[3].wait()
+    qkv_stage(y, 1, mod_ref[1], bias_ref, triple, cos_ref, sin_ref, me, h_ref, (c0, c1, c2, c3), c_hold)
+
+
+def peak_kernel(
+    scal, x_ref, mod_ref, bias_ref, cotangent, o0, o1, o2, o3, output_any, expand_any, shrink_any,
+    out_ref, o_ref, h2_ref, z_ref, dfm, dft, dum, dut, dam, dat, d0, d1, d2, d3, dm_ref, vec_ref,
+    output, expand, shrink, o_hold, m_ref, aout_ref, slope_ref, f_ref, df_hold, du_hold, da_hold, sems,
+):
+    copies = fetch([(output_any.at[1], output), (expand_any.at[1], expand), (shrink_any.at[1], shrink)], sems)
+    me, core = scal[0], scal[2]
+    y = mlp_forward(
+        1, x_ref[...], mod_ref[1], bias_ref, me, (o0, o1, o2, o3), output, expand, shrink, copies, o_hold, o_ref,
+        aout_ref, m_ref, h2_ref, z_ref, slope_ref, f_ref,
+    )
+    out_ref[0] = y.astype(BF)
+    mlp_backward(
+        cotangent[0].astype(F32), mod_ref[1], me, core, m_ref, f_ref, slope_ref, aout_ref, output, expand, shrink,
+        [Done()] * 3, o_hold, (df_hold, du_hold, da_hold), (dfm, dft), (dum, dut), (dam, dat), (d0, d1, d2, d3),
+        dm_ref, vec_ref,
+    )
+
+
+def back_kernel(
+    scal, x_ref, dm_in, mod_ref, g0, g1, g2, g3, m_ref, f_ref, slope_ref, aout_ref,
+    triple_any, output_any, expand_any, shrink_any,
+    dqm, dqt, vec_first, dfm, dft, dum, dut, dam, dat, d0, d1, d2, d3, dm_ref, vec_ref,
+    triple, output, expand, shrink, g_hold, dq_hold, full, o_hold, df_hold, du_hold, da_hold, sems,
+):
+    copies = fetch(
+        [(triple_any.at[1], triple), (shrink_any.at[0], shrink), (expand_any.at[0], expand), (output_any.at[0], output)],
+        sems,
+    )
+    me, core = scal[0], scal[2]
+    dy = qkv_backward(
+        x_ref[...], dm_in[...], mod_ref[1], me, core, (g0, g1, g2, g3), triple, copies[0], g_hold, dq_hold, full,
+        (dqm, dqt), vec_first,
+    )
+    mlp_backward(
+        dy, mod_ref[0], me, core, m_ref, f_ref, slope_ref, aout_ref, output, expand, shrink,
+        [copies[3], copies[2], copies[1]], o_hold, (df_hold, du_hold, da_hold), (dfm, dft), (dum, dut), (dam, dat),
+        (d0, d1, d2, d3), dm_ref, vec_ref,
+    )
+
+
+def last_kernel(
+    scal, x_ref, dm_in, mod_ref, g0, g1, g2, g3, triple_any,
+    dqm, dqt, vec_first, input_grad, mask_ref,
+    triple, g_hold, dq_hold, full, sems,
+):
+    copies = fetch([(triple_any.at[0], triple)], sems)
+    me, core = scal[0], scal[2]
+    dx = qkv_backward(
+        x_ref[...], dm_in[...], mod_ref[0], me, core, (g0, g1, g2, g3), triple, copies[0], g_hold, dq_hold, full,
+        (dqm, dqt), vec_first,
+    )
+    rows = dx.shape[0]
+    position = me * rows + lax.broadcasted_iota(jnp.int32, dx.shape, 0)
+    masked = position >= scal[3]
+    input_grad[0] = jnp.where(masked, 0.0, dx)
+    mask_ref[...] = column_sum(jnp.where(masked, dx, 0.0))
+
+
+BIT = {"x": 4, "y": 8, "a": 1, "b": 2}
+ORDERS = ("xyab", "yxab", "abxy")
+STEP = {"x": ("blk", 1), "y": ("blk", 2), "a": ("dp", 2), "b": ("dp", 4)}
+
+
+def place_at(order, index):
+    place = 0
+    for depth, name in enumerate(order):
+        if index & (8 >> depth):
+            place |= BIT[name]
+    return place
+
+
+def deliver(result, rows, me16, send_ref, keep_ref, order, row_at, lane_at):
+    for index in range(16):
+        source = pl.multiple_of((place_at(order, index) ^ me16) * rows, 16)
+        block = result[pl.ds(source, rows), lane_at : lane_at + 128]
+        if index < 8:
+            keep_ref[index, row_at : row_at + rows, :] = block
+        else:
+            send_ref[index - 8, row_at : row_at + rows, :] = block
+
+
+def weights_kernel(
+    counts, scal, a_own, a_far, b_own, b_far, e_own, e_far, g_own, g_far, *rest
+):
+    sends, keeps = rest[0:3], rest[3:6]
+    first, second = rest[6:8]
+    me16 = scal[0] * 4 + scal[1]
+    per_first, per_second = counts
+    first_rows, second_rows = a_own.shape[1] // 16, e_own.shape[1] // 16
+    a = jnp.concatenate([a_own[...], a_far[...]], 0)
+    e = jnp.concatenate([e_own[...], e_far[...]], 0)
+    for part in range(3):
+        order = ORDERS[part]
+        width = per_first * 128
+        columns = slice(part * width, (part + 1) * width)
+        b = jnp.concatenate([b_own[:, columns], b_far[:, columns]], 0)
+        first[...] = dot_tn(a, b).astype(BF)
+        row = 0
+        for number in range(per_first):
+            deliver(first, first_rows, me16, sends[part], keeps[part], order, row, number * 128)
+            row += first_rows
+        width = per_second * 128
+        columns = slice(part * width, (part + 1) * width)
+        g = jnp.concatenate([g_own[:, columns], g_far[:, columns]], 0)
+        second[...] = dot_tn(e, g).astype(BF)
+        for number in range(per_second):
+            deliver(second, second_rows, me16, sends[part], keeps[part], order, row, number * 128)
+            row += second_rows
+
+
+def shaped(*shape, dtype=F32):
+    return jax.ShapeDtypeStruct(shape, dtype)
+
+
+def call(kernel, specs, outs, scratch, cost, name):
+    flops, moved = cost
+    return pl.pallas_call(
+        kernel,
+        in_specs=specs,
+        out_specs=[VM] * len(outs),
+        out_shape=outs,
+        scratch_shapes=scratch,
+        compiler_params=pltpu.CompilerParams(vmem_limit_bytes=VMEM_LIMIT),
+        cost_estimate=pl.CostEstimate(flops=int(flops), bytes_accessed=int(moved), transcendentals=0),
+        name=name,
+    )
+
+
+def swap(values, axis, bit):
+    size = 4 if axis == "blk" else 8
+    return lax.ppermute(values, axis, [(i, i ^ bit) for i in range(size)])
+
+
+def swap_chunks(chunks):
+    return [chunks[0]] + [swap(chunks[place], "blk", place) for place in (1, 2, 3)]
+
+
+def scatter_part(keep, send, order):
+    held = [keep, swap(send, *STEP[order[0]])]
+    for name in order[1:]:
+        half = held[0].shape[0] // 2
+        out = sum(piece[half:].astype(F32) for piece in held).astype(BF)
+        held = [piece[:half] for piece in held]
+        held.append(swap(out, *STEP[name]))
+    return sum(piece[0].astype(F32) for piece in held)
+
+
+def settle(units, core):
+    rows = units.shape[1] // 2
+    mine = lax.dynamic_slice_in_dim(units, core * rows, rows, 1)
+    theirs = lax.dynamic_slice_in_dim(units, (1 - core) * rows, rows, 1)
+    got = swap(theirs, "dp", 1)
+    low = jnp.where(core == 0, mine, got)
+    high = jnp.where(core == 0, got, mine)
+    both = jnp.concatenate([low, high], 0)
+    return jnp.transpose(both, (1, 0, 2)).reshape(rows, both.shape[0] * 128)
+
+
+def weight_gradients(scal, core, a, b, e, g, counts, name):
+    a_width, e_width = a[0].shape[1], e[0].shape[1]
+    rows = counts[0] * a_width // 16 + counts[1] * e_width // 16
+    shapes = [shaped(8, rows, 128, dtype=BF)] * 6
+    flops = 2 * 512 * (a_width * b[0].shape[1] + e_width * g[0].shape[1])
+    outs = call(
+        functools.partial(weights_kernel, counts),
+        [SM] + [VM] * 8,
+        shapes,
+        [pltpu.VMEM((a_width, counts[0] * 128), BF), pltpu.VMEM((e_width, counts[1] * 128), BF)],
+        (flops, 2 * flops // 512),
+        name,
+    )(scal, *a, *b, *e, *g)
+    first, second = [], []
+    a_rows, e_rows = a_width // 16, e_width // 16
+    for part in range(3):
+        total = scatter_part(outs[3 + part], outs[part], ORDERS[part])
+        cut = counts[0] * a_rows
+        first.append(total[:cut].reshape(counts[0], a_rows, 128))
+        second.append(total[cut:].reshape(counts[1], e_rows, 128))
+    return settle(jnp.concatenate(first, 0), core), settle(jnp.concatenate(second, 0), core)
+
+
+def local_fast(
+    inputs, condition, prefix, mask_embed, adaptive_weight, adaptive_bias, triple_weight, triple_bias, output_weight,
+    output_bias, expand_weight, expand_bias, shrink_weight, shrink_bias, cotangent,
+):
+    rows = inputs.shape[1]
+    hidden = expand_weight.shape[2]
+    blk, dp = lax.axis_index("blk"), lax.axis_index("dp")
+    core = dp % 2
+    scal = jnp.stack([blk, dp // 2, core, prefix[0]]).astype(jnp.int32)
+    start = (blk ^ jnp.arange(4, dtype=jnp.int32)) * rows
+    position = (start[:, None] + jnp.arange(rows, dtype=jnp.int32)[None, :]).astype(F32)
+    lane = jnp.arange(128, dtype=jnp.int32)
+    frequency = jnp.exp((lane % 32).astype(F32) * (-2.0 * math.log(10000.0) / HEAD_DIM))
+    angles = position[:, :, None] * frequency
+    cosine = jnp.cos(angles)
+    sine = jnp.sin(angles) * jnp.where(lane % 64 < 32, -1.0, 1.0)
+    biases = jnp.concatenate(
+        [part.astype(F32) for part in (triple_bias, output_bias, expand_bias, shrink_bias)], 1
+    )[:, None, :]
+    conditions = lax.all_gather(condition[0], "dp", axis=0)
+
+    f_square = shaped(rows, WIDTH)
+    b_square = shaped(rows, WIDTH, dtype=BF)
+    b_tall = shaped(rows, hidden, dtype=BF)
+    packed = rows + rows // 2
+    chunk = shaped(packed, 2 * GROUP, dtype=BF)
+    o_chunk = shaped(rows // 2, 2 * GROUP, dtype=BF)
+    c_hold = pltpu.VMEM((4, packed, 2 * GROUP), BF)
+    o_hold = pltpu.VMEM((4, rows // 2, 2 * GROUP), BF)
+    triple_hold = pltpu.VMEM((WIDTH, 3 * WIDTH), BF)
+    output_hold = pltpu.VMEM((WIDTH, WIDTH), BF)
+    expand_hold = pltpu.VMEM((WIDTH, hidden), BF)
+    shrink_hold = pltpu.VMEM((hidden, WIDTH), BF)
+
+    def halved(width):
+        return pltpu.VMEM((2, rows, width // 2), BF)
+
+    def half_pair(width):
+        return [shaped(rows, width // 2, dtype=BF)] * 2
+
+    product = 2 * rows * WIDTH
+    qkv_cost = product * 3 * WIDTH
+    mlp_cost = product * (WIDTH + 2 * hidden)
+
+    x0, mod, h0, *chunks = call(
+        first_kernel,
+        [SM] + [VM] * 8 + [ANY],
+        [f_square, shaped(LAYERS, 1, 6 * WIDTH), b_square] + [chunk] * 4,
+        [triple_hold, c_hold, pltpu.SemaphoreType.DMA((1,))],
+        (qkv_cost, 12e6),
+        "qkv_first",
+    )(
+        scal, inputs, mask_embed[None], condition, adaptive_weight, adaptive_bias[:, None, :], biases, cosine, sine,
+        triple_weight,
+    )
+
+    def attend(chunks):
+        return call(
+            attend_kernel,
+            [VM] * 4,
+            [o_chunk] * 4 + [shaped(4, 8, rows), shaped(4, GROUP, rows)],
+            [
+                pltpu.VMEM((4, rows, GROUP), BF),
+                pltpu.VMEM((4 * rows, GROUP), BF),
+                pltpu.VMEM((GROUP, 4 * rows), BF),
+            ],
+            (6e9, 6e6),
+            "attend",
+        )(*chunks)
+
+    def attend_back(chunks, given, lse, turned):
+        return call(
+            attend_back_kernel,
+            [VM] * 12,
+            [chunk] * 4,
+            [
+                pltpu.VMEM((3, 4 * rows, GROUP), BF),
+                pltpu.VMEM((3, 4 * rows, GROUP), BF),
+                pltpu.VMEM((4, rows, GROUP), BF),
+                pltpu.VMEM((4, rows, GROUP), BF),
+                pltpu.VMEM((4, GROUP, rows), BF),
+                pltpu.VMEM((8, 4 * rows), F32),
+                pltpu.VMEM((8, 4 * rows), F32),
+                pltpu.VMEM((GROUP, 4 * rows), F32),
+                pltpu.VMEM((4, rows, GROUP), F32),
+                pltpu.VMEM((4, rows, GROUP), F32),
+            ],
+            (15e9, 10e6),
+            "attend_back",
+        )(*chunks, *given, lse, turned, cosine, sine)
+
+    chunks0 = swap_chunks(chunks)
+    *o_chunks, lse0, turned0 = attend(chunks0)
+    o_chunks = swap_chunks(o_chunks)
+    o0, aout0, m0, h20, z0, slope0, f0, x1, h1, *chunks = call(
+        middle_kernel,
+        [SM] + [VM] * 9 + [ANY] * 4,
+        [b_square, b_square, f_square, b_square, b_tall, b_tall, b_square, f_square, b_square] + [chunk] * 4,
+        [output_hold, expand_hold, shrink_hold, triple_hold, o_hold, c_hold, pltpu.SemaphoreType.DMA((4,))],
+        (qkv_cost + mlp_cost, 25e6),
+        "mlp_qkv",
+    )(scal, x0, mod, biases, cosine, sine, *o_chunks, output_weight, expand_weight, shrink_weight, triple_weight)
+    chunks1 = swap_chunks(chunks)
+    *o_chunks, lse1, turned1 = attend(chunks1)
+    o_chunks = swap_chunks(o_chunks)
+    back_outs = half_pair(WIDTH) + half_pair(hidden) + half_pair(WIDTH) + [o_chunk] * 4 + [f_square, shaped(1, 7680)]
+    back_holds = [halved(WIDTH), halved(hidden), halved(WIDTH)]
+    outputs, o1, h21, z1, dfm1, dft1, dum1, dut1, dam1, dat1, *given, dm1, vec1 = call(
+        peak_kernel,
+        [SM] + [VM] * 8 + [ANY] * 3,
+        [shaped(1, rows, WIDTH, dtype=BF), b_square, b_square, b_tall] + back_outs,
+        [output_hold, expand_hold, shrink_hold, o_hold]
+        + [
+            pltpu.VMEM((rows, WIDTH), F32),
+            pltpu.VMEM((rows, WIDTH), BF),
+            pltpu.VMEM((rows, hidden), BF),
+            pltpu.VMEM((rows, WIDTH), BF),
+        ]
+        + back_holds
+        + [pltpu.SemaphoreType.DMA((3,))],
+        (2 * mlp_cost, 25e6),
+        "mlp_turn",
+    )(scal, x1, mod, biases, cotangent, *o_chunks, output_weight, expand_weight, shrink_weight)
+
+    def far(values):
+        return swap(values, "dp", 1)
+
+    given = swap_chunks(given)
+    h2_far1, z_far1, h_far1, o_far1 = far(h21), far(z1), far(h1), far(o1)
+    h2_far0, z_far0, h_far0, o_far0 = far(h20), far(z0), far(h0), far(o0)
+    expand1, shrink1 = weight_gradients(
+        scal, core, (h21, h2_far1), (dum1, far(dut1)), (z1, z_far1), (dfm1, far(dft1)), (4, 1), "mlp_weights"
+    )
+    grads = attend_back(chunks1, given, lse1, turned1)
+    grads = swap_chunks(grads)
+    dqm1, dqt1, first1, dfm0, dft0, dum0, dut0, dam0, dat0, *given, dm0, vec0 = call(
+        back_kernel,
+        [SM] + [VM] * 11 + [ANY] * 4,
+        half_pair(3 * WIDTH) + [shaped(1, 3840)] + back_outs,
+        [triple_hold, output_hold, expand_hold, shrink_hold, c_hold, halved(3 * WIDTH)]
+        + [pltpu.VMEM((rows, 3 * WIDTH), BF), o_hold]
+        + back_holds
+        + [pltpu.SemaphoreType.DMA((4,))],
+        (qkv_cost + mlp_cost, 25e6),
+        "qkv_mlp_back",
+    )(
+        scal, x1, dm1, mod, *grads, m0, f0, slope0, aout0, triple_weight, output_weight, expand_weight, shrink_weight
+    )
+    given = swap_chunks(given)
+    triple1, output1 = weight_gradients(
+        scal, core, (h1, h_far1), (dqm1, far(dqt1)), (o1, o_far1), (dam1, far(dat1)), (3, 1), "attention_weights"
+    )
+    expand0, shrink0 = weight_gradients(
+        scal, core, (h20, h2_far0), (dum0, far(dut0)), (z0, z_far0), (dfm0, far(dft0)), (4, 1), "mlp_weights"
+    )
+    grads = attend_back(chunks0, given, lse0, turned0)
+    grads = swap_chunks(grads)
+    dqm0, dqt0, first0, input_grad, mask_term = call(
+        last_kernel,
+        [SM] + [VM] * 7 + [ANY],
+        half_pair(3 * WIDTH) + [shaped(1, 3840), shaped(1, rows, WIDTH), shaped(1, WIDTH)],
+        [triple_hold, c_hold, halved(3 * WIDTH), pltpu.VMEM((rows, 3 * WIDTH), BF), pltpu.SemaphoreType.DMA((1,))],
+        (qkv_cost, 10e6),
+        "qkv_back",
+    )(scal, x0, dm0, mod, *grads, triple_weight)
+    triple0, output0 = weight_gradients(
+        scal, core, (h0, h_far0), (dqm0, far(dqt0)), (o0, o_far0), (dam0, far(dat0)), (3, 1), "attention_weights"
+    )
+
+    small = jnp.concatenate([first0, vec0, first1, vec1, mask_term], 1)
+    small = small + swap(small, "blk", 1)
+    small = small + swap(small, "blk", 2)
+    dmods, sums = [], []
+    for layer in range(LAYERS):
+        first = small[:, layer * 11520 : layer * 11520 + 3840]
+        vec = small[:, layer * 11520 + 3840 : (layer + 1) * 11520]
+        dmods += [first[:, 0:1536], vec[:, 2304:3072], vec[:, 768:2304], vec[:, 0:768]]
+        sums += [first[:, 1536:3840], vec[:, 6912:7680], vec[:, 3840:6912], vec[:, 3072:3840]]
+    dmod = jnp.concatenate(dmods, 1)
+    total = jnp.concatenate(sums + [small[:, 2 * 11520 :]], 1)
+    condition_grad = sum(
+        lax.dot_general(
+            dmod[:, layer * 6 * WIDTH : (layer + 1) * 6 * WIDTH],
+            adaptive_weight[layer].astype(F32),
+            (((1,), (1,)), ((), ())),
+            precision=HIGHEST,
+        )
+        for layer in range(LAYERS)
+    )
+    gathered = dmod
+    for bit in (1, 2, 4):
+        gathered = jnp.concatenate([gathered, swap(gathered, "dp", bit)], 0)
+        total = total + swap(total, "dp", bit)
+    index = blk * 8 + dp
+    share_rows = condition.shape[1] // 32
+    near = conditions[dp ^ jnp.arange(8, dtype=jnp.int32)]
+    near = lax.dynamic_slice_in_dim(near, index * share_rows, share_rows, 1)
+    adaptive_w = jnp.sum(near[:, :, None] * gathered[:, None, :], 0)
+    adaptive_w = jnp.stack([adaptive_w[:, : 6 * WIDTH], adaptive_w[:, 6 * WIDTH :]], 0)
+    adaptive_all = jnp.sum(gathered, 0)
+
+    def cut(values):
+        size = values.shape[0] // 32
+        return lax.dynamic_slice_in_dim(values, index * size, size, 0)
+
+    adaptive_b = jnp.stack([cut(adaptive_all[: 6 * WIDTH]), cut(adaptive_all[6 * WIDTH :])], 0)
+    total = total[0]
+    bias_grads = []
+    for low, high in BIAS_AT.values():
+        bias_grads.append(jnp.stack([cut(total[low:high]), cut(total[6912 + low : 6912 + high])], 0))
+    mask_sum = cut(total[2 * 6912 :])
+    return (
+        outputs,
+        input_grad,
+        condition_grad,
+        mask_sum,
+        adaptive_w,
+        adaptive_b,
+        jnp.stack([triple0, triple1], 0),
+        bias_grads[0],
+        jnp.stack([output0, output1], 0),
+        bias_grads[1],
+        jnp.stack([expand0, expand1], 0),
+        bias_grads[2],
+        jnp.stack([shrink0, shrink1], 0),
+        bias_grads[3],
+    )
+
+
 def solution(mesh):
     in_specs = (
         P("dp", "blk", None),
@@ -482,4 +1258,6 @@
         P(None, ("blk", "dp"), None),
         P(None, ("blk", "dp")),
     )
-    return jax.shard_map(local, mesh=mesh, in_specs=in_specs, out_specs=out_specs, check_vma=False)
+    whole = mesh.shape["blk"] == 4 and mesh.shape["dp"] == 8
+    body = local_fast if whole else local
+    return jax.shard_map(body, mesh=mesh, in_specs=in_specs, out_specs=out_specs, check_vma=False)

time: 1800 us -> 504 us (0.28)
  waiting for transfers between devices: 1440 us -> 189 us
  matrix products: 197 us -> 2.58 us
  Pallas kernels: 0 us -> 132 us
  starting transfers between devices: 0.91 us -> 98 us
  local copies, waits for them, and re-layouts: 74.8 us -> 16.5 us
    reduce_scatter x12 -> x0, waiting for transfers between devices: 1060 us -> none  [the longest x8 946 us: local(): lax.psum_scatter(flat_terms + (mask_term,), ('blk', 'dp'), scatter_dimens...]
    unnamed x20 -> x0, waiting for transfers between devices: 274 us -> none
    dot_general x64 -> x2, matrix products: 197 us -> 2.58 us  [local_fast(): lax.dot_general(dmod[:, layer * 6 * WIDTH:(layer + 1) * 6 * WIDTH], adapt...]
    ppermute x0 -> x104, waiting for transfers between devices: none -> 189 us  [swap(): return lax.ppermute(values, axis, [(i, i ^ bit) for i in range(size)])]
    pallas_call x0 -> x13, Pallas kernels: none -> 132 us  [the longest x2 29.1 us: attend_back(): call(attend_back_kernel, [VM] * 12, [chunk] * 4, [pltpu.VMEM((3, 4 * rows...]
    all_gather x4 -> x0, waiting for transfers between devices: 113 us -> none  [the longest x2 57.7 us: forward_layer(): lax.all_gather(value_flat, 'blk', axis=0, tiled=True)]
    ppermute x0 -> x104, starting transfers between devices: none -> 98 us  [swap(): return lax.ppermute(values, axis, [(i, i ^ bit) for i in range(size)])]
    convert_element_type x5 -> x37, other arithmetic: 1.74 us -> 23.5 us  [the longest x36 23.5 us: scatter_part(): out = sum((piece[half:].astype(F32) for piece in held)).astype(BF)]
  transfers between devices with their start and end apart: 18 -> 104, of which waited for: 18 -> 58; matrix products, arithmetic and copies ran while one was open for 6% -> 9% of each run, Pallas kernels for 0% -> 5%
where the time goes in v1:
time: 504 us; the launch traced here: 499 us
  waiting for transfers between devices  189 us (38%)
  Pallas kernels  132 us (26%)
  starting transfers between devices  98 us (19%)
  other arithmetic  45.2 us (9%)
  local copies, waits for them, and re-layouts  16.5 us (3%)
  blocking collectives  12.4 us (2%)
    ppermute x104, waiting for transfers between devices, swap(): return lax.ppermute(values, axis, [(i, i ^ bit) for i in range(size)])  189 us
    ppermute x104, starting transfers between devices, swap(): return lax.ppermute(values, axis, [(i, i ^ bit) for i in range(size)])  98 us
    pallas_call x2, Pallas kernels, attend_back(): call(attend_back_kernel, [VM] * 12, [chunk] * 4, [pltpu.VMEM((3, 4 * rows...  29.1 us
    pallas_call x4, Pallas kernels, weight_gradients(): call(functools.partial(weights_kernel, counts), [SM] + [VM] * 8, shapes,...  27.2 us
    convert_element_type x36, other arithmetic, scatter_part(): out = sum((piece[half:].astype(F32) for piece in held)).astype(BF)  23.5 us
    pallas_call x2, Pallas kernels, attend(): call(attend_kernel, [VM] * 4, [o_chunk] * 4 + [shaped(4, 8, rows), shaped...  21.5 us
    pallas_call x1, Pallas kernels, local_fast(): call(peak_kernel, [SM] + [VM] * 8 + [ANY] * 3, [shaped(1, rows, WIDTH, dt...  14.7 us
    pallas_call x1, Pallas kernels, local_fast(): call(middle_kernel, [SM] + [VM] * 9 + [ANY] * 4, [b_square, b_square, f_s...  13.6 us
  transfers between devices with their start and end apart: 104, of which 58 were waited for; matrix products, arithmetic and copies ran while one was open for 9% of the time, Pallas kernels for 5%

profile of v1, /device:TPU:0, one launch (start us, length us, event | category | flops | bytes accessed | tf_op | source)
XLA Modules:
  0.0 498.8 jit_solution(13535472833347835231)
XLA Ops:
  5.5 3.1 fusion.18
  9.1 6.8 %qkv_first.1 = (f32[256,768]{1,0:T(8,128)}, f32[2,1,4608]{2,1,0:T(1,128)}, bf16[256,768]{1,0:T(8,128)(2,1)}, bf16[384,384]{1,0:T(8,128)(2,1)}, bf16[384,384]{1,0...) custom-call(s32[4]{0:T(128)} %pad_add_fusion.scal, bf16[1,256,768]{2,1,0:T(8,128)(2,1)} %inputs.1, ...), custom_call_target="tpu_custom_call" | custom-call | flops 905969664 | bytes 12000000 | tf_op jit(solution)/shard_map/qkv_first/pallas_call | solution.py:1042
  15.9 3.0 collective-permute-start
  20.5 6.5 %collective-permute-done.c1 = bf16[384,384]{1,0:T(8,128)(2,1)S(1)} collective-permute-done((bf16[384,384]{1,0:T(8,128)(2,1)}, bf16[384,384]{1,0:T(8,128)(2,1)S(1)}, u32[]{:S(2)}, u32[]{:S(2)}) %collective-permute-start) | collective-permute-done | bytes 294944 | tf_op jit(solution)/shard_map/ppermute | solution.py:947
  27.0 6.9 %collective-permute-done.1.c2 = bf16[384,384]{1,0:T(8,128)(2,1)S(1)} collective-permute-done((bf16[384,384]{1,0:T(8,128)(2,1)}, bf16[384,384]{1,0:T(8,128)(2,1)S(1)}, u32[]{:S(2)}, u32[]{:S(2)}) %collective-permute-start.1) | collective-permute-done | bytes 294944 | tf_op jit(solution)/shard_map/ppermute | solution.py:947
  34.8 10.9 %attend.2 = (bf16[128,384]{1,0:T(8,128)(2,1)}, bf16[128,384]{1,0:T(8,128)(2,1)}, bf16[128,384]{1,0:T(8,128)(2,1)}, bf16[128,384]{1,0:T(8,128)(2,1)}, f32[4,8,256]{2,1,0:T(8,128)}, /*index=5*/f32[4,192,256]{2,1,0:T(8,128)}) custom-call(bf16[384,384]{1,0:T(8,128)(2,1)} %get-tuple-element.116.c0, bf16[384,384]{1,0:T(8,128)(2,1)} %copy-done.49, ...), custom_call_target="tpu_custom_call" | custom-call | flops 6000000000 | bytes 6000000 | tf_op jit(solution)/shard_map/attend/pallas_call | solution.py:1055
  54.1 13.6 %mlp_qkv.1 = (bf16[256,768]{1,0:T(8,128)(2,1)}, bf16[256,768]{1,0:T(8,128)(2,1)}, f32[256,768]{1,0:T(8,128)}, bf16[256,768]{1,0:T(8,128)(2,1)}, bf16[256,3072]{1...) custom-call(s32[4]{0:T(128)} %pad_add_fusion.scal, ...), custom_call_target="tpu_custom_call" | custom-call | flops 3623878656 | bytes 25000000 | tf_op jit(solution)/shard_map/mlp_qkv/pallas_call | solution.py:1092
  71.3 5.8 %collective-permute-done.6.c1 = bf16[384,384]{1,0:T(8,128)(2,1)S(1)} collective-permute-done((bf16[384,384]{1,0:T(8,128)(2,1)}, bf16[384,384]{1,0:T(8,128)(2,1)S(1)}, u32[]{:S(2)}, u32[]{:S(2)}) %collective-permute-start.6) | collective-permute-done | bytes 294944 | tf_op jit(solution)/shard_map/ppermute | solution.py:947
  77.1 5.5 %collective-permute-done.7.c2 = bf16[384,384]{1,0:T(8,128)(2,1)S(1)} collective-permute-done((bf16[384,384]{1,0:T(8,128)(2,1)}, bf16[384,384]{1,0:T(8,128)(2,1)S(1)}, u32[]{:S(2)}, u32[]{:S(2)}) %collective-permute-start.7) | collective-permute-done | bytes 294944 | tf_op jit(solution)/shard_map/ppermute | solution.py:947
  83.4 10.6 %attend.3 = (bf16[128,384]{1,0:T(8,128)(2,1)}, bf16[128,384]{1,0:T(8,128)(2,1)}, bf16[128,384]{1,0:T(8,128)(2,1)}, bf16[128,384]{1,0:T(8,128)(2,1)}, f32[4,8,256]{2,1,0:T(8,128)}, /*index=5*/f32[4,192,256]{2,1,0:T(8,128)}) custom-call(bf16[384,384]{1,0:T(8,128)(2,1)} %get-tuple-element.125.c0, bf16[384,384]{1,0:T(8,128)(2,1)} %copy-done.52, ...), custom_call_target="tpu_custom_call" | custom-call | flops 6000000000 | bytes 6000000 | tf_op jit(solution)/shard_map/attend/pallas_call | solution.py:1055
  102.2 14.7 %mlp_turn.1 = (bf16[1,256,768]{2,1,0:T(8,128)(2,1)}, bf16[256,768]{1,0:T(8,128)(2,1)}, bf16[256,768]{1,0:T(8,128)(2,1)}, bf16[256,3072]{1,0:T(8,128)(2,1)}, bf16...) custom-call(s32[4]{0:T(128)} %pad_add_fusion.scal, ...), custom_call_target="tpu_custom_call" | custom-call | flops 5435817984 | bytes 25000000 | tf_op jit(solution)/shard_map/mlp_turn/pallas_call | solution.py:1105
  122.1 2.7 collective-permute-done.14.d3
  125.5 14.6 %attend_back.2 = (bf16[384,384]{1,0:T(8,128)(2,1)}, bf16[384,384]{1,0:T(8,128)(2,1)}, bf16[384,384]{1,0:T(8,128)(2,1)}, bf16[384,384]{1,0:T(8,128)(2,1)}) custom-call(bf16[384,384]{1,0:T(8,128)(2,1)} %get-tuple-element.125.c0, bf16[384,384]{1,0:T(8,128)(2,1)} %copy-done.52, bf16[384,384]{1,0:T(8,128)(2,1)} %copy-done.53, bf16[384,384]{1,0:T(8,128)(2,1)} %copy-done.54, ...), custom_call_target="tpu_custom_call" | custom-call | flops 15000000512 | bytes 10000000 | tf_op jit(solution)/shard_map/attend_back/pallas_call | solution.py:1069
  143.6 3.9 collective-permute-done.15.g1
  147.5 4.6 collective-permute-done.16.g2
  152.9 12.9 %qkv_mlp_back.1 = (bf16[256,1152]{1,0:T(8,128)(2,1)}, bf16[256,1152]{1,0:T(8,128)(2,1)}, f32[1,3840]{1,0:T(1,128)}, bf16[256,384]{1,0:T(8,128)(2,1)}, bf16[256,3...) custom-call(s32[4]{0:T(128)} %pad_add_fusion.scal, ...), custom_call_target="tpu_custom_call" | custom-call | flops 3623878656 | bytes 25000000 | tf_op jit(solution)/shard_map/qkv_mlp_back/pallas_call | solution.py:1133
  174.4 14.5 %attend_back.3 = (bf16[384,384]{1,0:T(8,128)(2,1)}, bf16[384,384]{1,0:T(8,128)(2,1)}, bf16[384,384]{1,0:T(8,128)(2,1)}, bf16[384,384]{1,0:T(8,128)(2,1)}) custom-call(bf16[384,384]{1,0:T(8,128)(2,1)} %get-tuple-element.116.c0, bf16[384,384]{1,0:T(8,128)(2,1)} %copy-done.49, bf16[384,384]{1,0:T(8,128)(2,1)} %copy-done.50, bf16[384,384]{1,0:T(8,128)(2,1)} %copy-done.51, ...), custom_call_target="tpu_custom_call" | custom-call | flops 15000000512 | bytes 10000000 | tf_op jit(solution)/shard_map/attend_back/pallas_call | solution.py:1069
  192.3 12.4 %all-gather = f32[8,1,128]{2,1,0:T(1,128)S(1)} all-gather(f32[1,1,128]{2,1,0:T(1,128)S(1)} %bitcast.92), channel_id=1, replica_groups=mesh['blk'=4,'dp'=8] {'dp'}, dimensions={0}, use_global_device_ids=true | all-gather | bytes 4608 | tf_op jit(solution)/shard_map/all_gather | solution.py:1017
  205.7 6.3 %qkv_back.1 = (bf16[256,1152]{1,0:T(8,128)(2,1)}, bf16[256,1152]{1,0:T(8,128)(2,1)}, f32[1,3840]{1,0:T(1,128)}, f32[1,256,768]{2,1,0:T(8,128)}, f32[1,768]{1,0:T(1,128)}) custom-call(s32[4]{0:T(128)} %pad_add_fusion.scal, f32[256,768]{1,0:T(8,128)} %get-tuple-element.114.x_ref, f32[256,768]{1,0:T(8,128)} %get-tuple-element.149.dm_in, ...), custom_call_target="tpu_custom_call" | custom-call | flops 905969664 | bytes 10000000 | tf_op jit(solution)/shard_map/qkv_back/pallas_call | solution.py:1155
  215.7 2.7 collective-permute-done.24
  230.6 5.1 %attention_weights.3 = (bf16[8,192,128]{2,1,0:T(8,128)(2,1)}, bf16[8,192,128]{2,1,0:T(8,128)(2,1)}, bf16[8,192,128]{2,1,0:T(8,128)(2,1)}, bf16[8,192,128]{2,1,0:...) custom-call(s32[4]{0:T(128)} %pad_add_fusion.scal, bf16[256,768]{1,0:T(8,128)(2,1)} %get-tuple-element.178.a_own, ...), custom_call_target="tpu_custom_call" | custom-call | flops 1207959552 | bytes 4718592 | tf_op jit(solution)/shard_map/attention_weights/pallas_call | solution.py:980
  237.5 5.0 %collective-permute-done.28 = f32[1,14592]{1,0:T(1,128)S(1)} collective-permute-done((f32[1,14592]{1,0:T(1,128)S(1)}, f32[1,14592]{1,0:T(1,128)S(1)}, u32[]{:S(2)}, u32[]{:S(2)}) %collective-permute-start.28) | collective-permute-done | bytes 58400 | tf_op jit(solution)/shard_map/ppermute | solution.py:947
  249.2 8.5 %mlp_weights.2 = (bf16[8,384,128]{2,1,0:T(8,128)(2,1)}, bf16[8,384,128]{2,1,0:T(8,128)(2,1)}, bf16[8,384,128]{2,1,0:T(8,128)(2,1)}, bf16[8,384,128]{2,1,0:T(8,12...) custom-call(s32[4]{0:T(128)} %pad_add_fusion.scal, bf16[256,768]{1,0:T(8,128)(2,1)} %get-tuple-element.190.a_own, ...), custom_call_target="tpu_custom_call" | custom-call | flops 2415919104 | bytes 9437184 | tf_op jit(solution)/shard_map/mlp_weights/pallas_call | solution.py:980
  263.8 6.6 %collective-permute-done.57 = bf16[8,192,128]{2,1,0:T(8,128)(2,1)S(1)} collective-permute-done((bf16[8,192,128]{2,1,0:T(8,128)(2,1)}, bf16[8,192,128]{2,1,0:T(8,128)(2,1)S(1)}, u32[]{:S(2)}, u32[]{:S(2)}) %collective-permute-start.57) | collective-permute-done | bytes 393248 | tf_op jit(solution)/shard_map/ppermute | solution.py:947
  271.0 3.2 collective-permute-done.53
  274.2 3.4 collective-permute-start.62
  278.5 5.0 %attention_weights.2 = (bf16[8,192,128]{2,1,0:T(8,128)(2,1)}, bf16[8,192,128]{2,1,0:T(8,128)(2,1)}, bf16[8,192,128]{2,1,0:T(8,128)(2,1)}, bf16[8,192,128]{2,1,0:...) custom-call(s32[4]{0:T(128)} %pad_add_fusion.scal, bf16[256,768]{1,0:T(8,128)(2,1)} %get-tuple-element.166.a_own, ...), custom_call_target="tpu_custom_call" | custom-call | flops 1207959552 | bytes 4718592 | tf_op jit(solution)/shard_map/attention_weights/pallas_call | solution.py:980
  285.9 6.5 %collective-permute-done.58 = bf16[4,192,128]{2,1,0:T(8,128)(2,1)S(1)} collective-permute-done((bf16[4,192,128]{2,1,0:T(8,128)(2,1)S(1)}, bf16[4,192,128]{2,1,0:T(8,128)(2,1)S(1)}, u32[]{:S(2)}, u32[]{:S(2)}) %collective-permute-start.58) | collective-permute-done | bytes 196640 | tf_op jit(solution)/shard_map/ppermute | solution.py:947
  292.6 5.7 %collective-permute-done.54 = bf16[4,192,128]{2,1,0:T(8,128)(2,1)S(1)} collective-permute-done((bf16[4,192,128]{2,1,0:T(8,128)(2,1)S(1)}, bf16[4,192,128]{2,1,0:T(8,128)(2,1)S(1)}, u32[]{:S(2)}, u32[]{:S(2)}) %collective-permute-start.54) | collective-permute-done | bytes 196640 | tf_op jit(solution)/shard_map/ppermute | solution.py:947
  302.7 8.5 %mlp_weights.3 = (bf16[8,384,128]{2,1,0:T(8,128)(2,1)}, bf16[8,384,128]{2,1,0:T(8,128)(2,1)}, bf16[8,384,128]{2,1,0:T(8,128)(2,1)}, bf16[8,384,128]{2,1,0:T(8,12...) custom-call(s32[4]{0:T(128)} %pad_add_fusion.scal, bf16[256,768]{1,0:T(8,128)(2,1)} %get-tuple-element.202.a_own, ...), custom_call_target="tpu_custom_call" | custom-call | flops 2415919104 | bytes 9437184 | tf_op jit(solution)/shard_map/mlp_weights/pallas_call | solution.py:980
  311.3 7.2 %collective-permute-done.63 = bf16[2,192,128]{2,1,0:T(8,128)(2,1)S(1)} collective-permute-done((bf16[2,192,128]{2,1,0:T(8,128)(2,1)S(1)}, bf16[2,192,128]{2,1,0:T(8,128)(2,1)S(1)}, u32[]{:S(2)}, u32[]{:S(2)}) %collective-permute-start.63) | collective-permute-done | bytes 98336 | tf_op jit(solution)/shard_map/ppermute | solution.py:947
  320.2 6.5 %collective-permute-done.59 = bf16[2,192,128]{2,1,0:T(8,128)(2,1)S(1)} collective-permute-done((bf16[2,192,128]{2,1,0:T(8,128)(2,1)S(1)}, bf16[2,192,128]{2,1,0:T(8,128)(2,1)S(1)}, u32[]{:S(2)}, u32[]{:S(2)}) %collective-permute-start.59) | collective-permute-done | bytes 98336 | tf_op jit(solution)/shard_map/ppermute | solution.py:947
  326.9 4.4 collective-permute-done.55
  331.6 3.8 collective-permute-done.64
  335.4 5.1 %collective-permute-done.60 = bf16[1,192,128]{2,1,0:T(8,128)(2,1)S(1)} collective-permute-done((bf16[1,192,128]{2,1,0:T(8,128)(2,1)S(1)}, bf16[1,192,128]{2,1,0:T(8,128)(2,1)S(1)}, u32[]{:S(2)}, u32[]{:S(2)}) %collective-permute-start.60) | collective-permute-done | bytes 49184 | tf_op jit(solution)/shard_map/ppermute | solution.py:947
  340.7 4.9 collective-permute-done.56
  350.0 8.6 %collective-permute-done.40 = bf16[8,192,128]{2,1,0:T(8,128)(2,1)S(1)} collective-permute-done((bf16[8,192,128]{2,1,0:T(8,128)(2,1)}, bf16[8,192,128]{2,1,0:T(8,128)(2,1)S(1)}, u32[]{:S(2)}, u32[]{:S(2)}) %collective-permute-start.40) | collective-permute-done | bytes 393248 | tf_op jit(solution)/shard_map/ppermute | solution.py:947
  369.5 10.2 %collective-permute-done.45 = bf16[4,192,128]{2,1,0:T(8,128)(2,1)S(1)} collective-permute-done((bf16[4,192,128]{2,1,0:T(8,128)(2,1)}, bf16[4,192,128]{2,1,0:T(8,128)(2,1)S(1)}, u32[]{:S(2)}, u32[]{:S(2)}) %collective-permute-start.45) | collective-permute-done | bytes 196640 | tf_op jit(solution)/shard_map/ppermute | solution.py:947
  380.0 6.0 %collective-permute-done.41 = bf16[4,192,128]{2,1,0:T(8,128)(2,1)S(1)} collective-permute-done((bf16[4,192,128]{2,1,0:T(8,128)(2,1)S(1)}, bf16[4,192,128]{2,1,0:T(8,128)(2,1)S(1)}, u32[]{:S(2)}, u32[]{:S(2)}) %collective-permute-start.41) | collective-permute-done | bytes 196640 | tf_op jit(solution)/shard_map/ppermute | solution.py:947
  387.6 3.3 collective-permute-done.46
  392.1 4.0 collective-permute-done.42
  398.6 8.1 %collective-permute-done.38 = bf16[2,192,128]{2,1,0:T(8,128)(2,1)S(1)} collective-permute-done((bf16[2,192,128]{2,1,0:T(8,128)(2,1)S(1)}, bf16[2,192,128]{2,1,0:T(8,128)(2,1)S(1)}, u32[]{:S(2)}, u32[]{:S(2)}) %collective-permute-start.38) | collective-permute-done | bytes 98336 | tf_op jit(solution)/shard_map/ppermute | solution.py:947
  407.4 3.4 collective-permute-done.47
  444.3 4.9 collective-permute-done.82
  452.2 2.7 collective-permute-done.78
  463.1 3.0 collective-permute-done.79
  467.1 2.8 collective-permute-done.75
  486.0 2.7 collective-permute-start.92
  (499 shorter events, 184.9 us)
Async XLA Ops:
  15.9 11.1 %collective-permute-start = (bf16[384,384]{1,0:T(8,128)(2,1)}, bf16[384,384]{1,0:T(8,128)(2,1)S(1)}, u32[]{:S(2)}, u32[]{:S(2)}) collective-permute-start(bf16[384,384]{1,0:T(8,128)(2,1)} %get-tuple-element.117), channel_id=1, source_target_pairs={{0,8},{8,0},{16,24},{24,16},{1,9},{9,1},{17,25},{25,17},{2,10},{10... | collective-permute-start | bytes 884744 | tf_op jit(solution)/shard_map/ppermute | solution.py:947
  18.9 15.0 %collective-permute-start.1 = (bf16[384,384]{1,0:T(8,128)(2,1)}, bf16[384,384]{1,0:T(8,128)(2,1)S(1)}, u32[]{:S(2)}, u32[]{:S(2)}) collective-permute-start(bf16[384,384]{1,0:T(8,128)(2,1)} %get-tuple-element.118), channel_id=1, source_target_pairs={{0,16},{8,24},{16,0},{24,8},{1,17},{9,25},{17,1},{25,9},{2,18},{10... | collective-permute-start | bytes 884744 | tf_op jit(solution)/shard_map/ppermute | solution.py:947
  20.5 13.5 %collective-permute-start.2 = (bf16[384,384]{1,0:T(8,128)(2,1)}, bf16[384,384]{1,0:T(8,128)(2,1)S(1)}, u32[]{:S(2)}, u32[]{:S(2)}) collective-permute-start(bf16[384,384]{1,0:T(8,128)(2,1)} %get-tuple-element.119), channel_id=1, source_target_pairs={{0,24},{8,16},{16,8},{24,0},{1,25},{9,17},{17,9},{25,1},{2,26},{10... | collective-permute-start | bytes 884744 | tf_op jit(solution)/shard_map/ppermute | solution.py:947
  67.8 9.3 %collective-permute-start.6 = (bf16[384,384]{1,0:T(8,128)(2,1)}, bf16[384,384]{1,0:T(8,128)(2,1)S(1)}, u32[]{:S(2)}, u32[]{:S(2)}) collective-permute-start(bf16[384,384]{1,0:T(8,128)(2,1)} %get-tuple-element.126), channel_id=1, source_target_pairs={{0,8},{8,0},{16,24},{24,16},{1,9},{9,1},{17,25},{25,17},{2,10},{10... | collective-permute-start | bytes 884744 | tf_op jit(solution)/shard_map/ppermute | solution.py:947
  69.3 13.2 %collective-permute-start.7 = (bf16[384,384]{1,0:T(8,128)(2,1)}, bf16[384,384]{1,0:T(8,128)(2,1)S(1)}, u32[]{:S(2)}, u32[]{:S(2)}) collective-permute-start(bf16[384,384]{1,0:T(8,128)(2,1)} %get-tuple-element.127), channel_id=1, source_target_pairs={{0,16},{8,24},{16,0},{24,8},{1,17},{9,25},{17,1},{25,9},{2,18},{10... | collective-permute-start | bytes 884744 | tf_op jit(solution)/shard_map/ppermute | solution.py:947
  69.8 12.7 %collective-permute-start.8 = (bf16[384,384]{1,0:T(8,128)(2,1)}, bf16[384,384]{1,0:T(8,128)(2,1)S(1)}, u32[]{:S(2)}, u32[]{:S(2)}) collective-permute-start(bf16[384,384]{1,0:T(8,128)(2,1)} %get-tuple-element.128), channel_id=1, source_target_pairs={{0,24},{8,16},{16,8},{24,0},{1,25},{9,17},{17,9},{25,1},{2,26},{10... | collective-permute-start | bytes 884744 | tf_op jit(solution)/shard_map/ppermute | solution.py:947
  140.2 11.9 %collective-permute-start.16 = (bf16[384,384]{1,0:T(8,128)(2,1)}, bf16[384,384]{1,0:T(8,128)(2,1)S(1)}, u32[]{:S(2)}, u32[]{:S(2)}) collective-permute-start(bf16[384,384]{1,0:T(8,128)(2,1)} %get-tuple-element.143), channel_id=1, source_target_pairs={{0,16},{8,24},{16,0},{24,8},{1,17},{9,25},{17,1},{25,9},{2,18},{10... | collective-permute-start | bytes 884744 | tf_op jit(solution)/shard_map/ppermute | solution.py:947
  142.0 10.1 %collective-permute-start.17 = (bf16[384,384]{1,0:T(8,128)(2,1)}, bf16[384,384]{1,0:T(8,128)(2,1)S(1)}, u32[]{:S(2)}, u32[]{:S(2)}) collective-permute-start(bf16[384,384]{1,0:T(8,128)(2,1)} %get-tuple-element.144), channel_id=1, source_target_pairs={{0,24},{8,16},{16,8},{24,0},{1,25},{9,17},{17,9},{25,1},{2,26},{10... | collective-permute-start | bytes 884744 | tf_op jit(solution)/shard_map/ppermute | solution.py:947
  188.8 15.9 %collective-permute-start.21 = (bf16[384,384]{1,0:T(8,128)(2,1)}, bf16[384,384]{1,0:T(8,128)(2,1)S(1)}, u32[]{:S(2)}, u32[]{:S(2)}) collective-permute-start(bf16[384,384]{1,0:T(8,128)(2,1)} %get-tuple-element.157), channel_id=1, source_target_pairs={{0,8},{8,0},{16,24},{24,16},{1,9},{9,1},{17,25},{25,17},{2,10},{10... | collective-permute-start | bytes 884744 | tf_op jit(solution)/shard_map/ppermute | solution.py:947
  190.5 14.2 %collective-permute-start.22 = (bf16[384,384]{1,0:T(8,128)(2,1)}, bf16[384,384]{1,0:T(8,128)(2,1)S(1)}, u32[]{:S(2)}, u32[]{:S(2)}) collective-permute-start(bf16[384,384]{1,0:T(8,128)(2,1)} %get-tuple-element.158), channel_id=1, source_target_pairs={{0,16},{8,24},{16,0},{24,8},{1,17},{9,25},{17,1},{25,9},{2,18},{10... | collective-permute-start | bytes 884744 | tf_op jit(solution)/shard_map/ppermute | solution.py:947
  190.8 13.9 %collective-permute-start.23 = (bf16[384,384]{1,0:T(8,128)(2,1)}, bf16[384,384]{1,0:T(8,128)(2,1)S(1)}, u32[]{:S(2)}, u32[]{:S(2)}) collective-permute-start(bf16[384,384]{1,0:T(8,128)(2,1)} %get-tuple-element.159), channel_id=1, source_target_pairs={{0,24},{8,16},{16,8},{24,0},{1,25},{9,17},{17,9},{25,1},{2,26},{10... | collective-permute-start | bytes 884744 | tf_op jit(solution)/shard_map/ppermute | solution.py:947
  227.5 42.9 %collective-permute-start.32 = (bf16[256,768]{1,0:T(8,128)(2,1)}, bf16[256,768]{1,0:T(8,128)(2,1)}, u32[]{:S(2)}, u32[]{:S(2)}) collective-permute-start(bf16[256,768]{1,0:T(8,128)(2,1)} %get-tuple-element.166.a_own), channel_id=1, source_target_pairs={{0,1},{1,0},{2,3},{3,2},{4,5},{5,4},{6,7},{7,6},{8,9},{9,8},{10,11... | collective-permute-start | bytes 1179656 | tf_op jit(solution)/shard_map/ppermute | solution.py:947
  227.9 18.1 %collective-permute-start.68 = (bf16[256,768]{1,0:T(8,128)(2,1)}, bf16[256,768]{1,0:T(8,128)(2,1)S(1)}, u32[]{:S(2)}, u32[]{:S(2)}) collective-permute-start(bf16[256,768]{1,0:T(8,128)(2,1)} %get-tuple-element.190.a_own), channel_id=1, source_target_pairs={{0,1},{1,0},{2,3},{3,2},{4,5},{5,4},{6,7},{7,6},{8,9},{9,8},{10,11... | collective-permute-start | bytes 1179656 | tf_op jit(solution)/shard_map/ppermute | solution.py:947
  228.2 18.5 %collective-permute-start.70 = (bf16[256,3072]{1,0:T(8,128)(2,1)}, bf16[256,3072]{1,0:T(8,128)(2,1)}, u32[]{:S(2)}, u32[]{:S(2)}) collective-permute-start(bf16[256,3072]{1,0:T(8,128)(2,1)} %get-tuple-element.193.e_own), channel_id=1, source_target_pairs={{0,1},{1,0},{2,3},{3,2},{4,5},{5,4},{6,7},{7,6},{8,9},{9,8},{10,11... | collective-permute-start | bytes 4718600 | tf_op jit(solution)/shard_map/ppermute | solution.py:947
  235.8 10.9 %collective-permute-start.69 = (bf16[256,1536]{1,0:T(8,128)(2,1)S(1)}, bf16[256,1536]{1,0:T(8,128)(2,1)S(1)}, u32[]{:S(2)}, u32[]{:S(2)}) collective-permute-start(bf16[256,1536]{1,0:T(8,128)(2,1)S(1)} %copy-done.40), channel_id=1, source_target_pairs={{0,1},{1,0},{2,3},{3,2},{4,5},{5,4},{6,7},{7,6},{8,9},{9,8},{10,11... | collective-permute-start | bytes 2359304 | tf_op jit(solution)/shard_map/ppermute | solution.py:947
  246.1 56.3 %collective-permute-start.87 = (bf16[256,3072]{1,0:T(8,128)(2,1)}, bf16[256,3072]{1,0:T(8,128)(2,1)}, u32[]{:S(2)}, u32[]{:S(2)}) collective-permute-start(bf16[256,3072]{1,0:T(8,128)(2,1)} %get-tuple-element.205.e_own), channel_id=1, source_target_pairs={{0,1},{1,0},{2,3},{3,2},{4,5},{5,4},{6,7},{7,6},{8,9},{9,8},{10,11... | collective-permute-start | bytes 4718600 | tf_op jit(solution)/shard_map/ppermute | solution.py:947
  246.6 31.7 %collective-permute-start.33 = (bf16[256,1152]{1,0:T(8,128)(2,1)}, bf16[256,1152]{1,0:T(8,128)(2,1)}, u32[]{:S(2)}, u32[]{:S(2)}) collective-permute-start(bf16[256,1152]{1,0:T(8,128)(2,1)} %get-tuple-element.168), channel_id=1, source_target_pairs={{0,1},{1,0},{2,3},{3,2},{4,5},{5,4},{6,7},{7,6},{8,9},{9,8},{10,11... | collective-permute-start | bytes 1769480 | tf_op jit(solution)/shard_map/ppermute | solution.py:947
  246.7 16.7 %collective-permute-start.61 = (bf16[8,192,128]{2,1,0:T(8,128)(2,1)}, bf16[8,192,128]{2,1,0:T(8,128)(2,1)S(1)}, u32[]{:S(2)}, u32[]{:S(2)}) collective-permute-start(bf16[8,192,128]{2,1,0:T(8,128)(2,1)} %get-tuple-element.189), channel_id=1, source_target_pairs={{0,2},{1,3},{2,0},{3,1},{4,6},{5,7},{6,4},{7,5},{8,10},{9,11},{10,... | collective-permute-start | bytes 1179656 | tf_op jit(solution)/shard_map/ppermute | solution.py:947
  246.7 12.6 %collective-permute-start.31 = (f32[4,9216]{1,0:T(4,128)S(1)}, f32[4,9216]{1,0:T(4,128)S(1)}, u32[]{:S(2)}, u32[]{:S(2)}) collective-permute-start(f32[4,9216]{1,0:T(4,128)S(1)} %pad_maximum_fusion.10), channel_id=1, source_target_pairs={{0,4},{1,5},{2,6},{3,7},{4,0},{5,1},{6,2},{7,3},{8,12},{9,13},{10,... | collective-permute-start | bytes 442376 | tf_op jit(solution)/shard_map/ppermute | solution.py:947
  259.3 11.1 %collective-permute-start.57 = (bf16[8,192,128]{2,1,0:T(8,128)(2,1)}, bf16[8,192,128]{2,1,0:T(8,128)(2,1)S(1)}, u32[]{:S(2)}, u32[]{:S(2)}) collective-permute-start(bf16[8,192,128]{2,1,0:T(8,128)(2,1)} %get-tuple-element.187), channel_id=1, source_target_pairs={{0,16},{8,24},{16,0},{24,8},{1,17},{9,25},{17,1},{25,9},{2,18},{10... | collective-permute-start | bytes 1179656 | tf_op jit(solution)/shard_map/ppermute | solution.py:947
  263.4 10.8 %collective-permute-start.53 = (bf16[8,192,128]{2,1,0:T(8,128)(2,1)}, bf16[8,192,128]{2,1,0:T(8,128)(2,1)S(1)}, u32[]{:S(2)}, u32[]{:S(2)}) collective-permute-start(bf16[8,192,128]{2,1,0:T(8,128)(2,1)} %get-tuple-element.185), channel_id=1, source_target_pairs={{0,8},{8,0},{16,24},{24,16},{1,9},{9,1},{17,25},{25,17},{2,10},{10... | collective-permute-start | bytes 1179656 | tf_op jit(solution)/shard_map/ppermute | solution.py:947
  274.2 11.3 %collective-permute-start.62 = (bf16[4,192,128]{2,1,0:T(8,128)(2,1)S(1)}, bf16[4,192,128]{2,1,0:T(8,128)(2,1)S(1)}, u32[]{:S(2)}, u32[]{:S(2)}) collective-permute-start(bf16[4,192,128]{2,1,0:T(8,128)(2,1)S(1)} %add_convert_fusion.12), channel_id=1, source_target_pairs={{0,4},{1,5},{2,6},{3,7},{4,0},{5,1},{6,2},{7,3},{8,12},{9,13},{10,... | collective-permute-start | bytes 589832 | tf_op jit(solution)/shard_map/ppermute | solution.py:947
  277.7 21.0 %collective-permute-start.85 = (bf16[256,768]{1,0:T(8,128)(2,1)}, bf16[256,768]{1,0:T(8,128)(2,1)S(1)}, u32[]{:S(2)}, u32[]{:S(2)}) collective-permute-start(bf16[256,768]{1,0:T(8,128)(2,1)} %get-tuple-element.202.a_own), channel_id=1, source_target_pairs={{0,1},{1,0},{2,3},{3,2},{4,5},{5,4},{6,7},{7,6},{8,9},{9,8},{10,11... | collective-permute-start | bytes 1179656 | tf_op jit(solution)/shard_map/ppermute | solution.py:947
  277.8 22.6 %collective-permute-start.86 = (bf16[256,1536]{1,0:T(8,128)(2,1)S(1)}, bf16[256,1536]{1,0:T(8,128)(2,1)S(1)}, u32[]{:S(2)}, u32[]{:S(2)}) collective-permute-start(bf16[256,1536]{1,0:T(8,128)(2,1)S(1)} %copy-done.39), channel_id=1, source_target_pairs={{0,1},{1,0},{2,3},{3,2},{4,5},{5,4},{6,7},{7,6},{8,9},{9,8},{10,11... | collective-permute-start | bytes 2359304 | tf_op jit(solution)/shard_map/ppermute | solution.py:947
  278.3 20.0 %collective-permute-start.88 = (bf16[256,384]{1,0:T(8,128)(2,1)}, bf16[256,384]{1,0:T(8,128)(2,1)S(1)}, u32[]{:S(2)}, u32[]{:S(2)}) collective-permute-start(bf16[256,384]{1,0:T(8,128)(2,1)} %get-tuple-element.207), channel_id=1, source_target_pairs={{0,1},{1,0},{2,3},{3,2},{4,5},{5,4},{6,7},{7,6},{8,9},{9,8},{10,11... | collective-permute-start | bytes 589832 | tf_op jit(solution)/shard_map/ppermute | solution.py:947
  298.2 64.0 %collective-permute-start.80 = (bf16[8,384,128]{2,1,0:T(8,128)(2,1)}, bf16[8,384,128]{2,1,0:T(8,128)(2,1)}, u32[]{:S(2)}, u32[]{:S(2)}) collective-permute-start(bf16[8,384,128]{2,1,0:T(8,128)(2,1)} %get-tuple-element.201), channel_id=1, source_target_pairs={{0,2},{1,3},{2,0},{3,1},{4,6},{5,7},{6,4},{7,5},{8,10},{9,11},{10,... | collective-permute-start | bytes 2359304 | tf_op jit(solution)/shard_map/ppermute | solution.py:947
  298.3 66.0 %collective-permute-start.76 = (bf16[8,384,128]{2,1,0:T(8,128)(2,1)}, bf16[8,384,128]{2,1,0:T(8,128)(2,1)}, u32[]{:S(2)}, u32[]{:S(2)}) collective-permute-start(bf16[8,384,128]{2,1,0:T(8,128)(2,1)} %get-tuple-element.199), channel_id=1, source_target_pairs={{0,16},{8,24},{16,0},{24,8},{1,17},{9,25},{17,1},{25,9},{2,18},{10... | collective-permute-start | bytes 2359304 | tf_op jit(solution)/shard_map/ppermute | solution.py:947
  298.7 68.2 %collective-permute-start.72 = (bf16[8,384,128]{2,1,0:T(8,128)(2,1)}, bf16[8,384,128]{2,1,0:T(8,128)(2,1)}, u32[]{:S(2)}, u32[]{:S(2)}) collective-permute-start(bf16[8,384,128]{2,1,0:T(8,128)(2,1)} %get-tuple-element.197), channel_id=1, source_target_pairs={{0,8},{8,0},{16,24},{24,16},{1,9},{9,1},{17,25},{25,17},{2,10},{10... | collective-permute-start | bytes 2359304 | tf_op jit(solution)/shard_map/ppermute | solution.py:947
  300.3 47.2 %collective-permute-start.44 = (bf16[8,192,128]{2,1,0:T(8,128)(2,1)}, bf16[8,192,128]{2,1,0:T(8,128)(2,1)S(1)}, u32[]{:S(2)}, u32[]{:S(2)}) collective-permute-start(bf16[8,192,128]{2,1,0:T(8,128)(2,1)} %get-tuple-element.177), channel_id=1, source_target_pairs={{0,2},{1,3},{2,0},{3,1},{4,6},{5,7},{6,4},{7,5},{8,10},{9,11},{10,... | collective-permute-start | bytes 1179656 | tf_op jit(solution)/shard_map/ppermute | solution.py:947
  302.4 16.1 %collective-permute-start.63 = (bf16[2,192,128]{2,1,0:T(8,128)(2,1)S(1)}, bf16[2,192,128]{2,1,0:T(8,128)(2,1)S(1)}, u32[]{:S(2)}, u32[]{:S(2)}) collective-permute-start(bf16[2,192,128]{2,1,0:T(8,128)(2,1)S(1)} %add_convert_fusion.24), channel_id=1, source_target_pairs={{0,8},{8,0},{16,24},{24,16},{1,9},{9,1},{17,25},{25,17},{2,10},{10... | collective-permute-start | bytes 294920 | tf_op jit(solution)/shard_map/ppermute | solution.py:947
  347.1 11.4 %collective-permute-start.40 = (bf16[8,192,128]{2,1,0:T(8,128)(2,1)}, bf16[8,192,128]{2,1,0:T(8,128)(2,1)S(1)}, u32[]{:S(2)}, u32[]{:S(2)}) collective-permute-start(bf16[8,192,128]{2,1,0:T(8,128)(2,1)} %get-tuple-element.175), channel_id=1, source_target_pairs={{0,16},{8,24},{16,0},{24,8},{1,17},{9,25},{17,1},{25,9},{2,18},{10... | collective-permute-start | bytes 1179656 | tf_op jit(solution)/shard_map/ppermute | solution.py:947
  347.6 11.7 %collective-permute-start.36 = (bf16[8,192,128]{2,1,0:T(8,128)(2,1)}, bf16[8,192,128]{2,1,0:T(8,128)(2,1)S(1)}, u32[]{:S(2)}, u32[]{:S(2)}) collective-permute-start(bf16[8,192,128]{2,1,0:T(8,128)(2,1)} %get-tuple-element.173), channel_id=1, source_target_pairs={{0,8},{8,0},{16,24},{24,16},{1,9},{9,1},{17,25},{25,17},{2,10},{10... | collective-permute-start | bytes 1179656 | tf_op jit(solution)/shard_map/ppermute | solution.py:947
  358.5 70.2 %collective-permute-start.97 = (bf16[8,384,128]{2,1,0:T(8,128)(2,1)}, bf16[8,384,128]{2,1,0:T(8,128)(2,1)}, u32[]{:S(2)}, u32[]{:S(2)}) collective-permute-start(bf16[8,384,128]{2,1,0:T(8,128)(2,1)} %get-tuple-element.213), channel_id=1, source_target_pairs={{0,2},{1,3},{2,0},{3,1},{4,6},{5,7},{6,4},{7,5},{8,10},{9,11},{10,... | collective-permute-start | bytes 2359304 | tf_op jit(solution)/shard_map/ppermute | solution.py:947
  360.9 69.2 %collective-permute-start.93 = (bf16[8,384,128]{2,1,0:T(8,128)(2,1)}, bf16[8,384,128]{2,1,0:T(8,128)(2,1)}, u32[]{:S(2)}, u32[]{:S(2)}) collective-permute-start(bf16[8,384,128]{2,1,0:T(8,128)(2,1)} %get-tuple-element.211), channel_id=1, source_target_pairs={{0,16},{8,24},{16,0},{24,8},{1,17},{9,25},{17,1},{25,9},{2,18},{10... | collective-permute-start | bytes 2359304 | tf_op jit(solution)/shard_map/ppermute | solution.py:947
  362.3 71.5 %collective-permute-start.89 = (bf16[8,384,128]{2,1,0:T(8,128)(2,1)}, bf16[8,384,128]{2,1,0:T(8,128)(2,1)}, u32[]{:S(2)}, u32[]{:S(2)}) collective-permute-start(bf16[8,384,128]{2,1,0:T(8,128)(2,1)} %get-tuple-element.209), channel_id=1, source_target_pairs={{0,8},{8,0},{16,24},{24,16},{1,9},{9,1},{17,25},{25,17},{2,10},{10... | collective-permute-start | bytes 2359304 | tf_op jit(solution)/shard_map/ppermute | solution.py:947
  364.4 15.3 %collective-permute-start.45 = (bf16[4,192,128]{2,1,0:T(8,128)(2,1)}, bf16[4,192,128]{2,1,0:T(8,128)(2,1)S(1)}, u32[]{:S(2)}, u32[]{:S(2)}) collective-permute-start(bf16[4,192,128]{2,1,0:T(8,128)(2,1)} %add_convert_fusion.15), channel_id=1, source_target_pairs={{0,4},{1,5},{2,6},{3,7},{4,0},{5,1},{6,2},{7,3},{8,12},{9,13},{10,... | collective-permute-start | bytes 589832 | tf_op jit(solution)/shard_map/ppermute | solution.py:947
  366.9 19.2 %collective-permute-start.41 = (bf16[4,192,128]{2,1,0:T(8,128)(2,1)S(1)}, bf16[4,192,128]{2,1,0:T(8,128)(2,1)S(1)}, u32[]{:S(2)}, u32[]{:S(2)}) collective-permute-start(bf16[4,192,128]{2,1,0:T(8,128)(2,1)S(1)} %copy-done.27), channel_id=1, source_target_pairs={{0,8},{8,0},{16,24},{24,16},{1,9},{9,1},{17,25},{25,17},{2,10},{10... | collective-permute-start | bytes 589832 | tf_op jit(solution)/shard_map/ppermute | solution.py:947
  386.1 50.9 %collective-permute-start.81 = (bf16[4,384,128]{2,1,0:T(8,128)(2,1)S(1)}, bf16[4,384,128]{2,1,0:T(8,128)(2,1)}, u32[]{:S(2)}, u32[]{:S(2)}) collective-permute-start(bf16[4,384,128]{2,1,0:T(8,128)(2,1)S(1)} %add_convert_fusion.3), channel_id=1, source_target_pairs={{0,4},{1,5},{2,6},{3,7},{4,0},{5,1},{6,2},{7,3},{8,12},{9,13},{10,... | collective-permute-start | bytes 1179656 | tf_op jit(solution)/shard_map/ppermute | solution.py:947
  396.0 10.6 %collective-permute-start.38 = (bf16[2,192,128]{2,1,0:T(8,128)(2,1)S(1)}, bf16[2,192,128]{2,1,0:T(8,128)(2,1)S(1)}, u32[]{:S(2)}, u32[]{:S(2)}) collective-permute-start(bf16[2,192,128]{2,1,0:T(8,128)(2,1)S(1)} %add_convert_fusion.29), channel_id=1, source_target_pairs={{0,2},{1,3},{2,0},{3,1},{4,6},{5,7},{6,4},{7,5},{8,10},{9,11},{10,... | collective-permute-start | bytes 294920 | tf_op jit(solution)/shard_map/ppermute | solution.py:947
  424.8 13.3 %collective-permute-start.77 = (bf16[4,384,128]{2,1,0:T(8,128)(2,1)}, bf16[4,384,128]{2,1,0:T(8,128)(2,1)}, u32[]{:S(2)}, u32[]{:S(2)}) collective-permute-start(bf16[4,384,128]{2,1,0:T(8,128)(2,1)} %add_convert_fusion.4), channel_id=1, source_target_pairs={{0,8},{8,0},{16,24},{24,16},{1,9},{9,1},{17,25},{25,17},{2,10},{10... | collective-permute-start | bytes 1179656 | tf_op jit(solution)/shard_map/ppermute | solution.py:947
  428.8 12.5 %collective-permute-start.73 = (bf16[4,384,128]{2,1,0:T(8,128)(2,1)}, bf16[4,384,128]{2,1,0:T(8,128)(2,1)S(1)}, u32[]{:S(2)}, u32[]{:S(2)}) collective-permute-start(bf16[4,384,128]{2,1,0:T(8,128)(2,1)} %add_convert_fusion.5), channel_id=1, source_target_pairs={{0,16},{8,24},{16,0},{24,8},{1,17},{9,25},{17,1},{25,9},{2,18},{10... | collective-permute-start | bytes 1179656 | tf_op jit(solution)/shard_map/ppermute | solution.py:947
  430.1 41.5 %collective-permute-start.98 = (bf16[4,384,128]{2,1,0:T(8,128)(2,1)S(1)}, bf16[4,384,128]{2,1,0:T(8,128)(2,1)S(1)}, u32[]{:S(2)}, u32[]{:S(2)}) collective-permute-start(bf16[4,384,128]{2,1,0:T(8,128)(2,1)S(1)} %add_convert_fusion), channel_id=1, source_target_pairs={{0,4},{1,5},{2,6},{3,7},{4,0},{5,1},{6,2},{7,3},{8,12},{9,13},{10,... | collective-permute-start | bytes 1179656 | tf_op jit(solution)/shard_map/ppermute | solution.py:947
  433.7 39.0 %collective-permute-start.94 = (bf16[4,384,128]{2,1,0:T(8,128)(2,1)S(1)}, bf16[4,384,128]{2,1,0:T(8,128)(2,1)S(1)}, u32[]{:S(2)}, u32[]{:S(2)}) collective-permute-start(bf16[4,384,128]{2,1,0:T(8,128)(2,1)S(1)} %add_convert_fusion.1), channel_id=1, source_target_pairs={{0,8},{8,0},{16,24},{24,16},{1,9},{9,1},{17,25},{25,17},{2,10},{10... | collective-permute-start | bytes 1179656 | tf_op jit(solution)/shard_map/ppermute | solution.py:947
  436.9 37.3 %collective-permute-start.90 = (bf16[4,384,128]{2,1,0:T(8,128)(2,1)S(1)}, bf16[4,384,128]{2,1,0:T(8,128)(2,1)S(1)}, u32[]{:S(2)}, u32[]{:S(2)}) collective-permute-start(bf16[4,384,128]{2,1,0:T(8,128)(2,1)S(1)} %add_convert_fusion.2), channel_id=1, source_target_pairs={{0,16},{8,24},{16,0},{24,8},{1,17},{9,25},{17,1},{25,9},{2,18},{10... | collective-permute-start | bytes 1179656 | tf_op jit(solution)/shard_map/ppermute | solution.py:947
  438.2 11.1 %collective-permute-start.82 = (bf16[2,384,128]{2,1,0:T(8,128)(2,1)S(1)}, bf16[2,384,128]{2,1,0:T(8,128)(2,1)S(1)}, u32[]{:S(2)}, u32[]{:S(2)}) collective-permute-start(bf16[2,384,128]{2,1,0:T(8,128)(2,1)S(1)} %add_convert_fusion.9), channel_id=1, source_target_pairs={{0,8},{8,0},{16,24},{24,16},{1,9},{9,1},{17,25},{25,17},{2,10},{10... | collective-permute-start | bytes 589832 | tf_op jit(solution)/shard_map/ppermute | solution.py:947
  441.2 13.6 %collective-permute-start.78 = (bf16[2,384,128]{2,1,0:T(8,128)(2,1)S(1)}, bf16[2,384,128]{2,1,0:T(8,128)(2,1)S(1)}, u32[]{:S(2)}, u32[]{:S(2)}) collective-permute-start(bf16[2,384,128]{2,1,0:T(8,128)(2,1)S(1)} %add_convert_fusion.10), channel_id=1, source_target_pairs={{0,2},{1,3},{2,0},{3,1},{4,6},{5,7},{6,4},{7,5},{8,10},{9,11},{10,... | collective-permute-start | bytes 589832 | tf_op jit(solution)/shard_map/ppermute | solution.py:947
  449.2 8.8 %collective-permute-start.74 = (bf16[2,384,128]{2,1,0:T(8,128)(2,1)S(1)}, bf16[2,384,128]{2,1,0:T(8,128)(2,1)S(1)}, u32[]{:S(2)}, u32[]{:S(2)}) collective-permute-start(bf16[2,384,128]{2,1,0:T(8,128)(2,1)S(1)} %add_convert_fusion.11), channel_id=1, source_target_pairs={{0,2},{1,3},{2,0},{3,1},{4,6},{5,7},{6,4},{7,5},{8,10},{9,11},{10,... | collective-permute-start | bytes 589832 | tf_op jit(solution)/shard_map/ppermute | solution.py:947
  475.3 9.7 %collective-permute-start.91 = (bf16[2,384,128]{2,1,0:T(8,128)(2,1)S(1)}, bf16[2,384,128]{2,1,0:T(8,128)(2,1)}, u32[]{:S(2)}, u32[]{:S(2)}) collective-permute-start(bf16[2,384,128]{2,1,0:T(8,128)(2,1)S(1)} %add_convert_fusion.8), channel_id=1, source_target_pairs={{0,2},{1,3},{2,0},{3,1},{4,6},{5,7},{6,4},{7,5},{8,10},{9,11},{10,... | collective-permute-start | bytes 589832 | tf_op jit(solution)/shard_map/ppermute | solution.py:947
  (123 other events, 734.7 us)

commit v2 on v1

--- a/solution.py
+++ b/solution.py
@@ -457,8 +457,9 @@
 GROUP = WIDTH // 4
 VM = pl.BlockSpec(memory_space=pltpu.VMEM)
 ANY = pl.BlockSpec(memory_space=pl.ANY)
+HBM = pl.BlockSpec(memory_space=pltpu.HBM)
 SM = pl.BlockSpec(memory_space=pltpu.SMEM)
-VMEM_LIMIT = 58 * 1024 * 1024
+MEBI = 1024 * 1024
 ROOT_TWO_PI = math.sqrt(2.0 / math.pi)
 CUBIC = 0.044715
 
@@ -521,8 +522,13 @@
 
 def qkv_stage(x, layer, mod_row, bias_ref, triple, cos_ref, sin_ref, me, h_ref, chunk_refs, hold):
     unit, _ = normalise(x)
-    h = (unit * (1.0 + piece_of(mod_row, 1)) + piece_of(mod_row, 0)).astype(BF)
-    h_ref[...] = h
+    h = unit * (1.0 + piece_of(mod_row, 1)) + piece_of(mod_row, 0)
+    turned = h.T
+    h = h.astype(BF)
+    each = WIDTH // 32
+    for half in range(2):
+        picked = [turned[each * (b * 8 + z * 2 + half) :][:each] for z in range(4) for b in range(4)]
+        h_ref[half] = jnp.concatenate(picked, 0).astype(BF)
     bias = bias_of(bias_ref, layer, "triple")
     cosine, sine = cos_ref[0], sin_ref[0]
     parts = []
@@ -567,7 +573,9 @@
     x = jnp.where(position >= scal[3], mask_embed[...].astype(F32), inputs[0].astype(F32))
     x_ref[...] = x
     copy.wait()
-    qkv_stage(x, 0, mod_ref[0], bias_ref, triple, cos_ref, sin_ref, me, h_ref, (c0, c1, c2, c3), hold)
+    qkv_stage(
+        x, 0, mod_ref[0], bias_ref, triple, cos_ref, sin_ref, me, h_ref, (c0, c1, c2, c3), hold,
+    )
 
 
 def attend_kernel(
@@ -610,8 +618,8 @@
 
 
 def mlp_forward(
-    layer, x, mod_row, bias_ref, me, o_refs, output, expand, shrink, waits, hold, o_ref, aout_ref, m_ref, h2_ref,
-    z_ref, slope_ref, f_ref,
+    layer, x, mod_row, bias_ref, me, o_refs, output, expand, shrink, waits, hold, o_ref, aout_ref, m_ref, turned_ref,
+    slope_ref, f_ref,
 ):
     gather_chunks(o_refs, hold)
     rows = x.shape[0]
@@ -621,21 +629,21 @@
         columns = slice(group * GROUP, (group + 1) * GROUP)
         o_ref[0:half, columns] = chunk[:, 0:GROUP]
         o_ref[half:rows, columns] = chunk[:, GROUP : 2 * GROUP]
+    o = o_ref[...]
+    hidden = expand.shape[1]
+    turned_ref[hidden + WIDTH : hidden + 2 * WIDTH, :] = o.T
     waits[0].wait()
-    a_out = dot_nn(o_ref[...], output[...]) + bias_of(bias_ref, layer, "output")
+    a_out = dot_nn(o, output[...]) + bias_of(bias_ref, layer, "output")
     aout_ref[...] = a_out.astype(BF)
     m = x + piece_of(mod_row, 2) * a_out
     m_ref[...] = m
     unit, _ = normalise(m)
     h2 = (unit * (1.0 + piece_of(mod_row, 4)) + piece_of(mod_row, 3)).astype(BF)
-    h2_ref[...] = h2
+    turned_ref[hidden : hidden + WIDTH, :] = h2.T
     waits[1].wait()
     bias = bias_of(bias_ref, layer, "expand")
     f = bias_of(bias_ref, layer, "shrink")
-    hidden = expand.shape[1]
     for start in range(0, hidden, 768):
-        if start == 0:
-            waited = False
         columns = slice(start, start + 768)
         u = dot_nn(h2, expand[:, columns]) + bias[:, columns]
         square = u * u
@@ -643,27 +651,24 @@
         active = u * gate
         slope = gate + 2.0 * active * (1.0 - gate) * (ROOT_TWO_PI + 3.0 * ROOT_TWO_PI * CUBIC * square)
         z = active.astype(BF)
-        z_ref[:, columns] = z
+        turned_ref[columns, :] = z.T
         slope_ref[:, columns] = slope.astype(BF)
-        if not waited:
+        if start == 0:
             waits[2].wait()
-            waited = True
         f = f + dot_nn(z, shrink[columns, :])
     f_ref[...] = f.astype(BF)
     return m + piece_of(mod_row, 5) * f
 
 
-def share(values, hold, core, mine_ref, theirs_ref):
+def share(values, hold, at):
     half = values.shape[1] // 2
-    hold[0] = values[:, 0:half]
-    hold[1] = values[:, half : 2 * half]
-    mine_ref[...] = hold[core]
-    theirs_ref[...] = hold[1 - core]
+    hold[0, :, at : at + half] = values[:, 0:half]
+    hold[1, :, at : at + half] = values[:, half : 2 * half]
 
 
 def mlp_backward(
-    dy, mod_row, me, core, m_ref, f_ref, slope_ref, aout_ref, output, expand, shrink, waits, hold, holds,
-    df_refs, du_refs, da_refs, do_refs, dm_ref, vec_ref,
+    dy, mod_row, me, core, m_ref, f_ref, slope_ref, aout_ref, output, expand, shrink, waits, hold, halves,
+    do_refs, dm_ref, vec_ref,
 ):
     def put(place, row):
         vec_ref[:, place : place + row.shape[1]] = row
@@ -671,8 +676,8 @@
     put(0, column_sum(dy * f_ref[...].astype(F32)))
     df = (dy * piece_of(mod_row, 5)).astype(BF)
     put(3072, column_sum(df.astype(F32)))
-    share(df, holds[0], core, *df_refs)
     hidden = expand.shape[1]
+    share(df, halves, hidden // 2)
     dh2 = jnp.zeros(dy.shape, F32)
     waits[2].wait()
     for start in range(0, hidden, 768):
@@ -681,12 +686,10 @@
         du = (slope_ref[:, columns].astype(F32) * dz).astype(BF)
         put(3840 + start, column_sum(du.astype(F32)))
         half = hidden // 2
-        holds[1][start // half, :, start % half : start % half + 768] = du
+        halves[start // half, :, start % half : start % half + 768] = du
         if start == 0:
             waits[1].wait()
         dh2 = dh2 + dot_nt(du, expand[:, columns])
-    du_refs[0][...] = holds[1][core]
-    du_refs[1][...] = holds[1][1 - core]
     unit, rstd = normalise(m_ref[...])
     put(768, column_sum(dh2))
     put(1536, column_sum(dh2 * unit))
@@ -695,7 +698,7 @@
     put(2304, column_sum(dm * aout_ref[...].astype(F32)))
     da = (dm * piece_of(mod_row, 2)).astype(BF)
     put(6912, column_sum(da.astype(F32)))
-    share(da, holds[2], core, *da_refs)
+    share(da, halves, hidden // 2 + WIDTH // 2)
     waits[0].wait()
     do = dot_nt(da, output[...])
     for group in range(4):
@@ -706,7 +709,7 @@
 
 def attend_back_kernel(
     c0, c1, c2, c3, d0, d1, d2, d3, lse_ref, ot_ref, cos_ref, sin_ref,
-    g0, g1, g2, g3,
+    g0, g1, g2, g3, stacked,
     q_masked, do_masked, k_all, v_all, k_turned, lse_rows, delta_rows, dq_turned, dk_all, dv_all,
 ):
     rows = 256
@@ -754,11 +757,14 @@
         span = slice(place * rows, (place + 1) * rows)
         dq = dq_turned[:, span].T * HEAD_DIM**-0.5
         pair = jnp.concatenate([dq, dk_all[place]], 1)
-        out[0:rows, :] = turn(pair, cos_ref[place], -sin_ref[place]).astype(BF)
-        out[rows : rows + rows // 2, :] = pack_rows(dv_all[place]).astype(BF)
-
-
-def qkv_backward(x, dm, mod_row, me, core, g_refs, triple, wait, hold, share_hold, full, dqkv_refs, vec_ref):
+        pair = turn(pair, cos_ref[place], -sin_ref[place]).astype(BF)
+        tail = pack_rows(dv_all[place]).astype(BF)
+        for target in (out, stacked.at[place]):
+            target[0:rows, :] = pair
+            target[rows : rows + rows // 2, :] = tail
+
+
+def qkv_backward(x, dm, mod_row, me, g_refs, triple, wait, hold, full, vec_ref):
     gather_chunks(g_refs, hold)
     rows = x.shape[0]
     half = rows // 2
@@ -770,7 +776,6 @@
         full[0:half, 2 * WIDTH + low : 2 * WIDTH + low + GROUP] = chunk[rows : rows + half, 0:GROUP]
         full[half:rows, 2 * WIDTH + low : 2 * WIDTH + low + GROUP] = chunk[rows : rows + half, GROUP : 2 * GROUP]
     dqkv = full[...]
-    share(dqkv, share_hold, core, *dqkv_refs)
     vec_ref[:, 1536:3840] = column_sum(dqkv.astype(F32))
     wait.wait()
     dh = dot_nt(dqkv, triple[...])
@@ -796,8 +801,8 @@
 
 def middle_kernel(
     scal, x_ref, mod_ref, bias_ref, cos_ref, sin_ref, o0, o1, o2, o3, output_any, expand_any, shrink_any, triple_any,
-    o_ref, aout_ref, m_ref, h2_ref, z_ref, slope_ref, f_ref, y_ref, h_ref, c0, c1, c2, c3,
-    output, expand, shrink, triple, o_hold, c_hold, sems,
+    aout_ref, m_ref, turned_ref, slope_ref, f_ref, y_ref, h_ref, c0, c1, c2, c3,
+    output, expand, shrink, triple, o_hold, o_ref, c_hold, sems,
 ):
     copies = fetch(
         [(output_any.at[0], output), (expand_any.at[0], expand), (shrink_any.at[0], shrink), (triple_any.at[1], triple)],
@@ -806,37 +811,48 @@
     me = scal[0]
     y = mlp_forward(
         0, x_ref[...], mod_ref[0], bias_ref, me, (o0, o1, o2, o3), output, expand, shrink, copies, o_hold, o_ref,
-        aout_ref, m_ref, h2_ref, z_ref, slope_ref, f_ref,
+        aout_ref, m_ref, turned_ref, slope_ref, f_ref,
     )
     y_ref[...] = y
     copies[3].wait()
-    qkv_stage(y, 1, mod_ref[1], bias_ref, triple, cos_ref, sin_ref, me, h_ref, (c0, c1, c2, c3), c_hold)
-
-
-def peak_kernel(
-    scal, x_ref, mod_ref, bias_ref, cotangent, o0, o1, o2, o3, output_any, expand_any, shrink_any,
-    out_ref, o_ref, h2_ref, z_ref, dfm, dft, dum, dut, dam, dat, d0, d1, d2, d3, dm_ref, vec_ref,
-    output, expand, shrink, o_hold, m_ref, aout_ref, slope_ref, f_ref, df_hold, du_hold, da_hold, sems,
+    qkv_stage(
+        y, 1, mod_ref[1], bias_ref, triple, cos_ref, sin_ref, me, h_ref, (c0, c1, c2, c3), c_hold,
+    )
+
+
+def ahead_kernel(
+    scal, x_ref, mod_ref, bias_ref, o0, o1, o2, o3, output_any, expand_any, shrink_any,
+    out_ref, aout_ref, m_ref, turned_ref, slope_ref, f_ref,
+    output, expand, shrink, o_hold, o_ref, sems,
 ):
     copies = fetch([(output_any.at[1], output), (expand_any.at[1], expand), (shrink_any.at[1], shrink)], sems)
+    y = mlp_forward(
+        1, x_ref[...], mod_ref[1], bias_ref, scal[0], (o0, o1, o2, o3), output, expand, shrink, copies, o_hold, o_ref,
+        aout_ref, m_ref, turned_ref, slope_ref, f_ref,
+    )
+    out_ref[0] = y.astype(BF)
+
+
+def turn_kernel(
+    scal, cotangent, mod_ref, m_ref, f_ref, slope_ref, aout_ref, output_any, expand_any, shrink_any,
+    mine, theirs, d0, d1, d2, d3, dm_ref, vec_ref,
+    output, expand, shrink, o_hold, halves, sems,
+):
+    copies = fetch([(shrink_any.at[1], shrink), (expand_any.at[1], expand), (output_any.at[1], output)], sems)
     me, core = scal[0], scal[2]
-    y = mlp_forward(
-        1, x_ref[...], mod_ref[1], bias_ref, me, (o0, o1, o2, o3), output, expand, shrink, copies, o_hold, o_ref,
-        aout_ref, m_ref, h2_ref, z_ref, slope_ref, f_ref,
-    )
-    out_ref[0] = y.astype(BF)
     mlp_backward(
         cotangent[0].astype(F32), mod_ref[1], me, core, m_ref, f_ref, slope_ref, aout_ref, output, expand, shrink,
-        [Done()] * 3, o_hold, (df_hold, du_hold, da_hold), (dfm, dft), (dum, dut), (dam, dat), (d0, d1, d2, d3),
-        dm_ref, vec_ref,
-    )
+        [copies[2], copies[1], copies[0]], o_hold, halves, (d0, d1, d2, d3), dm_ref, vec_ref,
+    )
+    mine[...] = halves[core]
+    theirs[...] = halves[1 - core]
 
 
 def back_kernel(
     scal, x_ref, dm_in, mod_ref, g0, g1, g2, g3, m_ref, f_ref, slope_ref, aout_ref,
     triple_any, output_any, expand_any, shrink_any,
-    dqm, dqt, vec_first, dfm, dft, dum, dut, dam, dat, d0, d1, d2, d3, dm_ref, vec_ref,
-    triple, output, expand, shrink, g_hold, dq_hold, full, o_hold, df_hold, du_hold, da_hold, sems,
+    mine, theirs, vec_first, d0, d1, d2, d3, dm_ref, vec_ref,
+    triple, output, expand, shrink, g_hold, full, o_hold, halves, sems,
 ):
     copies = fetch(
         [(triple_any.at[1], triple), (shrink_any.at[0], shrink), (expand_any.at[0], expand), (output_any.at[0], output)],
@@ -844,26 +860,25 @@
     )
     me, core = scal[0], scal[2]
     dy = qkv_backward(
-        x_ref[...], dm_in[...], mod_ref[1], me, core, (g0, g1, g2, g3), triple, copies[0], g_hold, dq_hold, full,
-        (dqm, dqt), vec_first,
+        x_ref[...], dm_in[...], mod_ref[1], me, (g0, g1, g2, g3), triple, copies[0], g_hold, full, vec_first,
     )
     mlp_backward(
         dy, mod_ref[0], me, core, m_ref, f_ref, slope_ref, aout_ref, output, expand, shrink,
-        [copies[3], copies[2], copies[1]], o_hold, (df_hold, du_hold, da_hold), (dfm, dft), (dum, dut), (dam, dat),
-        (d0, d1, d2, d3), dm_ref, vec_ref,
-    )
+        [copies[3], copies[2], copies[1]], o_hold, halves, (d0, d1, d2, d3), dm_ref, vec_ref,
+    )
+    mine[...] = halves[core]
+    theirs[...] = halves[1 - core]
 
 
 def last_kernel(
     scal, x_ref, dm_in, mod_ref, g0, g1, g2, g3, triple_any,
-    dqm, dqt, vec_first, input_grad, mask_ref,
-    triple, g_hold, dq_hold, full, sems,
+    vec_first, input_grad, mask_ref,
+    triple, g_hold, full, sems,
 ):
     copies = fetch([(triple_any.at[0], triple)], sems)
-    me, core = scal[0], scal[2]
+    me = scal[0]
     dx = qkv_backward(
-        x_ref[...], dm_in[...], mod_ref[0], me, core, (g0, g1, g2, g3), triple, copies[0], g_hold, dq_hold, full,
-        (dqm, dqt), vec_first,
+        x_ref[...], dm_in[...], mod_ref[0], me, (g0, g1, g2, g3), triple, copies[0], g_hold, full, vec_first,
     )
     rows = dx.shape[0]
     position = me * rows + lax.broadcasted_iota(jnp.int32, dx.shape, 0)
@@ -872,8 +887,50 @@
     mask_ref[...] = column_sum(jnp.where(masked, dx, 0.0))
 
 
+def triple_kernel(
+    scal, h0, h1, h2, h3, chunks,
+    mine, theirs,
+    result,
+):
+    rows = chunks.shape[1] * 2 // 3
+    half = rows // 2
+    each = WIDTH // 8
+    for side in range(2):
+        qk = jnp.zeros((WIDTH // 2, 2 * GROUP), F32)
+        v = jnp.zeros((WIDTH // 2, GROUP), F32)
+        for place, h_ref in enumerate((h0, h1, h2, h3)):
+            h = h_ref[side]
+            qk = qk + dot_nn(h, chunks[place, 0:rows, :])
+            tail = chunks[place, rows : rows + half, :]
+            v = v + dot_nn(h, jnp.concatenate([tail[:, 0:GROUP], tail[:, GROUP : 2 * GROUP]], 0))
+        for z in range(4):
+            span = slice(z * each, (z + 1) * each)
+            result[side * 4 + z, 0:each, :] = qk[span].astype(BF)
+            result[side * 4 + z, each : each + each // 2, :] = pack_rows(v[span]).astype(BF)
+    for place, offset in enumerate((0, 2, 1, 3)):
+        at = scal[1] ^ offset
+        mine[place] = result[scal[2] * 4 + at]
+        theirs[place] = result[(1 - scal[2]) * 4 + at]
+
+
+def triple_settle_kernel(
+    scal, keep, core, first, second,
+    b0, b1, b2, b3,
+    hold,
+):
+    each = WIDTH // 8
+    total = keep[0].astype(F32) + core[0].astype(F32) + first[0].astype(F32) + second[0].astype(F32)
+    v = jnp.concatenate([total[each:, 0:GROUP], total[each:, GROUP : 2 * GROUP]], 0)
+    rows = WIDTH // 32
+    for b in range(4):
+        span = slice(b * rows, (b + 1) * rows)
+        hold[b, :, 0 : 2 * GROUP] = total[span]
+        hold[b, :, 2 * GROUP : 3 * GROUP] = v[span]
+    for place, out in enumerate((b0, b1, b2, b3)):
+        out[...] = hold[place ^ scal[0]]
+
+
 BIT = {"x": 4, "y": 8, "a": 1, "b": 2}
-ORDERS = ("xyab", "yxab", "abxy")
 STEP = {"x": ("blk", 1), "y": ("blk", 2), "a": ("dp", 2), "b": ("dp", 4)}
 
 
@@ -885,61 +942,108 @@
     return place
 
 
-def deliver(result, rows, me16, send_ref, keep_ref, order, row_at, lane_at):
-    for index in range(16):
-        source = pl.multiple_of((place_at(order, index) ^ me16) * rows, 16)
-        block = result[pl.ds(source, rows), lane_at : lane_at + 128]
-        if index < 8:
-            keep_ref[index, row_at : row_at + rows, :] = block
-        else:
-            send_ref[index - 8, row_at : row_at + rows, :] = block
-
-
-def weights_kernel(
-    counts, scal, a_own, a_far, b_own, b_far, e_own, e_far, g_own, g_far, *rest
-):
-    sends, keeps = rest[0:3], rest[3:6]
-    first, second = rest[6:8]
+def weights_kernel(products, orders, scal, own, far, mine, got, *rest):
+    count = len(orders)
+    sends, keeps, holds = rest[0:count], rest[count : 2 * count], rest[2 * count :]
     me16 = scal[0] * 4 + scal[1]
-    per_first, per_second = counts
-    first_rows, second_rows = a_own.shape[1] // 16, e_own.shape[1] // 16
-    a = jnp.concatenate([a_own[...], a_far[...]], 0)
-    e = jnp.concatenate([e_own[...], e_far[...]], 0)
-    for part in range(3):
-        order = ORDERS[part]
-        width = per_first * 128
-        columns = slice(part * width, (part + 1) * width)
-        b = jnp.concatenate([b_own[:, columns], b_far[:, columns]], 0)
-        first[...] = dot_tn(a, b).astype(BF)
+    for part, order in enumerate(orders):
+        row_at = 0
+        for (low, high, at, dealt), hold in zip(products, holds):
+            blocks = dealt[part]
+            begin = at + sum(dealt[:part]) * 128
+            columns = slice(begin, begin + blocks * 128)
+            hold[:, 0 : blocks * 128] = (
+                dot_nn(own[low:high, :], mine[:, columns]) + dot_nn(far[low:high, :], got[:, columns])
+            ).astype(BF)
+            rows = (high - low) // 16
+            for index in range(16):
+                start = pl.multiple_of((place_at(order, index) ^ me16) * rows, 16)
+                target = keeps[part] if index < 8 else sends[part]
+                for number in range(blocks):
+                    lane = number * 128
+                    spot = row_at + number * rows
+                    target[index % 8, spot : spot + rows, :] = hold[pl.ds(start, rows), lane : lane + 128]
+            row_at += blocks * rows
+
+
+def settle_kernel(spans, scal, *refs):
+    pieces, (mine, theirs), (hold, sems) = refs[:-4], refs[-4:-2], refs[-2:]
+    sizes = [sum(blocks) for blocks in spans[1]]
+    each = (len(pieces) - 1) // len(sizes)
+    sources = []
+    for part, size in enumerate(sizes):
+        sources += [piece.at[0] for piece in pieces[part * each : (part + 1) * each]]
+        sources.append(pieces[-1].at[0, sum(sizes[:part]) : sum(sizes[: part + 1]), :])
+    each += 1
+    copies = []
+    for number, source in enumerate(sources):
+        copy = pltpu.make_async_copy(source, hold.at[number, 0 : source.shape[0], :], sems.at[number])
+        copy.start()
+        copies.append(copy)
+    for copy in copies:
+        copy.wait()
+    core = scal[2]
+    at = 0
+    for part, blocks in enumerate(spans[1]):
         row = 0
-        for number in range(per_first):
-            deliver(first, first_rows, me16, sends[part], keeps[part], order, row, number * 128)
-            row += first_rows
-        width = per_second * 128
-        columns = slice(part * width, (part + 1) * width)
-        g = jnp.concatenate([g_own[:, columns], g_far[:, columns]], 0)
-        second[...] = dot_tn(e, g).astype(BF)
-        for number in range(per_second):
-            deliver(second, second_rows, me16, sends[part], keeps[part], order, row, number * 128)
-            row += second_rows
+        for rows in blocks:
+            half = rows // 2
+            total = hold[part * each, row : row + rows, :].astype(F32)
+            for number in range(1, each):
+                total = total + hold[part * each + number, row : row + rows, :].astype(F32)
+            low, high = total[0:half], total[half:rows]
+            mine[at : at + half, :] = jnp.where(core == 0, low, high)
+            theirs[at : at + half, :] = jnp.where(core == 0, high, low)
+            row += rows
+            at += half
+
+
+def finish_kernel(plans, scal, *refs):
+    pairs = 2 * len(plans)
+    groups = refs[pairs : pairs + 4 * LAYERS]
+    outs, hold = refs[pairs + 4 * LAYERS : -1], refs[-1]
+    core = scal[2]
+    for bucket, plan in enumerate(plans):
+        mine, got = refs[2 * bucket : 2 * bucket + 2]
+        at = 0
+        for out, layer, block, rows in plan:
+            own, other = mine[at : at + rows, :], got[at : at + rows, :]
+            half = outs[out].shape[2] // 2
+            low = block * 128
+            outs[out][layer, :, low : low + 128] = jnp.where(core == 0, own, other)
+            outs[out][layer, :, half + low : half + low + 128] = jnp.where(core == 0, other, own)
+            at += rows
+    for layer in range(LAYERS):
+        for place in range(4):
+            hold[place] = groups[layer * 4 + place][...]
+        for group in range(4):
+            block = hold[group ^ scal[0]]
+            for number in range(3):
+                low = number * WIDTH + group * GROUP
+                outs[0][layer, :, low : low + GROUP] = block[:, number * GROUP : (number + 1) * GROUP]
 
 
 def shaped(*shape, dtype=F32):
     return jax.ShapeDtypeStruct(shape, dtype)
 
 
-def call(kernel, specs, outs, scratch, cost, name):
-    flops, moved = cost
-    return pl.pallas_call(
-        kernel,
-        in_specs=specs,
+def call(kernel, specs, outs, scratch, micros, name, limit, after=()):
+    count, extra = len(specs), len(after)
+
+    def body(*refs):
+        kernel(*refs[:count], *refs[count + extra :])
+
+    made = pl.pallas_call(
+        body,
+        in_specs=specs + [ANY] * extra,
         out_specs=[VM] * len(outs),
         out_shape=outs,
         scratch_shapes=scratch,
-        compiler_params=pltpu.CompilerParams(vmem_limit_bytes=VMEM_LIMIT),
-        cost_estimate=pl.CostEstimate(flops=int(flops), bytes_accessed=int(moved), transcendentals=0),
+        compiler_params=pltpu.CompilerParams(vmem_limit_bytes=limit * MEBI),
+        cost_estimate=pl.CostEstimate(flops=int(micros * 1e9), bytes_accessed=int(micros * 1e6), transcendentals=0),
         name=name,
     )
+    return lambda *operands: made(*operands, *after)
 
 
 def swap(values, axis, bit):
@@ -951,48 +1055,114 @@
     return [chunks[0]] + [swap(chunks[place], "blk", place) for place in (1, 2, 3)]
 
 
-def scatter_part(keep, send, order):
-    held = [keep, swap(send, *STEP[order[0]])]
-    for name in order[1:]:
-        half = held[0].shape[0] // 2
-        out = sum(piece[half:].astype(F32) for piece in held).astype(BF)
-        held = [piece[:half] for piece in held]
-        held.append(swap(out, *STEP[name]))
-    return sum(piece[0].astype(F32) for piece in held)
-
-
-def settle(units, core):
-    rows = units.shape[1] // 2
-    mine = lax.dynamic_slice_in_dim(units, core * rows, rows, 1)
-    theirs = lax.dynamic_slice_in_dim(units, (1 - core) * rows, rows, 1)
-    got = swap(theirs, "dp", 1)
-    low = jnp.where(core == 0, mine, got)
-    high = jnp.where(core == 0, got, mine)
-    both = jnp.concatenate([low, high], 0)
-    return jnp.transpose(both, (1, 0, 2)).reshape(rows, both.shape[0] * 128)
-
-
-def weight_gradients(scal, core, a, b, e, g, counts, name):
-    a_width, e_width = a[0].shape[1], e[0].shape[1]
-    rows = counts[0] * a_width // 16 + counts[1] * e_width // 16
-    shapes = [shaped(8, rows, 128, dtype=BF)] * 6
-    flops = 2 * 512 * (a_width * b[0].shape[1] + e_width * g[0].shape[1])
+class Bucket:
+    def __init__(self, sends, keeps, orders):
+        self.orders = orders
+        self.sent = list(sends)
+        self.held = [[keep, swap(send, *STEP[order[0]])] for keep, send, order in zip(keeps, sends, orders)]
+        self.depth = 1
+        self.size = 8
+
+    def advance(self):
+        half = self.size // 2
+        self.sent = [
+            sum(piece[half : self.size].astype(F32) for piece in held).astype(BF) for held in self.held
+        ]
+        if half == 1:
+            self.sent = [jnp.concatenate(self.sent, 1)]
+            self.last = swap(self.sent[0], *STEP[self.orders[0][-1]])
+        else:
+            for held, out, order in zip(self.held, self.sent, self.orders):
+                held.append(swap(out, *STEP[order[self.depth]]))
+        self.size = half
+        self.depth += 1
+
+
+def weight_bucket(scal, own, far, mine, got, products, orders, after=()):
+    count = len(orders)
+    shapes = []
+    for part in range(count):
+        rows = sum(dealt[part] * (high - low) // 16 for low, high, _, dealt in products)
+        shapes.append(shaped(8, rows, 128, dtype=BF))
     outs = call(
-        functools.partial(weights_kernel, counts),
-        [SM] + [VM] * 8,
-        shapes,
-        [pltpu.VMEM((a_width, counts[0] * 128), BF), pltpu.VMEM((e_width, counts[1] * 128), BF)],
-        (flops, 2 * flops // 512),
-        name,
-    )(scal, *a, *b, *e, *g)
-    first, second = [], []
-    a_rows, e_rows = a_width // 16, e_width // 16
-    for part in range(3):
-        total = scatter_part(outs[3 + part], outs[part], ORDERS[part])
-        cut = counts[0] * a_rows
-        first.append(total[:cut].reshape(counts[0], a_rows, 128))
-        second.append(total[cut:].reshape(counts[1], e_rows, 128))
-    return settle(jnp.concatenate(first, 0), core), settle(jnp.concatenate(second, 0), core)
+        functools.partial(weights_kernel, products, orders),
+        [SM] + [VM] * 4,
+        shapes * 2,
+        [pltpu.VMEM((high - low, max(dealt) * 128), BF) for low, high, _, dealt in products],
+        0.1,
+        "mlp_weights",
+        28,
+        after,
+    )(scal, own, far, mine, got)
+    return Bucket(outs[:count], outs[count:], orders)
+
+
+def settle(bucket, scal, products):
+    count = len(bucket.orders)
+    spans = []
+    for part in range(count):
+        blocks = []
+        for low, high, _, dealt in products:
+            blocks += [(high - low) // 16] * dealt[part]
+        spans.append(blocks)
+    rows = sum(sum(blocks) for blocks in spans) // 2
+    pieces = [piece for held in bucket.held for piece in held] + [bucket.last]
+    number = len(pieces) - 1 + count
+    mine, theirs = call(
+        functools.partial(settle_kernel, (bucket.orders, spans)),
+        [SM] + [ANY] * len(pieces),
+        [shaped(rows, 128)] * 2,
+        [pltpu.VMEM((number, max(sum(blocks) for blocks in spans), 128), BF), pltpu.SemaphoreType.DMA((number,))],
+        0.1,
+        "settle",
+        10,
+    )(scal, *pieces)
+    return mine, swap(theirs, "dp", 1)
+
+
+def plan_of(products, names):
+    plan = []
+    for part in range(len(products[0][3])):
+        for (low, high, _, dealt), (out, layer) in zip(products, names):
+            first = sum(dealt[:part])
+            plan += [(out, layer, first + number, (high - low) // 32) for number in range(dealt[part])]
+    return plan
+
+
+class Triple:
+    def __init__(self, scal, h_rows, stacked, after=()):
+        self.scal = scal
+        shape = (WIDTH // 8 * 3 // 2, 2 * GROUP)
+        keep, theirs = call(
+            triple_kernel,
+            [SM] + [VM] * 5,
+            [shaped(4, *shape, dtype=BF)] * 2,
+            [pltpu.VMEM((8, *shape), BF)],
+            0.1,
+            "triple_weights",
+            20,
+            after,
+        )(scal, *h_rows, stacked)
+        self.sent = [theirs]
+        self.held = [keep, swap(theirs, "dp", 1)]
+        self.steps = [(2, 4, "a"), (1, 2, "b")]
+
+    def advance(self):
+        low, high, name = self.steps.pop(0)
+        self.sent = [sum(piece[low:high].astype(F32) for piece in self.held).astype(BF)]
+        self.held.append(swap(self.sent[0], *STEP[name]))
+
+    def settle(self):
+        blocks = call(
+            triple_settle_kernel,
+            [SM] + [VM] * 4,
+            [shaped(WIDTH // 32, 3 * GROUP)] * 4,
+            [pltpu.VMEM((4, WIDTH // 32, 3 * GROUP), F32)],
+            0.1,
+            "triple_settle",
+            8,
+        )(self.scal, *self.held)
+        return swap_chunks(blocks)
 
 
 def local_fast(
@@ -1014,8 +1184,6 @@
     biases = jnp.concatenate(
         [part.astype(F32) for part in (triple_bias, output_bias, expand_bias, shrink_bias)], 1
     )[:, None, :]
-    conditions = lax.all_gather(condition[0], "dp", axis=0)
-
     f_square = shaped(rows, WIDTH)
     b_square = shaped(rows, WIDTH, dtype=BF)
     b_tall = shaped(rows, hidden, dtype=BF)
@@ -1029,29 +1197,27 @@
     expand_hold = pltpu.VMEM((WIDTH, hidden), BF)
     shrink_hold = pltpu.VMEM((hidden, WIDTH), BF)
 
-    def halved(width):
-        return pltpu.VMEM((2, rows, width // 2), BF)
-
-    def half_pair(width):
-        return [shaped(rows, width // 2, dtype=BF)] * 2
-
-    product = 2 * rows * WIDTH
-    qkv_cost = product * 3 * WIDTH
-    mlp_cost = product * (WIDTH + 2 * hidden)
-
-    x0, mod, h0, *chunks = call(
+    h_both = shaped(2, WIDTH // 2, rows, dtype=BF)
+    half_width = hidden // 2 + WIDTH
+    tall = hidden + 2 * WIDTH
+
+    def far(values):
+        return swap(values, "dp", 1)
+
+    x0, mod, h_rows, c0, c1, c2, c3 = call(
         first_kernel,
-        [SM] + [VM] * 8 + [ANY],
-        [f_square, shaped(LAYERS, 1, 6 * WIDTH), b_square] + [chunk] * 4,
+        [SM] + [VM] * 8 + [HBM],
+        [f_square, shaped(LAYERS, 1, 6 * WIDTH), h_both] + [chunk] * 4,
         [triple_hold, c_hold, pltpu.SemaphoreType.DMA((1,))],
-        (qkv_cost, 12e6),
+        300,
         "qkv_first",
+        24,
     )(
         scal, inputs, mask_embed[None], condition, adaptive_weight, adaptive_bias[:, None, :], biases, cosine, sine,
         triple_weight,
     )
 
-    def attend(chunks):
+    def attend(chunks, after):
         return call(
             attend_kernel,
             [VM] * 4,
@@ -1061,15 +1227,17 @@
                 pltpu.VMEM((4 * rows, GROUP), BF),
                 pltpu.VMEM((GROUP, 4 * rows), BF),
             ],
-            (6e9, 6e6),
+            300,
             "attend",
+            20,
+            after,
         )(*chunks)
 
-    def attend_back(chunks, given, lse, turned):
+    def attend_back(chunks, given, lse, turned, after):
         return call(
             attend_back_kernel,
             [VM] * 12,
-            [chunk] * 4,
+            [chunk] * 4 + [shaped(4, packed, 2 * GROUP, dtype=BF)],
             [
                 pltpu.VMEM((3, 4 * rows, GROUP), BF),
                 pltpu.VMEM((3, 4 * rows, GROUP), BF),
@@ -1082,87 +1250,131 @@
                 pltpu.VMEM((4, rows, GROUP), F32),
                 pltpu.VMEM((4, rows, GROUP), F32),
             ],
-            (15e9, 10e6),
+            300,
             "attend_back",
+            24,
+            after,
         )(*chunks, *given, lse, turned, cosine, sine)
-
-    chunks0 = swap_chunks(chunks)
-    *o_chunks, lse0, turned0 = attend(chunks0)
-    o_chunks = swap_chunks(o_chunks)
-    o0, aout0, m0, h20, z0, slope0, f0, x1, h1, *chunks = call(
-        middle_kernel,
-        [SM] + [VM] * 9 + [ANY] * 4,
-        [b_square, b_square, f_square, b_square, b_tall, b_tall, b_square, f_square, b_square] + [chunk] * 4,
-        [output_hold, expand_hold, shrink_hold, triple_hold, o_hold, c_hold, pltpu.SemaphoreType.DMA((4,))],
-        (qkv_cost + mlp_cost, 25e6),
-        "mlp_qkv",
-    )(scal, x0, mod, biases, cosine, sine, *o_chunks, output_weight, expand_weight, shrink_weight, triple_weight)
-    chunks1 = swap_chunks(chunks)
-    *o_chunks, lse1, turned1 = attend(chunks1)
-    o_chunks = swap_chunks(o_chunks)
-    back_outs = half_pair(WIDTH) + half_pair(hidden) + half_pair(WIDTH) + [o_chunk] * 4 + [f_square, shaped(1, 7680)]
-    back_holds = [halved(WIDTH), halved(hidden), halved(WIDTH)]
-    outputs, o1, h21, z1, dfm1, dft1, dum1, dut1, dam1, dat1, *given, dm1, vec1 = call(
-        peak_kernel,
-        [SM] + [VM] * 8 + [ANY] * 3,
-        [shaped(1, rows, WIDTH, dtype=BF), b_square, b_square, b_tall] + back_outs,
-        [output_hold, expand_hold, shrink_hold, o_hold]
-        + [
-            pltpu.VMEM((rows, WIDTH), F32),
-            pltpu.VMEM((rows, WIDTH), BF),
-            pltpu.VMEM((rows, hidden), BF),
-            pltpu.VMEM((rows, WIDTH), BF),
-        ]
-        + back_holds
-        + [pltpu.SemaphoreType.DMA((3,))],
-        (2 * mlp_cost, 25e6),
-        "mlp_turn",
-    )(scal, x1, mod, biases, cotangent, *o_chunks, output_weight, expand_weight, shrink_weight)
 
     def far(values):
         return swap(values, "dp", 1)
 
+    def gather_rows(both):
+        near = swap(both, "blk", 1)
+        return [both, near, swap(both, "blk", 2), swap(near, "blk", 2)]
+
+    chunks0 = swap_chunks([c0, c1, c2, c3])
+    h_rows0 = gather_rows(h_rows)
+    *o_chunks, lse0, ot0 = attend(chunks0, ())
+    o_chunks = swap_chunks(o_chunks)
+    aout0, m0, turned0, slope0, f0, x1, h_rows, c0, c1, c2, c3 = call(
+        middle_kernel,
+        [SM] + [VM] * 9 + [HBM] * 4,
+        [b_square, f_square, shaped(tall, rows, dtype=BF), b_tall, b_square, f_square, h_both] + [chunk] * 4,
+        [output_hold, expand_hold, shrink_hold, triple_hold, o_hold, pltpu.VMEM((rows, WIDTH), BF), c_hold]
+        + [pltpu.SemaphoreType.DMA((4,))],
+        300,
+        "mlp_qkv",
+        36,
+        h_rows0[1:3],
+    )(scal, x0, mod, biases, cosine, sine, *o_chunks, output_weight, expand_weight, shrink_weight, triple_weight)
+    turned0_far = far(turned0)
+    chunks1 = swap_chunks([c0, c1, c2, c3])
+    h_rows1 = gather_rows(h_rows)
+    *o_chunks, lse1, ot1 = attend(chunks1, h_rows0[3:])
+    o_chunks = swap_chunks(o_chunks)
+    outputs, aout1, m1, turned1, slope1, f1 = call(
+        ahead_kernel,
+        [SM] + [VM] * 7 + [HBM] * 3,
+        [shaped(1, rows, WIDTH, dtype=BF), b_square, f_square, shaped(tall, rows, dtype=BF), b_tall, b_square],
+        [output_hold, expand_hold, shrink_hold, o_hold, pltpu.VMEM((rows, WIDTH), BF), pltpu.SemaphoreType.DMA((3,))],
+        300,
+        "mlp_ahead",
+        32,
+        [*h_rows1[1:3], turned0_far],
+    )(scal, x1, mod, biases, *o_chunks, output_weight, expand_weight, shrink_weight)
+    turned1_far = far(turned1)
+    back_outs = [o_chunk] * 4 + [f_square, shaped(1, 7680)]
+    mine1, theirs1, *given, dm1, vec1 = call(
+        turn_kernel,
+        [SM] + [VM] * 6 + [HBM] * 3,
+        [shaped(rows, half_width, dtype=BF)] * 2 + back_outs,
+        [output_hold, expand_hold, shrink_hold, o_hold, pltpu.VMEM((2, rows, half_width), BF)]
+        + [pltpu.SemaphoreType.DMA((3,))],
+        300,
+        "mlp_turn",
+        32,
+        h_rows1[3:],
+    )(scal, cotangent, mod, m1, f1, slope1, aout1, output_weight, expand_weight, shrink_weight)
     given = swap_chunks(given)
-    h2_far1, z_far1, h_far1, o_far1 = far(h21), far(z1), far(h1), far(o1)
-    h2_far0, z_far0, h_far0, o_far0 = far(h20), far(z0), far(h0), far(o0)
-    expand1, shrink1 = weight_gradients(
-        scal, core, (h21, h2_far1), (dum1, far(dut1)), (z1, z_far1), (dfm1, far(dft1)), (4, 1), "mlp_weights"
-    )
-    grads = attend_back(chunks1, given, lse1, turned1)
+    products = (
+        (hidden, hidden + WIDTH, 0, (7, 5)),
+        (0, hidden, hidden // 2, (1, 2)),
+        (hidden + WIDTH, tall, hidden // 2 + WIDTH // 2, (2, 1)),
+    )
+    bucket1 = weight_bucket(scal, turned1, turned1_far, mine1, far(theirs1), products, ("axyb", "yaxb"))
+    *grads, stacked = attend_back(chunks1, given, lse1, ot1, bucket1.sent[:1])
     grads = swap_chunks(grads)
-    dqm1, dqt1, first1, dfm0, dft0, dum0, dut0, dam0, dat0, *given, dm0, vec0 = call(
+    triple1 = Triple(scal, h_rows1, stacked)
+    bucket1.advance()
+    mine0, theirs0, first1, *given, dm0, vec0 = call(
         back_kernel,
-        [SM] + [VM] * 11 + [ANY] * 4,
-        half_pair(3 * WIDTH) + [shaped(1, 3840)] + back_outs,
-        [triple_hold, output_hold, expand_hold, shrink_hold, c_hold, halved(3 * WIDTH)]
-        + [pltpu.VMEM((rows, 3 * WIDTH), BF), o_hold]
-        + back_holds
-        + [pltpu.SemaphoreType.DMA((4,))],
-        (qkv_cost + mlp_cost, 25e6),
+        [SM] + [VM] * 11 + [HBM] * 4,
+        [shaped(rows, half_width, dtype=BF)] * 2 + [shaped(1, 3840)] + back_outs,
+        [triple_hold, output_hold, expand_hold, shrink_hold, c_hold, pltpu.VMEM((rows, 3 * WIDTH), BF), o_hold]
+        + [pltpu.VMEM((2, rows, half_width), BF), pltpu.SemaphoreType.DMA((4,))],
+        300,
         "qkv_mlp_back",
+        36,
+        bucket1.sent + triple1.sent,
     )(
         scal, x1, dm1, mod, *grads, m0, f0, slope0, aout0, triple_weight, output_weight, expand_weight, shrink_weight
     )
     given = swap_chunks(given)
-    triple1, output1 = weight_gradients(
-        scal, core, (h1, h_far1), (dqm1, far(dqt1)), (o1, o_far1), (dam1, far(dat1)), (3, 1), "attention_weights"
-    )
-    expand0, shrink0 = weight_gradients(
-        scal, core, (h20, h2_far0), (dum0, far(dut0)), (z0, z_far0), (dfm0, far(dft0)), (4, 1), "mlp_weights"
-    )
-    grads = attend_back(chunks0, given, lse0, turned0)
+    bucket1.advance()
+    bucket0 = weight_bucket(
+        scal, turned0, turned0_far, mine0, far(theirs0), products, ("ayxb", "xayb")
+    )
+    *grads, stacked = attend_back(chunks0, given, lse0, ot0, bucket0.sent[:1] + bucket1.sent)
     grads = swap_chunks(grads)
-    dqm0, dqt0, first0, input_grad, mask_term = call(
+    triple0 = Triple(scal, h_rows0, stacked)
+    triple1.advance()
+    bucket0.advance()
+    bucket1.advance()
+    first0, input_grad, mask_term = call(
         last_kernel,
-        [SM] + [VM] * 7 + [ANY],
-        half_pair(3 * WIDTH) + [shaped(1, 3840), shaped(1, rows, WIDTH), shaped(1, WIDTH)],
-        [triple_hold, c_hold, halved(3 * WIDTH), pltpu.VMEM((rows, 3 * WIDTH), BF), pltpu.SemaphoreType.DMA((1,))],
-        (qkv_cost, 10e6),
+        [SM] + [VM] * 7 + [HBM],
+        [shaped(1, 3840), shaped(1, rows, WIDTH), shaped(1, WIDTH)],
+        [triple_hold, c_hold, pltpu.VMEM((rows, 3 * WIDTH), BF), pltpu.SemaphoreType.DMA((1,))],
+        300,
         "qkv_back",
+        24,
+        [*triple0.sent, *triple1.sent, *bucket0.sent, *bucket1.sent],
     )(scal, x0, dm0, mod, *grads, triple_weight)
-    triple0, output0 = weight_gradients(
-        scal, core, (h0, h_far0), (dqm0, far(dqt0)), (o0, o_far0), (dam0, far(dat0)), (3, 1), "attention_weights"
-    )
+    triple0.advance()
+    triple0.advance()
+    bucket0.advance()
+    bucket0.advance()
+    triple1.advance()
+    parts = [*settle(bucket1, scal, products), *settle(bucket0, scal, products)]
+    plans = (
+        plan_of(products, ((2, 1), (3, 1), (1, 1))),
+        plan_of(products, ((2, 0), (3, 0), (1, 0))),
+    )
+    weight_grads = call(
+        functools.partial(finish_kernel, plans),
+        [SM] + [VM] * 12,
+        [
+            shaped(LAYERS, WIDTH // 32, 3 * WIDTH),
+            shaped(LAYERS, WIDTH // 32, WIDTH),
+            shaped(LAYERS, WIDTH // 32, hidden),
+            shaped(LAYERS, hidden // 32, WIDTH),
+        ],
+        [pltpu.VMEM((4, WIDTH // 32, 3 * GROUP), F32)],
+        0.1,
+        "finish",
+        12,
+    )(scal, *parts, *triple0.settle(), *triple1.settle())
 
     small = jnp.concatenate([first0, vec0, first1, vec1, mask_term], 1)
     small = small + swap(small, "blk", 1)
@@ -1174,6 +1386,7 @@
         dmods += [first[:, 0:1536], vec[:, 2304:3072], vec[:, 768:2304], vec[:, 0:768]]
         sums += [first[:, 1536:3840], vec[:, 6912:7680], vec[:, 3840:6912], vec[:, 3072:3840]]
     dmod = jnp.concatenate(dmods, 1)
+    gathered = jnp.concatenate([dmod, condition], 1)
     total = jnp.concatenate(sums + [small[:, 2 * 11520 :]], 1)
     condition_grad = sum(
         lax.dot_general(
@@ -1184,14 +1397,13 @@
         )
         for layer in range(LAYERS)
     )
-    gathered = dmod
     for bit in (1, 2, 4):
         gathered = jnp.concatenate([gathered, swap(gathered, "dp", bit)], 0)
         total = total + swap(total, "dp", bit)
     index = blk * 8 + dp
     share_rows = condition.shape[1] // 32
-    near = conditions[dp ^ jnp.arange(8, dtype=jnp.int32)]
-    near = lax.dynamic_slice_in_dim(near, index * share_rows, share_rows, 1)
+    near = lax.dynamic_slice_in_dim(gathered[:, 12 * WIDTH :], index * share_rows, share_rows, 1)
+    gathered = gathered[:, : 12 * WIDTH]
     adaptive_w = jnp.sum(near[:, :, None] * gathered[:, None, :], 0)
     adaptive_w = jnp.stack([adaptive_w[:, : 6 * WIDTH], adaptive_w[:, 6 * WIDTH :]], 0)
     adaptive_all = jnp.sum(gathered, 0)
@@ -1213,13 +1425,13 @@
         mask_sum,
         adaptive_w,
         adaptive_b,
-        jnp.stack([triple0, triple1], 0),
+        weight_grads[0],
         bias_grads[0],
-        jnp.stack([output0, output1], 0),
+        weight_grads[1],
         bias_grads[1],
-        jnp.stack([expand0, expand1], 0),
+        weight_grads[2],
         bias_grads[2],
-        jnp.stack([shrink0, shrink1], 0),
+        weight_grads[3],
         bias_grads[3],
     )
 

time: 504 us -> 362 us (0.72)
  waiting for transfers between devices: 189 us -> 103 us
  starting transfers between devices: 98 us -> 75 us
  Pallas kernels: 132 us -> 119 us
  blocking collectives: 12.4 us -> 0 us
  other arithmetic: 45.2 us -> 36.5 us
    ppermute x104 -> x70, waiting for transfers between devices: 189 us -> 103 us  [swap(): return lax.ppermute(values, axis, [(i, i ^ bit) for i in range(size)])]
    ppermute x104 -> x70, starting transfers between devices: 98 us -> 75 us  [swap(): return lax.ppermute(values, axis, [(i, i ^ bit) for i in range(size)])]
    pallas_call x13 -> x19, Pallas kernels: 132 us -> 119 us  [call(): return lambda *operands: made(*operands, *after)]
    all_gather x1 -> x0, blocking collectives: 12.4 us -> none  [local_fast(): conditions = lax.all_gather(condition[0], 'dp', axis=0)]
    add x12 -> x0, other arithmetic: 6.27 us -> none  [scatter_part(): return sum((piece[0].astype(F32) for piece in held))]
    unnamed x150 -> x171, local copies, waits for them, and re-layouts: 7 us -> 12.3 us
    convert_element_type x36 -> x16, other arithmetic: 23.5 us -> 24.6 us  [the longest x12 19.5 us: advance(): sum((piece[half:self.size].astype(F32) for piece in held)).astype(BF)]
  transfers between devices with their start and end apart: 104 -> 70, of which waited for: 58 -> 25; matrix products, arithmetic and copies ran while one was open for 9% -> 11% of each run, Pallas kernels for 5% -> 32%
where the time goes in v2:
time: 362 us; the launch traced here: 355 us
  Pallas kernels  119 us (33%)
  waiting for transfers between devices  103 us (28%)
  starting transfers between devices  75 us (21%)
  other arithmetic  36.5 us (10%)
  local copies, waits for them, and re-layouts  15.3 us (4%)
    pallas_call x19, Pallas kernels, call(): return lambda *operands: made(*operands, *after)  119 us
    ppermute x70, waiting for transfers between devices, swap(): return lax.ppermute(values, axis, [(i, i ^ bit) for i in range(size)])  103 us
    ppermute x70, starting transfers between devices, swap(): return lax.ppermute(values, axis, [(i, i ^ bit) for i in range(size)])  75 us
    convert_element_type x12, other arithmetic, advance(): sum((piece[half:self.size].astype(F32) for piece in held)).astype(BF)  19.5 us
    unnamed x171, local copies, waits for them, and re-layouts  12.3 us
  transfers between devices with their start and end apart: 70, of which 25 were waited for; matrix products, arithmetic and copies ran while one was open for 11% of the time, Pallas kernels for 32%

profile of v2, /device:TPU:0, one launch (start us, length us, event | category | flops | bytes accessed | tf_op | source)
XLA Modules:
  0.0 354.9 jit_solution(15081841016209669051)
XLA Ops:
  5.8 3.3 copy-done.36
  10.7 4.1 %qkv_first.1 = (f32[256,768]{1,0:T(8,128)S(1)}, f32[2,1,4608]{2,1,0:T(1,128)S(1)}, bf16[2,384,256]{2,1,0:T(8,128)(2,1)}, bf16[384,384]{1,0:T(8,128)(2,1)S(1)}, b...) custom-call(s32[4]{0:T(128)S(1)} %pad_add_fusion.refs_0_, ...), custom_call_target="tpu_custom_call" | custom-call | flops 299999985664 | bytes 300000000 | tf_op jit(solution)/shard_map/qkv_first/pallas_call | solution.py:1046
  14.9 3.0 collective-permute-start
  22.9 2.8 collective-permute-done.refs_1_
  25.8 8.4 %collective-permute-done.1.refs_2_ = bf16[384,384]{1,0:T(8,128)(2,1)S(1)} collective-permute-done((bf16[384,384]{1,0:T(8,128)(2,1)S(1)}, bf16[384,384]{1,0:T(8,128)(2,1)S(1)}, u32[]{:S(2)}, u32[]{:S(2)}) %collective-permute-start.1) | collective-permute-done | bytes 294944 | tf_op jit(solution)/shard_map/ppermute | solution.py:1051
  34.2 8.4 %attend.2 = (bf16[128,384]{1,0:T(8,128)(2,1)S(1)}, bf16[128,384]{1,0:T(8,128)(2,1)S(1)}, bf16[128,384]{1,0:T(8,128)(2,1)S(1)}, bf16[128,384]{1,0:T(8,128)(2,1)S(...) custom-call(bf16[384,384]{1,0:T(8,128)(2,1)S(1)} %get-tuple-element.110.refs_0_, ...), custom_call_target="tpu_custom_call" | custom-call | flops 299999985664 | bytes 300000000 | tf_op jit(solution)/shard_map/attend/pallas_call | solution.py:1046
  47.8 2.7 collective-permute-done.4.refs_8_
  50.6 11.7 %mlp_qkv.1 = (bf16[256,768]{1,0:T(8,128)(2,1)S(1)}, f32[256,768]{1,0:T(8,128)S(1)}, bf16[4608,256]{1,0:T(8,128)(2,1)}, bf16[256,3072]{1,0:T(8,128)(2,1)S(1)}, bf...) custom-call(s32[4]{0:T(128)S(1)} %copy-done.31, ...), custom_call_target="tpu_custom_call" | custom-call | flops 299999985664 | bytes 300000000 | tf_op jit(solution)/shard_map/mlp_qkv/pallas_call | solution.py:1046
  67.3 5.0 %collective-permute-done.8.refs_1_ = bf16[384,384]{1,0:T(8,128)(2,1)S(1)} collective-permute-done((bf16[384,384]{1,0:T(8,128)(2,1)S(1)}, bf16[384,384]{1,0:T(8,128)(2,1)S(1)}, u32[]{:S(2)}, u32[]{:S(2)}) %collective-permute-start.8) | collective-permute-done | bytes 294944 | tf_op jit(solution)/shard_map/ppermute | solution.py:1051
  73.4 2.6 collective-permute-done.9.refs_2_
  76.0 2.3 collective-permute-done.10.refs_3_
  78.3 8.4 %attend.3 = (bf16[128,384]{1,0:T(8,128)(2,1)S(1)}, bf16[128,384]{1,0:T(8,128)(2,1)S(1)}, bf16[128,384]{1,0:T(8,128)(2,1)S(1)}, bf16[128,384]{1,0:T(8,128)(2,1)S(...) custom-call(bf16[384,384]{1,0:T(8,128)(2,1)S(1)} %get-tuple-element.120.refs_0_, ...), custom_call_target="tpu_custom_call" | custom-call | flops 299999985664 | bytes 300000000 | tf_op jit(solution)/shard_map/attend/pallas_call | solution.py:1046
  87.9 2.4 collective-permute-start.14
  91.5 2.5 collective-permute-done.13.refs_6_
  94.1 8.3 %mlp_ahead.1 = (bf16[1,256,768]{2,1,0:T(8,128)(2,1)}, bf16[256,768]{1,0:T(8,128)(2,1)S(1)}, f32[256,768]{1,0:T(8,128)S(1)}, bf16[4608,256]{1,0:T(8,128)(2,1)}, b...) custom-call(s32[4]{0:T(128)S(1)} %copy-done.32, f32[256,768]{1,0:T(8,128)S(1)} %get-tuple-element.119.refs_1_, ...), custom_call_target="tpu_custom_call" | custom-call | flops 299999985664 | bytes 300000000 | tf_op jit(solution)/shard_map/mlp_ahead/pallas_call | solution.py:1046
  102.5 3.7 %copy-done.35 = bf16[2,768,3072]{2,1,0:T(8,128)(2,1)S(1)} copy-done((bf16[2,768,3072]{2,1,0:T(8,128)(2,1)S(1)}, bf16[2,768,3072]{2,1,0:T(8,128)(2,1)}, u32[]{:S(2)}) %copy-start.35) | copy-done | bytes 9437208
  106.2 7.4 %mlp_turn.1 = (bf16[256,2304]{1,0:T(8,128)(2,1)S(1)}, bf16[256,2304]{1,0:T(8,128)(2,1)S(1)}, bf16[128,384]{1,0:T(8,128)(2,1)S(1)}, bf16[128,384]{1,0:T(8,128)(2,...) custom-call(s32[4]{0:T(128)S(1)} %copy-done.32, ...), custom_call_target="tpu_custom_call" | custom-call | flops 299999985664 | bytes 300000000 | tf_op jit(solution)/shard_map/mlp_turn/pallas_call | solution.py:1046
  117.7 8.1 %mlp_weights.2 = (bf16[8,624,128]{2,1,0:T(8,128)(2,1)}, bf16[8,672,128]{2,1,0:T(8,128)(2,1)}, bf16[8,624,128]{2,1,0:T(8,128)(2,1)S(1)}, bf16[8,672,128]{2,1,0:T(8,128)(2,1)S(1)}) custom-call(s32[4]{0:T(128)S(1)} %copy-done.32, bf16[4608,256]{1,0:T(8,128)(2,1)} %get-tuple-element.142.refs_1_, bf16[4608,256]{1,0:T(8,128)(2,1)} %collective-permute-done.22.refs_2_, ...), custom_call_target="tpu_custom_call" | custom-call | flops 100000000 | bytes 100000 | tf_op jit(solution)/shard_map/mlp_weights/pallas_call | solution.py:1046
  128.5 12.0 %attend_back.2 = (bf16[384,384]{1,0:T(8,128)(2,1)S(1)}, bf16[384,384]{1,0:T(8,128)(2,1)S(1)}, bf16[384,384]{1,0:T(8,128)(2,1)S(1)}, bf16[384,384]{1,0:T(8,128)(2,1)S(1)}, bf16[4,384,384]{2,1,0:T(8,128)(2,1)S(1)}) custom-call(bf16[384,384]{1,0:T(8,128)(2,1)S(1)} %copy-done.67, bf16[384,384]{1,0:T(8,128)(2,1)S(1)} %collective-permute-done.8.refs_1_, ...), custom_call_target="tpu_custom_call" | custom-call | flops 299999985664 | bytes 300000000 | tf_op jit(solution)/shard_map/attend_back/pallas_call | solution.py:1046
  144.1 3.7 %triple_weights.2 = (bf16[4,144,384]{2,1,0:T(8,128)(2,1)S(1)}, bf16[4,144,384]{2,1,0:T(8,128)(2,1)}) custom-call(s32[4]{0:T(128)S(1)} %copy-done.32, bf16[2,384,256]{2,1,0:T(8,128)(2,1)} %get-tuple-element.128.refs_1_, bf16[2,384,256]{2,1,0:T(8,128)(2,1)} %collective-permute-done.15.refs_11_.refs_2_, ...), custom_call_target="tpu_custom_call" | custom-call | flops 100000000 | bytes 100000 | tf_op jit(solution)/shard_map/triple_weights/pallas_call | solution.py:1046
  147.7 7.7 %collective-permute-done.27.refs_2_ = bf16[8,624,128]{2,1,0:T(8,128)(2,1)} collective-permute-done((bf16[8,624,128]{2,1,0:T(8,128)(2,1)}, bf16[8,624,128]{2,1,0:T(8,128)(2,1)}, u32[]{:S(2)}, u32[]{:S(2)}) %collective-permute-start.27) | collective-permute-done | bytes 1277984 | tf_op jit(solution)/shard_map/ppermute | solution.py:1051
  155.5 2.1 add_convert_fusion.3.refs_16_
  157.6 9.6 %collective-permute-done.28.refs_6_ = bf16[8,672,128]{2,1,0:T(8,128)(2,1)} collective-permute-done((bf16[8,672,128]{2,1,0:T(8,128)(2,1)}, bf16[8,672,128]{2,1,0:T(8,128)(2,1)}, u32[]{:S(2)}, u32[]{:S(2)}) %collective-permute-start.28) | collective-permute-done | bytes 1376288 | tf_op jit(solution)/shard_map/ppermute | solution.py:1051
  168.8 2.1 add_convert_fusion.1.refs_17_
  171.4 9.3 %qkv_mlp_back.1 = (bf16[256,2304]{1,0:T(8,128)(2,1)S(1)}, bf16[256,2304]{1,0:T(8,128)(2,1)S(1)}, f32[1,3840]{1,0:T(1,128)S(1)}, bf16[128,384]{1,0:T(8,128)(2,1)S...) custom-call(s32[4]{0:T(128)S(1)} %copy-done.32, ...), custom_call_target="tpu_custom_call" | custom-call | flops 299999985664 | bytes 300000000 | tf_op jit(solution)/shard_map/qkv_mlp_back/pallas_call | solution.py:1046
  185.8 3.9 %collective-permute-done.65.refs_3_ = bf16[2,144,384]{2,1,0:T(8,128)(2,1)S(1)} collective-permute-done((bf16[2,144,384]{2,1,0:T(8,128)(2,1)S(1)}, bf16[2,144,384]{2,1,0:T(8,128)(2,1)S(1)}, u32[]{:S(2)}, u32[]{:S(2)}) %collective-permute-start.65) | collective-permute-done | bytes 221216 | tf_op jit(solution)/shard_map/ppermute | solution.py:1051
  191.4 2.6 collective-permute-start.66
  203.0 8.2 %mlp_weights.3 = (bf16[8,624,128]{2,1,0:T(8,128)(2,1)}, bf16[8,672,128]{2,1,0:T(8,128)(2,1)}, bf16[8,624,128]{2,1,0:T(8,128)(2,1)S(1)}, bf16[8,672,128]{2,1,0:T(8,128)(2,1)S(1)}) custom-call(s32[4]{0:T(128)S(1)} %copy-done.32, bf16[4608,256]{1,0:T(8,128)(2,1)} %get-tuple-element.129.refs_1_, bf16[4608,256]{1,0:T(8,128)(2,1)} %collective-permute-done.17.refs_13_.refs_2_, ...), custom_call_target="tpu_custom_call" | custom-call | flops 100000000 | bytes 100000 | tf_op jit(solution)/shard_map/mlp_weights/pallas_call | solution.py:1046
  213.3 12.0 %attend_back.3 = (bf16[384,384]{1,0:T(8,128)(2,1)S(1)}, bf16[384,384]{1,0:T(8,128)(2,1)S(1)}, bf16[384,384]{1,0:T(8,128)(2,1)S(1)}, bf16[384,384]{1,0:T(8,128)(2,1)S(1)}, bf16[4,384,384]{2,1,0:T(8,128)(2,1)S(1)}) custom-call(bf16[384,384]{1,0:T(8,128)(2,1)S(1)} %copy-done.69, bf16[384,384]{1,0:T(8,128)(2,1)S(1)} %copy-done.47, ...), custom_call_target="tpu_custom_call" | custom-call | flops 299999985664 | bytes 300000000 | tf_op jit(solution)/shard_map/attend_back/pallas_call | solution.py:1046
  225.4 3.1 triple_weights.3
  233.8 6.1 %collective-permute-done.39.refs_2_ = bf16[8,624,128]{2,1,0:T(8,128)(2,1)} collective-permute-done((bf16[8,624,128]{2,1,0:T(8,128)(2,1)}, bf16[8,624,128]{2,1,0:T(8,128)(2,1)}, u32[]{:S(2)}, u32[]{:S(2)}) %collective-permute-start.39) | collective-permute-done | bytes 1277984 | tf_op jit(solution)/shard_map/ppermute | solution.py:1051
  240.8 2.1 add_convert_fusion.2.refs_11_
  242.9 2.3 collective-permute-done.40.refs_6_
  245.5 2.2 add_convert_fusion.refs_12_
  247.7 3.7 %collective-permute-done.35.refs_5_ = bf16[384,384]{1,0:T(8,128)(2,1)S(1)} collective-permute-done((bf16[384,384]{1,0:T(8,128)(2,1)S(1)}, bf16[384,384]{1,0:T(8,128)(2,1)S(1)}, u32[]{:S(2)}, u32[]{:S(2)}) %collective-permute-start.35) | collective-permute-done | bytes 294944 | tf_op jit(solution)/shard_map/ppermute | solution.py:1051
  253.0 2.1 collective-permute-done.37.refs_7_
  255.2 3.9 %qkv_back.1 = (f32[1,3840]{1,0:T(1,128)S(1)}, f32[1,256,768]{2,1,0:T(8,128)}, f32[1,768]{1,0:T(1,128)S(1)}) custom-call(s32[4]{0:T(128)S(1)} %copy-done.32, f32[256,768]{1,0:T(8,128)S(1)} %copy-done.65, f32[256,768]{1,0:T(8,128)S(1)} %get-tuple-element.159.refs_2_, f32[2,1,4608]{2,1,0:T(1,128)S(1)} %copy-done.72, ...), custom_call_target="tpu_custom_call" | custom-call | flops 299999985664 | bytes 300000000 | tf_op jit(solution)/shard_map/qkv_back/pallas_call | solution.py:1046
  272.3 2.9 settle.2
  284.6 2.2 collective-permute-done.46
  289.1 3.8 %collective-permute-done.47 = f32[1,14592]{1,0:T(1,128)S(1)} collective-permute-done((f32[1,14592]{1,0:T(1,128)S(1)}, f32[1,14592]{1,0:T(1,128)S(1)}, u32[]{:S(2)}, u32[]{:S(2)}) %collective-permute-start.47) | collective-permute-done | bytes 58400 | tf_op jit(solution)/shard_map/ppermute | solution.py:1051
  297.7 3.0 collective-permute-done.50
  306.0 9.2 %collective-permute-done.55.refs_7_ = bf16[4,672,128]{2,1,0:T(8,128)(2,1)S(1)} collective-permute-done((bf16[4,672,128]{2,1,0:T(8,128)(2,1)}, bf16[4,672,128]{2,1,0:T(8,128)(2,1)S(1)}, u32[]{:S(2)}, u32[]{:S(2)}) %collective-permute-start.55) | collective-permute-done | bytes 688160 | tf_op jit(solution)/shard_map/ppermute | solution.py:1051
  318.7 5.0 %collective-permute-done.56.refs_8_ = bf16[2,672,128]{2,1,0:T(8,128)(2,1)S(1)} collective-permute-done((bf16[2,672,128]{2,1,0:T(8,128)(2,1)S(1)}, bf16[2,672,128]{2,1,0:T(8,128)(2,1)S(1)}, u32[]{:S(2)}, u32[]{:S(2)}) %collective-permute-start.56) | collective-permute-done | bytes 344096 | tf_op jit(solution)/shard_map/ppermute | solution.py:1051
  325.5 11.6 %collective-permute-done.57.refs_9_ = bf16[1,1296,128]{2,1,0:T(8,128)(2,1)S(1)} collective-permute-done((bf16[1,1296,128]{2,1,0:T(8,128)(2,1)S(1)}, bf16[1,1296,128]{2,1,0:T(8,128)(2,1)S(1)}, u32[]{:S(2)}, u32[]{:S(2)}) %collective-permute-start.57) | collective-permute-done | bytes 331808 | tf_op jit(solution)/shard_map/ppermute | solution.py:1051
  337.1 2.6 settle.3
  340.0 5.4 %collective-permute-start.62 = (f32[24,576]{1,0:T(8,128)S(1)}, f32[24,576]{1,0:T(8,128)S(1)}, u32[]{:S(2)}, u32[]{:S(2)}) collective-permute-start(f32[24,576]{1,0:T(8,128)S(1)} %copy-done.61), channel_id=1, source_target_pairs={{0,8},{8,0},{16,24},{24,16},{1,9},{9,1},{17,25},{25,17},{2,10},{10... | collective-permute-start | bytes 165896 | tf_op jit(solution)/shard_map/ppermute | solution.py:1051
  349.6 2.7 collective-permute-done.64.refs_8_
  352.3 2.2 finish.1
  (347 shorter events, 107.1 us)
Async XLA Ops:
  14.9 10.8 %collective-permute-start = (bf16[384,384]{1,0:T(8,128)(2,1)S(1)}, bf16[384,384]{1,0:T(8,128)(2,1)S(1)}, u32[]{:S(2)}, u32[]{:S(2)}) collective-permute-start(bf16[384,384]{1,0:T(8,128)(2,1)S(1)} %get-tuple-element.111), channel_id=1, source_target_pairs={{0,8},{8,0},{16,24},{24,16},{1,9},{9,1},{17,25},{25,17},{2,10},{10... | collective-permute-start | bytes 884744 | tf_op jit(solution)/shard_map/ppermute | solution.py:1051
  17.9 16.3 %collective-permute-start.1 = (bf16[384,384]{1,0:T(8,128)(2,1)S(1)}, bf16[384,384]{1,0:T(8,128)(2,1)S(1)}, u32[]{:S(2)}, u32[]{:S(2)}) collective-permute-start(bf16[384,384]{1,0:T(8,128)(2,1)S(1)} %get-tuple-element.112), channel_id=1, source_target_pairs={{0,16},{8,24},{16,0},{24,8},{1,17},{9,25},{17,1},{25,9},{2,18},{10... | collective-permute-start | bytes 884744 | tf_op jit(solution)/shard_map/ppermute | solution.py:1051
  19.5 14.7 %collective-permute-start.2 = (bf16[384,384]{1,0:T(8,128)(2,1)S(1)}, bf16[384,384]{1,0:T(8,128)(2,1)S(1)}, u32[]{:S(2)}, u32[]{:S(2)}) collective-permute-start(bf16[384,384]{1,0:T(8,128)(2,1)S(1)} %get-tuple-element.113), channel_id=1, source_target_pairs={{0,24},{8,16},{16,8},{24,0},{1,25},{9,17},{17,9},{25,1},{2,26},{10... | collective-permute-start | bytes 884744 | tf_op jit(solution)/shard_map/ppermute | solution.py:1051
  19.5 26.8 %collective-permute-start.6 = (bf16[2,384,256]{2,1,0:T(8,128)(2,1)}, bf16[2,384,256]{2,1,0:T(8,128)(2,1)}, u32[]{:S(2)}, u32[]{:S(2)}) collective-permute-start(bf16[2,384,256]{2,1,0:T(8,128)(2,1)} %get-tuple-element.118.refs_1_), channel_id=1, source_target_pairs={{0,8},{8,0},{16,24},{24,16},{1,9},{9,1},{17,25},{25,17},{2,10},{10... | collective-permute-start | bytes 1179656 | tf_op jit(solution)/shard_map/ppermute | solution.py:1051
  21.4 29.1 %collective-permute-start.7 = (bf16[2,384,256]{2,1,0:T(8,128)(2,1)}, bf16[2,384,256]{2,1,0:T(8,128)(2,1)}, u32[]{:S(2)}, u32[]{:S(2)}) collective-permute-start(bf16[2,384,256]{2,1,0:T(8,128)(2,1)} %get-tuple-element.118.refs_1_), channel_id=1, source_target_pairs={{0,16},{8,24},{16,0},{24,8},{1,17},{9,25},{17,1},{25,9},{2,18},{10... | collective-permute-start | bytes 1179656 | tf_op jit(solution)/shard_map/ppermute | solution.py:1051
  46.3 32.0 %collective-permute-start.11 = (bf16[2,384,256]{2,1,0:T(8,128)(2,1)}, bf16[2,384,256]{2,1,0:T(8,128)(2,1)}, u32[]{:S(2)}, u32[]{:S(2)}) collective-permute-start(bf16[2,384,256]{2,1,0:T(8,128)(2,1)} %collective-permute-done.6.refs_14_.refs_2_), channel_id=1, source_target_pairs={{0,16},{8,24},{16,0},{24,8},{1,17},{9,25},{17,1},{25,9},{2,18},{10... | collective-permute-start | bytes 1179656 | tf_op jit(solution)/shard_map/ppermute | solution.py:1051
  63.8 12.2 %collective-permute-start.9 = (bf16[384,384]{1,0:T(8,128)(2,1)S(1)}, bf16[384,384]{1,0:T(8,128)(2,1)S(1)}, u32[]{:S(2)}, u32[]{:S(2)}) collective-permute-start(bf16[384,384]{1,0:T(8,128)(2,1)S(1)} %get-tuple-element.122), channel_id=1, source_target_pairs={{0,16},{8,24},{16,0},{24,8},{1,17},{9,25},{17,1},{25,9},{2,18},{10... | collective-permute-start | bytes 884744 | tf_op jit(solution)/shard_map/ppermute | solution.py:1051
  65.0 13.3 %collective-permute-start.10 = (bf16[384,384]{1,0:T(8,128)(2,1)S(1)}, bf16[384,384]{1,0:T(8,128)(2,1)S(1)}, u32[]{:S(2)}, u32[]{:S(2)}) collective-permute-start(bf16[384,384]{1,0:T(8,128)(2,1)S(1)} %get-tuple-element.123), channel_id=1, source_target_pairs={{0,24},{8,16},{16,8},{24,0},{1,25},{9,17},{17,9},{25,1},{2,26},{10... | collective-permute-start | bytes 884744 | tf_op jit(solution)/shard_map/ppermute | solution.py:1051
  65.9 22.1 %collective-permute-start.15 = (bf16[2,384,256]{2,1,0:T(8,128)(2,1)}, bf16[2,384,256]{2,1,0:T(8,128)(2,1)}, u32[]{:S(2)}, u32[]{:S(2)}) collective-permute-start(bf16[2,384,256]{2,1,0:T(8,128)(2,1)} %get-tuple-element.128.refs_1_), channel_id=1, source_target_pairs={{0,8},{8,0},{16,24},{24,16},{1,9},{9,1},{17,25},{25,17},{2,10},{10... | collective-permute-start | bytes 1179656 | tf_op jit(solution)/shard_map/ppermute | solution.py:1051
  72.3 18.1 %collective-permute-start.16 = (bf16[2,384,256]{2,1,0:T(8,128)(2,1)}, bf16[2,384,256]{2,1,0:T(8,128)(2,1)}, u32[]{:S(2)}, u32[]{:S(2)}) collective-permute-start(bf16[2,384,256]{2,1,0:T(8,128)(2,1)} %get-tuple-element.128.refs_1_), channel_id=1, source_target_pairs={{0,16},{8,24},{16,0},{24,8},{1,17},{9,25},{17,1},{25,9},{2,18},{10... | collective-permute-start | bytes 1179656 | tf_op jit(solution)/shard_map/ppermute | solution.py:1051
  76.0 18.1 %collective-permute-start.17 = (bf16[4608,256]{1,0:T(8,128)(2,1)}, bf16[4608,256]{1,0:T(8,128)(2,1)}, u32[]{:S(2)}, u32[]{:S(2)}) collective-permute-start(bf16[4608,256]{1,0:T(8,128)(2,1)} %get-tuple-element.129.refs_1_), channel_id=1, source_target_pairs={{0,1},{1,0},{2,3},{3,2},{4,5},{5,4},{6,7},{7,6},{8,9},{9,8},{10,11... | collective-permute-start | bytes 7077896 | tf_op jit(solution)/shard_map/ppermute | solution.py:1051
  90.4 12.1 %collective-permute-start.18 = (bf16[2,384,256]{2,1,0:T(8,128)(2,1)}, bf16[2,384,256]{2,1,0:T(8,128)(2,1)}, u32[]{:S(2)}, u32[]{:S(2)}) collective-permute-start(bf16[2,384,256]{2,1,0:T(8,128)(2,1)} %collective-permute-done.15.refs_11_.refs_2_), channel_id=1, source_target_pairs={{0,16},{8,24},{16,0},{24,8},{1,17},{9,25},{17,1},{25,9},{2,18},{10... | collective-permute-start | bytes 1179656 | tf_op jit(solution)/shard_map/ppermute | solution.py:1051
  102.4 15.2 %collective-permute-start.22 = (bf16[4608,256]{1,0:T(8,128)(2,1)}, bf16[4608,256]{1,0:T(8,128)(2,1)}, u32[]{:S(2)}, u32[]{:S(2)}) collective-permute-start(bf16[4608,256]{1,0:T(8,128)(2,1)} %get-tuple-element.142.refs_1_), channel_id=1, source_target_pairs={{0,1},{1,0},{2,3},{3,2},{4,5},{5,4},{6,7},{7,6},{8,9},{9,8},{10,11... | collective-permute-start | bytes 7077896 | tf_op jit(solution)/shard_map/ppermute | solution.py:1051
  114.1 14.3 %collective-permute-start.19 = (bf16[128,384]{1,0:T(8,128)(2,1)S(1)}, bf16[128,384]{1,0:T(8,128)(2,1)S(1)}, u32[]{:S(2)}, u32[]{:S(2)}) collective-permute-start(bf16[128,384]{1,0:T(8,128)(2,1)S(1)} %get-tuple-element.137), channel_id=1, source_target_pairs={{0,8},{8,0},{16,24},{24,16},{1,9},{9,1},{17,25},{25,17},{2,10},{10... | collective-permute-start | bytes 294920 | tf_op jit(solution)/shard_map/ppermute | solution.py:1051
  115.8 12.7 %collective-permute-start.20 = (bf16[128,384]{1,0:T(8,128)(2,1)S(1)}, bf16[128,384]{1,0:T(8,128)(2,1)S(1)}, u32[]{:S(2)}, u32[]{:S(2)}) collective-permute-start(bf16[128,384]{1,0:T(8,128)(2,1)S(1)} %get-tuple-element.138), channel_id=1, source_target_pairs={{0,16},{8,24},{16,0},{24,8},{1,17},{9,25},{17,1},{25,9},{2,18},{10... | collective-permute-start | bytes 294920 | tf_op jit(solution)/shard_map/ppermute | solution.py:1051
  116.8 11.7 %collective-permute-start.21 = (bf16[128,384]{1,0:T(8,128)(2,1)S(1)}, bf16[128,384]{1,0:T(8,128)(2,1)S(1)}, u32[]{:S(2)}, u32[]{:S(2)}) collective-permute-start(bf16[128,384]{1,0:T(8,128)(2,1)S(1)} %get-tuple-element.139), channel_id=1, source_target_pairs={{0,24},{8,16},{16,8},{24,0},{1,25},{9,17},{17,9},{25,1},{2,26},{10... | collective-permute-start | bytes 294920 | tf_op jit(solution)/shard_map/ppermute | solution.py:1051
  125.8 29.6 %collective-permute-start.27 = (bf16[8,624,128]{2,1,0:T(8,128)(2,1)}, bf16[8,624,128]{2,1,0:T(8,128)(2,1)}, u32[]{:S(2)}, u32[]{:S(2)}) collective-permute-start(bf16[8,624,128]{2,1,0:T(8,128)(2,1)} %get-tuple-element.145.refs_12_), channel_id=1, source_target_pairs={{0,2},{1,3},{2,0},{3,1},{4,6},{5,7},{6,4},{7,5},{8,10},{9,11},{10,... | collective-permute-start | bytes 3833864 | tf_op jit(solution)/shard_map/ppermute | solution.py:1051
  127.4 39.8 %collective-permute-start.28 = (bf16[8,672,128]{2,1,0:T(8,128)(2,1)}, bf16[8,672,128]{2,1,0:T(8,128)(2,1)}, u32[]{:S(2)}, u32[]{:S(2)}) collective-permute-start(bf16[8,672,128]{2,1,0:T(8,128)(2,1)} %get-tuple-element.156), channel_id=1, source_target_pairs={{0,16},{8,24},{16,0},{24,8},{1,17},{9,25},{17,1},{25,9},{2,18},{10... | collective-permute-start | bytes 4128776 | tf_op jit(solution)/shard_map/ppermute | solution.py:1051
  140.5 30.4 %collective-permute-start.24 = (bf16[384,384]{1,0:T(8,128)(2,1)S(1)}, bf16[384,384]{1,0:T(8,128)(2,1)S(1)}, u32[]{:S(2)}, u32[]{:S(2)}) collective-permute-start(bf16[384,384]{1,0:T(8,128)(2,1)S(1)} %get-tuple-element.147), channel_id=1, source_target_pairs={{0,8},{8,0},{16,24},{24,16},{1,9},{9,1},{17,25},{25,17},{2,10},{10... | collective-permute-start | bytes 884744 | tf_op jit(solution)/shard_map/ppermute | solution.py:1051
  142.2 29.2 %collective-permute-start.25 = (bf16[384,384]{1,0:T(8,128)(2,1)S(1)}, bf16[384,384]{1,0:T(8,128)(2,1)S(1)}, u32[]{:S(2)}, u32[]{:S(2)}) collective-permute-start(bf16[384,384]{1,0:T(8,128)(2,1)S(1)} %get-tuple-element.148), channel_id=1, source_target_pairs={{0,16},{8,24},{16,0},{24,8},{1,17},{9,25},{17,1},{25,9},{2,18},{10... | collective-permute-start | bytes 884744 | tf_op jit(solution)/shard_map/ppermute | solution.py:1051
  143.2 28.2 %collective-permute-start.26 = (bf16[384,384]{1,0:T(8,128)(2,1)S(1)}, bf16[384,384]{1,0:T(8,128)(2,1)S(1)}, u32[]{:S(2)}, u32[]{:S(2)}) collective-permute-start(bf16[384,384]{1,0:T(8,128)(2,1)S(1)} %get-tuple-element.149), channel_id=1, source_target_pairs={{0,24},{8,16},{16,8},{24,0},{1,25},{9,17},{17,9},{25,1},{2,26},{10... | collective-permute-start | bytes 884744 | tf_op jit(solution)/shard_map/ppermute | solution.py:1051
  155.5 25.3 %collective-permute-start.38 = (bf16[4,144,384]{2,1,0:T(8,128)(2,1)}, bf16[4,144,384]{2,1,0:T(8,128)(2,1)}, u32[]{:S(2)}, u32[]{:S(2)}) collective-permute-start(bf16[4,144,384]{2,1,0:T(8,128)(2,1)} %get-tuple-element.158.refs_18_), channel_id=1, source_target_pairs={{0,1},{1,0},{2,3},{3,2},{4,5},{5,4},{6,7},{7,6},{8,9},{9,8},{10,11... | collective-permute-start | bytes 1327112 | tf_op jit(solution)/shard_map/ppermute | solution.py:1051
  167.2 16.3 %collective-permute-start.33 = (bf16[4,624,128]{2,1,0:T(8,128)(2,1)}, bf16[4,624,128]{2,1,0:T(8,128)(2,1)}, u32[]{:S(2)}, u32[]{:S(2)}) collective-permute-start(bf16[4,624,128]{2,1,0:T(8,128)(2,1)} %add_convert_fusion.3.refs_16_), channel_id=1, source_target_pairs={{0,8},{8,0},{16,24},{24,16},{1,9},{9,1},{17,25},{25,17},{2,10},{10... | collective-permute-start | bytes 1916936 | tf_op jit(solution)/shard_map/ppermute | solution.py:1051
  171.0 24.6 %collective-permute-start.34 = (bf16[4,672,128]{2,1,0:T(8,128)(2,1)}, bf16[4,672,128]{2,1,0:T(8,128)(2,1)}, u32[]{:S(2)}, u32[]{:S(2)}) collective-permute-start(bf16[4,672,128]{2,1,0:T(8,128)(2,1)} %add_convert_fusion.1.refs_17_), channel_id=1, source_target_pairs={{0,2},{1,3},{2,0},{3,1},{4,6},{5,7},{6,4},{7,5},{8,10},{9,11},{10,... | collective-permute-start | bytes 2064392 | tf_op jit(solution)/shard_map/ppermute | solution.py:1051
  180.7 20.6 %collective-permute-start.32 = (bf16[256,2304]{1,0:T(8,128)(2,1)S(1)}, bf16[256,2304]{1,0:T(8,128)(2,1)S(1)}, u32[]{:S(2)}, u32[]{:S(2)}) collective-permute-start(bf16[256,2304]{1,0:T(8,128)(2,1)S(1)} %get-tuple-element.167), channel_id=1, source_target_pairs={{0,1},{1,0},{2,3},{3,2},{4,5},{5,4},{6,7},{7,6},{8,9},{9,8},{10,11... | collective-permute-start | bytes 3538952 | tf_op jit(solution)/shard_map/ppermute | solution.py:1051
  184.7 13.9 %collective-permute-start.41 = (bf16[2,624,128]{2,1,0:T(8,128)(2,1)S(1)}, bf16[2,624,128]{2,1,0:T(8,128)(2,1)S(1)}, u32[]{:S(2)}, u32[]{:S(2)}) collective-permute-start(bf16[2,624,128]{2,1,0:T(8,128)(2,1)S(1)} %add_convert_fusion.7.refs_13_), channel_id=1, source_target_pairs={{0,16},{8,24},{16,0},{24,8},{1,17},{9,25},{17,1},{25,9},{2,18},{10... | collective-permute-start | bytes 958472 | tf_op jit(solution)/shard_map/ppermute | solution.py:1051
  191.4 74.3 %collective-permute-start.66 = (bf16[1,144,384]{2,1,0:T(8,128)(2,1)}, bf16[1,144,384]{2,1,0:T(8,128)(2,1)}, u32[]{:S(2)}, u32[]{:S(2)}) collective-permute-start(bf16[1,144,384]{2,1,0:T(8,128)(2,1)} %add_convert_fusion.14), channel_id=1, source_target_pairs={{0,4},{1,5},{2,6},{3,7},{4,0},{5,1},{6,2},{7,3},{8,12},{9,13},{10,... | collective-permute-start | bytes 331784 | tf_op jit(solution)/shard_map/ppermute | solution.py:1051
  194.0 17.3 %collective-permute-start.29 = (bf16[128,384]{1,0:T(8,128)(2,1)S(1)}, bf16[128,384]{1,0:T(8,128)(2,1)S(1)}, u32[]{:S(2)}, u32[]{:S(2)}) collective-permute-start(bf16[128,384]{1,0:T(8,128)(2,1)S(1)} %get-tuple-element.161), channel_id=1, source_target_pairs={{0,8},{8,0},{16,24},{24,16},{1,9},{9,1},{17,25},{25,17},{2,10},{10... | collective-permute-start | bytes 294920 | tf_op jit(solution)/shard_map/ppermute | solution.py:1051
  195.6 16.2 %collective-permute-start.30 = (bf16[128,384]{1,0:T(8,128)(2,1)S(1)}, bf16[128,384]{1,0:T(8,128)(2,1)S(1)}, u32[]{:S(2)}, u32[]{:S(2)}) collective-permute-start(bf16[128,384]{1,0:T(8,128)(2,1)S(1)} %get-tuple-element.162), channel_id=1, source_target_pairs={{0,16},{8,24},{16,0},{24,8},{1,17},{9,25},{17,1},{25,9},{2,18},{10... | collective-permute-start | bytes 294920 | tf_op jit(solution)/shard_map/ppermute | solution.py:1051
  198.6 14.7 %collective-permute-start.31 = (bf16[128,384]{1,0:T(8,128)(2,1)S(1)}, bf16[128,384]{1,0:T(8,128)(2,1)S(1)}, u32[]{:S(2)}, u32[]{:S(2)}) collective-permute-start(bf16[128,384]{1,0:T(8,128)(2,1)S(1)} %get-tuple-element.163), channel_id=1, source_target_pairs={{0,24},{8,16},{16,8},{24,0},{1,25},{9,17},{17,9},{25,1},{2,26},{10... | collective-permute-start | bytes 294920 | tf_op jit(solution)/shard_map/ppermute | solution.py:1051
  201.3 27.2 %collective-permute-start.42 = (bf16[2,672,128]{2,1,0:T(8,128)(2,1)}, bf16[2,672,128]{2,1,0:T(8,128)(2,1)}, u32[]{:S(2)}, u32[]{:S(2)}) collective-permute-start(bf16[2,672,128]{2,1,0:T(8,128)(2,1)} %add_convert_fusion.5.refs_14_), channel_id=1, source_target_pairs={{0,8},{8,0},{16,24},{24,16},{1,9},{9,1},{17,25},{25,17},{2,10},{10... | collective-permute-start | bytes 1032200 | tf_op jit(solution)/shard_map/ppermute | solution.py:1051
  211.3 28.7 %collective-permute-start.39 = (bf16[8,624,128]{2,1,0:T(8,128)(2,1)}, bf16[8,624,128]{2,1,0:T(8,128)(2,1)}, u32[]{:S(2)}, u32[]{:S(2)}) collective-permute-start(bf16[8,624,128]{2,1,0:T(8,128)(2,1)} %get-tuple-element.168.refs_12_), channel_id=1, source_target_pairs={{0,2},{1,3},{2,0},{3,1},{4,6},{5,7},{6,4},{7,5},{8,10},{9,11},{10,... | collective-permute-start | bytes 3833864 | tf_op jit(solution)/shard_map/ppermute | solution.py:1051
  211.8 33.4 %collective-permute-start.40 = (bf16[8,672,128]{2,1,0:T(8,128)(2,1)}, bf16[8,672,128]{2,1,0:T(8,128)(2,1)}, u32[]{:S(2)}, u32[]{:S(2)}) collective-permute-start(bf16[8,672,128]{2,1,0:T(8,128)(2,1)} %get-tuple-element.178), channel_id=1, source_target_pairs={{0,8},{8,0},{16,24},{24,16},{1,9},{9,1},{17,25},{25,17},{2,10},{10... | collective-permute-start | bytes 4128776 | tf_op jit(solution)/shard_map/ppermute | solution.py:1051
  231.6 19.9 %collective-permute-start.35 = (bf16[384,384]{1,0:T(8,128)(2,1)S(1)}, bf16[384,384]{1,0:T(8,128)(2,1)S(1)}, u32[]{:S(2)}, u32[]{:S(2)}) collective-permute-start(bf16[384,384]{1,0:T(8,128)(2,1)S(1)} %get-tuple-element.170), channel_id=1, source_target_pairs={{0,8},{8,0},{16,24},{24,16},{1,9},{9,1},{17,25},{25,17},{2,10},{10... | collective-permute-start | bytes 884744 | tf_op jit(solution)/shard_map/ppermute | solution.py:1051
  232.1 20.9 %collective-permute-start.36 = (bf16[384,384]{1,0:T(8,128)(2,1)S(1)}, bf16[384,384]{1,0:T(8,128)(2,1)S(1)}, u32[]{:S(2)}, u32[]{:S(2)}) collective-permute-start(bf16[384,384]{1,0:T(8,128)(2,1)S(1)} %get-tuple-element.171), channel_id=1, source_target_pairs={{0,16},{8,24},{16,0},{24,8},{1,17},{9,25},{17,1},{25,9},{2,18},{10... | collective-permute-start | bytes 884744 | tf_op jit(solution)/shard_map/ppermute | solution.py:1051
  239.9 15.2 %collective-permute-start.37 = (bf16[384,384]{1,0:T(8,128)(2,1)S(1)}, bf16[384,384]{1,0:T(8,128)(2,1)S(1)}, u32[]{:S(2)}, u32[]{:S(2)}) collective-permute-start(bf16[384,384]{1,0:T(8,128)(2,1)S(1)} %get-tuple-element.172), channel_id=1, source_target_pairs={{0,24},{8,16},{16,8},{24,0},{1,25},{9,17},{17,9},{25,1},{2,26},{10... | collective-permute-start | bytes 884744 | tf_op jit(solution)/shard_map/ppermute | solution.py:1051
  245.2 24.8 %collective-permute-start.51 = (bf16[1,1296,128]{2,1,0:T(8,128)(2,1)}, bf16[1,1296,128]{2,1,0:T(8,128)(2,1)}, u32[]{:S(2)}, u32[]{:S(2)}) collective-permute-start(bf16[1,1296,128]{2,1,0:T(8,128)(2,1)} %pad_maximum_fusion.refs_13_), channel_id=1, source_target_pairs={{0,4},{1,5},{2,6},{3,7},{4,0},{5,1},{6,2},{7,3},{8,12},{9,13},{10,... | collective-permute-start | bytes 995336 | tf_op jit(solution)/shard_map/ppermute | solution.py:1051
  262.4 12.8 %collective-permute-start.61 = (bf16[1,144,384]{2,1,0:T(8,128)(2,1)}, bf16[1,144,384]{2,1,0:T(8,128)(2,1)S(1)}, u32[]{:S(2)}, u32[]{:S(2)}) collective-permute-start(bf16[1,144,384]{2,1,0:T(8,128)(2,1)} %add_convert_fusion.15), channel_id=1, source_target_pairs={{0,4},{1,5},{2,6},{3,7},{4,0},{5,1},{6,2},{7,3},{8,12},{9,13},{10,... | collective-permute-start | bytes 331784 | tf_op jit(solution)/shard_map/ppermute | solution.py:1051
  264.6 13.2 %collective-permute-start.44 = (f32[1,23808]{1,0:T(1,128)}, f32[1,23808]{1,0:T(1,128)}, u32[]{:S(2)}, u32[]{:S(2)}) collective-permute-start(f32[1,23808]{1,0:T(1,128)} %add.197), channel_id=1, source_target_pairs={{0,16},{8,24},{16,0},{24,8},{1,17},{9,25},{17,1},{25,9},{2,18},{10... | collective-permute-start | bytes 285704 | tf_op jit(solution)/shard_map/ppermute | solution.py:1051
  267.5 72.5 %collective-permute-start.67 = (f32[24,576]{1,0:T(8,128)}, f32[24,576]{1,0:T(8,128)S(1)}, u32[]{:S(2)}, u32[]{:S(2)}) collective-permute-start(f32[24,576]{1,0:T(8,128)} %get-tuple-element.195), channel_id=1, source_target_pairs={{0,8},{8,0},{16,24},{24,16},{1,9},{9,1},{17,25},{25,17},{2,10},{10... | collective-permute-start | bytes 165896 | tf_op jit(solution)/shard_map/ppermute | solution.py:1051
  269.0 76.4 %collective-permute-start.68 = (f32[24,576]{1,0:T(8,128)}, f32[24,576]{1,0:T(8,128)S(1)}, u32[]{:S(2)}, u32[]{:S(2)}) collective-permute-start(f32[24,576]{1,0:T(8,128)} %get-tuple-element.196), channel_id=1, source_target_pairs={{0,16},{8,24},{16,0},{24,8},{1,17},{9,25},{17,1},{25,9},{2,18},{10... | collective-permute-start | bytes 165896 | tf_op jit(solution)/shard_map/ppermute | solution.py:1051
  270.0 77.2 %collective-permute-start.69 = (f32[24,576]{1,0:T(8,128)}, f32[24,576]{1,0:T(8,128)}, u32[]{:S(2)}, u32[]{:S(2)}) collective-permute-start(f32[24,576]{1,0:T(8,128)} %get-tuple-element.197), channel_id=1, source_target_pairs={{0,24},{8,16},{16,8},{24,0},{1,25},{9,17},{17,9},{25,1},{2,26},{10... | collective-permute-start | bytes 165896 | tf_op jit(solution)/shard_map/ppermute | solution.py:1051
  286.8 16.4 %collective-permute-start.53 = (bf16[4,624,128]{2,1,0:T(8,128)(2,1)}, bf16[4,624,128]{2,1,0:T(8,128)(2,1)}, u32[]{:S(2)}, u32[]{:S(2)}) collective-permute-start(bf16[4,624,128]{2,1,0:T(8,128)(2,1)} %add_convert_fusion.2.refs_11_), channel_id=1, source_target_pairs={{0,16},{8,24},{16,0},{24,8},{1,17},{9,25},{17,1},{25,9},{2,18},{10... | collective-permute-start | bytes 1916936 | tf_op jit(solution)/shard_map/ppermute | solution.py:1051
  300.7 14.5 %collective-permute-start.55 = (bf16[4,672,128]{2,1,0:T(8,128)(2,1)}, bf16[4,672,128]{2,1,0:T(8,128)(2,1)S(1)}, u32[]{:S(2)}, u32[]{:S(2)}) collective-permute-start(bf16[4,672,128]{2,1,0:T(8,128)(2,1)} %add_convert_fusion.refs_12_), channel_id=1, source_target_pairs={{0,2},{1,3},{2,0},{3,1},{4,6},{5,7},{6,4},{7,5},{8,10},{9,11},{10,... | collective-permute-start | bytes 2064392 | tf_op jit(solution)/shard_map/ppermute | solution.py:1051
  304.5 13.0 %collective-permute-start.54 = (bf16[2,624,128]{2,1,0:T(8,128)(2,1)S(1)}, bf16[2,624,128]{2,1,0:T(8,128)(2,1)S(1)}, u32[]{:S(2)}, u32[]{:S(2)}) collective-permute-start(bf16[2,624,128]{2,1,0:T(8,128)(2,1)S(1)} %add_convert_fusion.6), channel_id=1, source_target_pairs={{0,8},{8,0},{16,24},{24,16},{1,9},{9,1},{17,25},{25,17},{2,10},{10... | collective-permute-start | bytes 958472 | tf_op jit(solution)/shard_map/ppermute | solution.py:1051
  317.5 30.3 %collective-permute-start.52 = (f32[648,128]{1,0:T(8,128)S(1)}, f32[648,128]{1,0:T(8,128)S(1)}, u32[]{:S(2)}, u32[]{:S(2)}) collective-permute-start(f32[648,128]{1,0:T(8,128)S(1)} %copy-done.45), channel_id=1, source_target_pairs={{0,1},{1,0},{2,3},{3,2},{4,5},{5,4},{6,7},{7,6},{8,9},{9,8},{10,11... | collective-permute-start | bytes 995336 | tf_op jit(solution)/shard_map/ppermute | solution.py:1051
  324.7 12.4 %collective-permute-start.57 = (bf16[1,1296,128]{2,1,0:T(8,128)(2,1)S(1)}, bf16[1,1296,128]{2,1,0:T(8,128)(2,1)S(1)}, u32[]{:S(2)}, u32[]{:S(2)}) collective-permute-start(bf16[1,1296,128]{2,1,0:T(8,128)(2,1)S(1)} %pad_maximum_fusion.1), channel_id=1, source_target_pairs={{0,4},{1,5},{2,6},{3,7},{4,0},{5,1},{6,2},{7,3},{8,12},{9,13},{10,... | collective-permute-start | bytes 995336 | tf_op jit(solution)/shard_map/ppermute | solution.py:1051
  339.7 12.6 %collective-permute-start.58 = (f32[648,128]{1,0:T(8,128)S(1)}, f32[648,128]{1,0:T(8,128)S(1)}, u32[]{:S(2)}, u32[]{:S(2)}) collective-permute-start(f32[648,128]{1,0:T(8,128)S(1)} %get-tuple-element.188), channel_id=1, source_target_pairs={{0,1},{1,0},{2,3},{3,2},{4,5},{5,4},{6,7},{7,6},{8,9},{9,8},{10,11... | collective-permute-start | bytes 995336 | tf_op jit(solution)/shard_map/ppermute | solution.py:1051
  (99 other events, 1210.6 us)

commit v3 on v2

--- a/solution.py
+++ b/solution.py
@@ -458,6 +458,7 @@
 VM = pl.BlockSpec(memory_space=pltpu.VMEM)
 ANY = pl.BlockSpec(memory_space=pl.ANY)
 HBM = pl.BlockSpec(memory_space=pltpu.HBM)
+HV = pl.BlockSpec(memory_space=pltpu.VMEM)
 SM = pl.BlockSpec(memory_space=pltpu.SMEM)
 MEBI = 1024 * 1024
 ROOT_TWO_PI = math.sqrt(2.0 / math.pi)
@@ -507,12 +508,8 @@
     return row[:, number * WIDTH : (number + 1) * WIDTH]
 
 
-BIAS_AT = {"triple": (0, 2304), "output": (2304, 3072), "expand": (3072, 6144), "shrink": (6144, 6912)}
-
-
-def bias_of(bias_ref, layer, name):
-    low, high = BIAS_AT[name]
-    return bias_ref[layer][:, low:high]
+def row_of(ref, layer):
+    return ref[...].astype(F32)[layer : layer + 1, :]
 
 
 def pack_rows(values):
@@ -520,7 +517,7 @@
     return jnp.concatenate([values[:half], values[half:]], 1)
 
 
-def qkv_stage(x, layer, mod_row, bias_ref, triple, cos_ref, sin_ref, me, h_ref, chunk_refs, hold):
+def qkv_stage(x, layer, mod_row, triple_bias, triple, cos_ref, sin_ref, me, h_ref, chunk_refs, hold):
     unit, _ = normalise(x)
     h = unit * (1.0 + piece_of(mod_row, 1)) + piece_of(mod_row, 0)
     turned = h.T
@@ -529,7 +526,7 @@
     for half in range(2):
         picked = [turned[each * (b * 8 + z * 2 + half) :][:each] for z in range(4) for b in range(4)]
         h_ref[half] = jnp.concatenate(picked, 0).astype(BF)
-    bias = bias_of(bias_ref, layer, "triple")
+    bias = row_of(triple_bias, layer)
     cosine, sine = cos_ref[0], sin_ref[0]
     parts = []
     for number in range(3):
@@ -550,40 +547,60 @@
         chunk_refs[place][...] = hold[place ^ me]
 
 
+def fetch(pairs, sems):
+    copies = []
+    for number, (source, target) in enumerate(pairs):
+        copy = pltpu.make_async_copy(source, target, sems.at[number])
+        copy.start()
+        copies.append(copy)
+    return copies
+
+
+def three_rows(row):
+    upper = row.astype(BF).astype(F32)
+    rest = row - upper
+    middle = rest.astype(BF).astype(F32)
+    low = rest - middle
+    number = lax.broadcasted_iota(jnp.int32, (8, row.shape[1]), 0)
+    return jnp.where(number == 0, upper, jnp.where(number == 1, middle, jnp.where(number == 2, low, 0.0))).astype(BF)
+
+
+def modulation(cond, adaptive, adaptive_bias, layer):
+    return column_sum(dot_nn(three_rows(cond), adaptive[...])) + row_of(adaptive_bias, layer)
+
+
 def first_kernel(
-    scal, inputs, mask_embed, condition, adaptive_weight, adaptive_bias, bias_ref, cos_ref, sin_ref, triple_any,
+    scal, mask_embed, cos_ref, sin_ref, inputs_any, condition_any, adaptive_bias_any, triple_bias_any, adaptive_any,
+    triple_any,
     x_ref, mod_ref, h_ref, c0, c1, c2, c3,
-    triple, hold, sems,
+    inputs, condition, adaptive_bias, triple_bias, adaptive, triple, hold, sems,
 ):
-    copy = pltpu.make_async_copy(triple_any.at[0], triple, sems.at[0])
-    copy.start()
+    copies = fetch(
+        [
+            (adaptive_any.at[0], adaptive), (triple_any.at[0], triple), (inputs_any, inputs),
+            (condition_any, condition), (adaptive_bias_any, adaptive_bias), (triple_bias_any, triple_bias),
+        ],
+        sems,
+    )
+    for copy in copies[2:]:
+        copy.wait()
     me = scal[0]
-    cond = condition[...]
-    upper = cond.astype(BF).astype(F32)
-    rest = cond - upper
-    mid = rest.astype(BF).astype(F32)
-    low = rest - mid
-    row = lax.broadcasted_iota(jnp.int32, (8, cond.shape[1]), 0)
-    stack = jnp.where(row == 0, upper, jnp.where(row == 1, mid, jnp.where(row == 2, low, 0.0))).astype(BF)
-    for layer in range(LAYERS):
-        total = column_sum(dot_nn(stack, adaptive_weight[layer]))
-        mod_ref[layer] = total + adaptive_bias[layer].astype(F32)
     rows = inputs.shape[1]
     position = me * rows + lax.broadcasted_iota(jnp.int32, (rows, WIDTH), 0)
     x = jnp.where(position >= scal[3], mask_embed[...].astype(F32), inputs[0].astype(F32))
     x_ref[...] = x
-    copy.wait()
-    qkv_stage(
-        x, 0, mod_ref[0], bias_ref, triple, cos_ref, sin_ref, me, h_ref, (c0, c1, c2, c3), hold,
-    )
+    copies[0].wait()
+    mod = modulation(condition[...], adaptive, adaptive_bias, 0)
+    mod_ref[...] = mod
+    copies[1].wait()
+    qkv_stage(x, 0, mod, triple_bias, triple, cos_ref, sin_ref, me, h_ref, (c0, c1, c2, c3), hold)
 
 
 def attend_kernel(
     c0, c1, c2, c3,
-    o0, o1, o2, o3, lse_ref, ot_ref,
-    q_all, k_all, v_turned,
+    o0, o1, o2, o3, lse_ref, of_ref,
+    ot_ref, q_all, k_all, v_turned,
 ):
-    rows = c0.shape[1] * 2 // 3
     rows = 256
     for place, chunk in enumerate((c0, c1, c2, c3)):
         span = slice(place * rows, (place + 1) * rows)
@@ -591,25 +608,32 @@
         k_all[span, :] = chunk[0:rows, GROUP : 2 * GROUP]
         tail = chunk[rows : rows + rows // 2, :]
         v_block = jnp.concatenate([tail[:, 0:GROUP], tail[:, GROUP : 2 * GROUP]], 0)
-        v_turned[:, span] = v_block.T
-    head = lax.broadcasted_iota(jnp.int32, (rows, GROUP), 1) // HEAD_DIM
-
-    def step(block, carry):
-        q = q_all[block]
+        v_block = v_block.T
+        for number in range(3):
+            v_turned[number, 0:HEAD_DIM, span] = v_block[number * HEAD_DIM : (number + 1) * HEAD_DIM]
+    v_turned[:, HEAD_DIM:, :] = jnp.ones((3, 16, 4 * rows), BF)
+    head = lax.broadcasted_iota(jnp.int32, (2 * rows, GROUP), 1) // HEAD_DIM
+
+    for block in range(0, 4, 2):
+        q = q_all[block : block + 2].reshape(2 * rows, GROUP)
         for number in range(3):
             masked = jnp.where(head == number, q, jnp.zeros_like(q))
             scores = dot_nt(k_all[...], masked)
             peak = jnp.max(scores, 0, keepdims=True)
-            weights = jnp.exp(scores - peak)
-            total = jnp.sum(weights, 0, keepdims=True)
+            weights = jnp.exp(scores - peak).astype(BF)
+            both = dot_nn(v_turned[number], weights)
+            total = both[HEAD_DIM : HEAD_DIM + 1]
             span = slice(number * HEAD_DIM, (number + 1) * HEAD_DIM)
-            ot_ref[block, span, :] = dot_nn(v_turned[span, :], weights.astype(BF)) / total
-            lse_ref[block, number : number + 1, :] = peak + jnp.log(total)
-        return carry
-
-    lax.fori_loop(0, 4, step, 0)
+            found = both[0:HEAD_DIM] / total
+            lse = peak + jnp.log(total)
+            for part in range(2):
+                columns = slice(part * rows, (part + 1) * rows)
+                ot_ref[block + part, span, :] = found[:, columns]
+                lse_ref[block + part, number : number + 1, :] = lse[:, columns]
     for place, out in enumerate((o0, o1, o2, o3)):
-        out[...] = pack_rows(ot_ref[place].T).astype(BF)
+        found = ot_ref[place].T
+        of_ref[place] = found
+        out[...] = pack_rows(found).astype(BF)
 
 
 def gather_chunks(refs, hold):
@@ -618,7 +642,7 @@
 
 
 def mlp_forward(
-    layer, x, mod_row, bias_ref, me, o_refs, output, expand, shrink, waits, hold, o_ref, aout_ref, m_ref, turned_ref,
+    layer, x, mod_row, biases, me, o_refs, output, expand, shrink, waits, hold, o_ref, aout_ref, m_ref, turned_ref,
     slope_ref, f_ref,
 ):
     gather_chunks(o_refs, hold)
@@ -633,7 +657,7 @@
     hidden = expand.shape[1]
     turned_ref[hidden + WIDTH : hidden + 2 * WIDTH, :] = o.T
     waits[0].wait()
-    a_out = dot_nn(o, output[...]) + bias_of(bias_ref, layer, "output")
+    a_out = dot_nn(o, output[...]) + row_of(biases[0], layer)
     aout_ref[...] = a_out.astype(BF)
     m = x + piece_of(mod_row, 2) * a_out
     m_ref[...] = m
@@ -641,8 +665,8 @@
     h2 = (unit * (1.0 + piece_of(mod_row, 4)) + piece_of(mod_row, 3)).astype(BF)
     turned_ref[hidden : hidden + WIDTH, :] = h2.T
     waits[1].wait()
-    bias = bias_of(bias_ref, layer, "expand")
-    f = bias_of(bias_ref, layer, "shrink")
+    bias = row_of(biases[1], layer)
+    f = row_of(biases[2], layer)
     for start in range(0, hidden, 768):
         columns = slice(start, start + 768)
         u = dot_nn(h2, expand[:, columns]) + bias[:, columns]
@@ -667,8 +691,8 @@
 
 
 def mlp_backward(
-    dy, mod_row, me, core, m_ref, f_ref, slope_ref, aout_ref, output, expand, shrink, waits, hold, halves,
-    do_refs, dm_ref, vec_ref,
+    dy, mod_row, me, core, m_ref, f_ref, slope_ref, aout_ref, output, expand, shrink, waits, halves,
+    do_ref, dm_ref, vec_ref,
 ):
     def put(place, row):
         vec_ref[:, place : place + row.shape[1]] = row
@@ -702,21 +726,21 @@
     waits[0].wait()
     do = dot_nt(da, output[...])
     for group in range(4):
-        hold[group] = pack_rows(do[:, group * GROUP : (group + 1) * GROUP]).astype(BF)
-    for place in range(4):
-        do_refs[place][...] = hold[place ^ me]
+        do_ref[group] = pack_rows(do[:, group * GROUP : (group + 1) * GROUP]).astype(BF)
 
 
 def attend_back_kernel(
-    c0, c1, c2, c3, d0, d1, d2, d3, lse_ref, ot_ref, cos_ref, sin_ref,
-    g0, g1, g2, g3, stacked,
-    q_masked, do_masked, k_all, v_all, k_turned, lse_rows, delta_rows, dq_turned, dk_all, dv_all,
+    scal, given_ref, c0, c1, c2, c3, lse_ref, of_ref, cos_any, sin_any, stacked,
+    cos_ref, sin_ref, sems, q_masked, do_masked, k_all, v_all, k_turned, lse_rows, delta_rows, dq_turned, dk_all, dv_all,
 ):
+    copies = fetch([(cos_any, cos_ref), (sin_any, sin_ref)], sems)
     rows = 256
     head = lax.broadcasted_iota(jnp.int32, (rows, GROUP), 1) // HEAD_DIM
+    of_head = lax.broadcasted_iota(jnp.int32, (8, GROUP), 1) // HEAD_DIM
+    pick = jnp.where(of_head == lax.broadcasted_iota(jnp.int32, (8, GROUP), 0), 1.0, 0.0).astype(BF)
     for place in range(4):
         chunk = (c0, c1, c2, c3)[place]
-        given = (d0, d1, d2, d3)[place][...]
+        given = given_ref[place ^ scal[0]]
         span = slice(place * rows, (place + 1) * rows)
         q = chunk[0:rows, 0:GROUP]
         k = chunk[0:rows, GROUP : 2 * GROUP]
@@ -725,20 +749,21 @@
         k_all[place] = k
         k_turned[place] = k.T
         do = jnp.concatenate([given[:, 0:GROUP], given[:, GROUP : 2 * GROUP]], 0)
-        product = do.astype(F32).T * ot_ref[place]
+        product = do.astype(F32) * of_ref[place]
+        upper = product.astype(BF)
+        lower = (product - upper.astype(F32)).astype(BF)
+        delta_rows[:, span] = dot_nt(pick, upper) + dot_nt(pick, lower)
         for number in range(3):
             q_masked[number, span, :] = jnp.where(head == number, q, jnp.zeros_like(q))
             do_masked[number, span, :] = jnp.where(head == number, do, jnp.zeros_like(do))
-            part = product[number * HEAD_DIM : (number + 1) * HEAD_DIM, :]
-            delta_rows[number : number + 1, span] = jnp.sum(part, 0, keepdims=True)
             lse_rows[number : number + 1, span] = lse_ref[place, number : number + 1, :]
     dq_turned[...] = jnp.zeros(dq_turned.shape, F32)
 
-    def step(block, carry):
-        k = k_all[block]
-        v = v_all[block]
-        dk = jnp.zeros((rows, GROUP), F32)
-        dv = jnp.zeros((rows, GROUP), F32)
+    for block in range(4 // 2):
+        k = k_all[block * 2 : (block + 1) * 2].reshape(2 * rows, GROUP)
+        v = v_all[block * 2 : (block + 1) * 2].reshape(2 * rows, GROUP)
+        dk = jnp.zeros((2 * rows, GROUP), F32)
+        dv = jnp.zeros((2 * rows, GROUP), F32)
         for number in range(3):
             span = slice(number * HEAD_DIM, (number + 1) * HEAD_DIM)
             scores = dot_nt(k, q_masked[number])
@@ -747,29 +772,27 @@
             score_grad = (probs * (prob_grad - delta_rows[number : number + 1, :])).astype(BF)
             dv = dv + dot_nn(probs.astype(BF), do_masked[number])
             dk = dk + dot_nn(score_grad, q_masked[number])
-            dq_turned[span, :] += dot_nn(k_turned[block, span, :], score_grad)
-        dk_all[block] = dk
-        dv_all[block] = dv
-        return carry
-
-    lax.fori_loop(0, 4, step, 0)
-    for place, out in enumerate((g0, g1, g2, g3)):
+            for part in range(2):
+                dq_turned[span, :] += dot_nn(k_turned[block * 2 + part, span, :], score_grad[part * rows : (part + 1) * rows])
+        dk_all[block * 2 : (block + 1) * 2] = dk.reshape(2, rows, GROUP)
+        dv_all[block * 2 : (block + 1) * 2] = dv.reshape(2, rows, GROUP)
+    for copy in copies:
+        copy.wait()
+    for place in range(4):
         span = slice(place * rows, (place + 1) * rows)
         dq = dq_turned[:, span].T * HEAD_DIM**-0.5
         pair = jnp.concatenate([dq, dk_all[place]], 1)
         pair = turn(pair, cos_ref[place], -sin_ref[place]).astype(BF)
         tail = pack_rows(dv_all[place]).astype(BF)
-        for target in (out, stacked.at[place]):
-            target[0:rows, :] = pair
-            target[rows : rows + rows // 2, :] = tail
-
-
-def qkv_backward(x, dm, mod_row, me, g_refs, triple, wait, hold, full, vec_ref):
-    gather_chunks(g_refs, hold)
+        stacked[place ^ scal[0], 0:rows, :] = pair
+        stacked[place ^ scal[0], rows : rows + rows // 2, :] = tail
+
+
+def qkv_backward(x, dm, mod_row, chunks, triple, wait, full, vec_ref):
     rows = x.shape[0]
     half = rows // 2
     for group in range(4):
-        chunk = hold[group ^ me]
+        chunk = chunks(group)
         low = group * GROUP
         full[:, low : low + GROUP] = chunk[0:rows, 0:GROUP]
         full[:, WIDTH + low : WIDTH + low + GROUP] = chunk[0:rows, GROUP : 2 * GROUP]
@@ -785,74 +808,74 @@
     return dm + normalise_back(dh * (1.0 + piece_of(mod_row, 1)), unit, rstd)
 
 
-def fetch(pairs, sems):
-    copies = []
-    for number, (source, target) in enumerate(pairs):
-        copy = pltpu.make_async_copy(source, target, sems.at[number])
-        copy.start()
-        copies.append(copy)
-    return copies
-
-
-class Done:
-    def wait(self):
-        pass
-
-
 def middle_kernel(
-    scal, x_ref, mod_ref, bias_ref, cos_ref, sin_ref, o0, o1, o2, o3, output_any, expand_any, shrink_any, triple_any,
-    aout_ref, m_ref, turned_ref, slope_ref, f_ref, y_ref, h_ref, c0, c1, c2, c3,
-    output, expand, shrink, triple, o_hold, o_ref, c_hold, sems,
+    scal, x_ref, mod_ref, condition, adaptive_bias, output_bias, expand_bias, shrink_bias, triple_bias,
+    cos_ref, sin_ref, o0, o1, o2, o3, output_any, expand_any, shrink_any, triple_any, adaptive_any,
+    aout_ref, m_ref, turned_ref, slope_ref, f_ref, y_ref, mod_next, h_ref, c0, c1, c2, c3,
+    output, expand, shrink, triple, adaptive, o_hold, o_ref, c_hold, sems,
 ):
     copies = fetch(
-        [(output_any.at[0], output), (expand_any.at[0], expand), (shrink_any.at[0], shrink), (triple_any.at[1], triple)],
+        [
+            (output_any.at[0], output), (expand_any.at[0], expand), (shrink_any.at[0], shrink),
+            (triple_any.at[1], triple), (adaptive_any.at[1], adaptive),
+        ],
         sems,
     )
     me = scal[0]
     y = mlp_forward(
-        0, x_ref[...], mod_ref[0], bias_ref, me, (o0, o1, o2, o3), output, expand, shrink, copies, o_hold, o_ref,
+        0, x_ref[...], mod_ref[...], (output_bias, expand_bias, shrink_bias), me, (o0, o1, o2, o3), output, expand, shrink, copies, o_hold, o_ref,
         aout_ref, m_ref, turned_ref, slope_ref, f_ref,
     )
     y_ref[...] = y
     copies[3].wait()
+    copies[4].wait()
+    mod = modulation(condition[...], adaptive, adaptive_bias, 1)
+    mod_next[...] = mod
     qkv_stage(
-        y, 1, mod_ref[1], bias_ref, triple, cos_ref, sin_ref, me, h_ref, (c0, c1, c2, c3), c_hold,
+        y, 1, mod, triple_bias, triple, cos_ref, sin_ref, me, h_ref, (c0, c1, c2, c3), c_hold,
     )
 
 
 def ahead_kernel(
-    scal, x_ref, mod_ref, bias_ref, o0, o1, o2, o3, output_any, expand_any, shrink_any,
+    scal, x_ref, mod_ref, output_bias, expand_bias, shrink_bias, o0, o1, o2, o3, output_any, expand_any, shrink_any,
     out_ref, aout_ref, m_ref, turned_ref, slope_ref, f_ref,
     output, expand, shrink, o_hold, o_ref, sems,
 ):
     copies = fetch([(output_any.at[1], output), (expand_any.at[1], expand), (shrink_any.at[1], shrink)], sems)
     y = mlp_forward(
-        1, x_ref[...], mod_ref[1], bias_ref, scal[0], (o0, o1, o2, o3), output, expand, shrink, copies, o_hold, o_ref,
+        1, x_ref[...], mod_ref[...], (output_bias, expand_bias, shrink_bias), scal[0], (o0, o1, o2, o3), output, expand, shrink, copies, o_hold, o_ref,
         aout_ref, m_ref, turned_ref, slope_ref, f_ref,
     )
     out_ref[0] = y.astype(BF)
 
 
 def turn_kernel(
-    scal, cotangent, mod_ref, m_ref, f_ref, slope_ref, aout_ref, output_any, expand_any, shrink_any,
-    mine, theirs, d0, d1, d2, d3, dm_ref, vec_ref,
-    output, expand, shrink, o_hold, halves, sems,
+    scal, mod_ref, m_ref, f_ref, slope_ref, aout_ref, cotangent_any, output_any, expand_any, shrink_any,
+    mine, theirs, do_ref, dm_ref, vec_ref,
+    output, expand, shrink, cotangent, halves, sems,
 ):
-    copies = fetch([(shrink_any.at[1], shrink), (expand_any.at[1], expand), (output_any.at[1], output)], sems)
+    copies = fetch(
+        [
+            (shrink_any.at[1], shrink), (expand_any.at[1], expand), (output_any.at[1], output),
+            (cotangent_any, cotangent),
+        ],
+        sems,
+    )
+    copies[3].wait()
     me, core = scal[0], scal[2]
     mlp_backward(
-        cotangent[0].astype(F32), mod_ref[1], me, core, m_ref, f_ref, slope_ref, aout_ref, output, expand, shrink,
-        [copies[2], copies[1], copies[0]], o_hold, halves, (d0, d1, d2, d3), dm_ref, vec_ref,
+        cotangent[0].astype(F32), mod_ref[...], me, core, m_ref, f_ref, slope_ref, aout_ref, output, expand, shrink,
+        [copies[2], copies[1], copies[0]], halves, do_ref, dm_ref, vec_ref,
     )
     mine[...] = halves[core]
     theirs[...] = halves[1 - core]
 
 
 def back_kernel(
-    scal, x_ref, dm_in, mod_ref, g0, g1, g2, g3, m_ref, f_ref, slope_ref, aout_ref,
+    scal, x_ref, dm_in, mod_ref, mod_low, grads, m_ref, f_ref, slope_ref, aout_ref,
     triple_any, output_any, expand_any, shrink_any,
-    mine, theirs, vec_first, d0, d1, d2, d3, dm_ref, vec_ref,
-    triple, output, expand, shrink, g_hold, full, o_hold, halves, sems,
+    mine, theirs, vec_first, do_ref, dm_ref, vec_ref,
+    triple, output, expand, shrink, full, halves, sems,
 ):
     copies = fetch(
         [(triple_any.at[1], triple), (shrink_any.at[0], shrink), (expand_any.at[0], expand), (output_any.at[0], output)],
@@ -860,25 +883,25 @@
     )
     me, core = scal[0], scal[2]
     dy = qkv_backward(
-        x_ref[...], dm_in[...], mod_ref[1], me, (g0, g1, g2, g3), triple, copies[0], g_hold, full, vec_first,
+        x_ref[...], dm_in[...], mod_ref[...], lambda group: grads[group], triple, copies[0], full, vec_first,
     )
     mlp_backward(
-        dy, mod_ref[0], me, core, m_ref, f_ref, slope_ref, aout_ref, output, expand, shrink,
-        [copies[3], copies[2], copies[1]], o_hold, halves, (d0, d1, d2, d3), dm_ref, vec_ref,
+        dy, mod_low[...], me, core, m_ref, f_ref, slope_ref, aout_ref, output, expand, shrink,
+        [copies[3], copies[2], copies[1]], halves, do_ref, dm_ref, vec_ref,
     )
     mine[...] = halves[core]
     theirs[...] = halves[1 - core]
 
 
 def last_kernel(
-    scal, x_ref, dm_in, mod_ref, g0, g1, g2, g3, triple_any,
+    scal, x_ref, dm_in, mod_ref, grads, triple_any,
     vec_first, input_grad, mask_ref,
-    triple, g_hold, full, sems,
+    triple, full, sems,
 ):
     copies = fetch([(triple_any.at[0], triple)], sems)
     me = scal[0]
     dx = qkv_backward(
-        x_ref[...], dm_in[...], mod_ref[0], me, (g0, g1, g2, g3), triple, copies[0], g_hold, full, vec_first,
+        x_ref[...], dm_in[...], mod_ref[...], lambda group: grads[group], triple, copies[0], full, vec_first,
     )
     rows = dx.shape[0]
     position = me * rows + lax.broadcasted_iota(jnp.int32, dx.shape, 0)
@@ -900,34 +923,55 @@
         v = jnp.zeros((WIDTH // 2, GROUP), F32)
         for place, h_ref in enumerate((h0, h1, h2, h3)):
             h = h_ref[side]
-            qk = qk + dot_nn(h, chunks[place, 0:rows, :])
-            tail = chunks[place, rows : rows + half, :]
+            at = place ^ scal[0]
+            qk = qk + dot_nn(h, chunks[at, 0:rows, :])
+            tail = chunks[at, rows : rows + half, :]
             v = v + dot_nn(h, jnp.concatenate([tail[:, 0:GROUP], tail[:, GROUP : 2 * GROUP]], 0))
         for z in range(4):
             span = slice(z * each, (z + 1) * each)
-            result[side * 4 + z, 0:each, :] = qk[span].astype(BF)
-            result[side * 4 + z, each : each + each // 2, :] = pack_rows(v[span]).astype(BF)
+            block = jnp.concatenate([qk[span], pack_rows(v[span])], 0).astype(BF)
+            tall = block.shape[0]
+            for number in range(3):
+                lanes = slice(number * 128, (number + 1) * 128)
+                result[side * 4 + z, number * tall : (number + 1) * tall, :] = block[:, lanes]
     for place, offset in enumerate((0, 2, 1, 3)):
         at = scal[1] ^ offset
-        mine[place] = result[scal[2] * 4 + at]
-        theirs[place] = result[(1 - scal[2]) * 4 + at]
-
-
-def triple_settle_kernel(
-    scal, keep, core, first, second,
-    b0, b1, b2, b3,
-    hold,
-):
-    each = WIDTH // 8
-    total = keep[0].astype(F32) + core[0].astype(F32) + first[0].astype(F32) + second[0].astype(F32)
-    v = jnp.concatenate([total[each:, 0:GROUP], total[each:, GROUP : 2 * GROUP]], 0)
-    rows = WIDTH // 32
-    for b in range(4):
-        span = slice(b * rows, (b + 1) * rows)
-        hold[b, :, 0 : 2 * GROUP] = total[span]
-        hold[b, :, 2 * GROUP : 3 * GROUP] = v[span]
-    for place, out in enumerate((b0, b1, b2, b3)):
-        out[...] = hold[place ^ scal[0]]
+        tall = result.shape[1]
+        mine[place * tall : (place + 1) * tall, :] = result[scal[2] * 4 + at]
+        theirs[place * tall : (place + 1) * tall, :] = result[(1 - scal[2]) * 4 + at]
+
+
+def bring(layout, pieces, hold, sems):
+    copies = []
+    for number, (piece, source, slot, target, rows) in enumerate(layout):
+        copy = pltpu.make_async_copy(
+            pieces[piece].at[source : source + rows, :], hold.at[slot, target : target + rows, :], sems.at[number]
+        )
+        copy.start()
+        copies.append(copy)
+    for copy in copies:
+        copy.wait()
+
+
+def triple_settle_kernel(layout, scal, *refs):
+    pieces, outs, (hold, blocks, sems) = refs[:-7], refs[-7:-3], refs[-3:]
+    bring(layout, pieces, hold, sems)
+    each, rows = WIDTH // 8, WIDTH // 32
+    tall = each * 3 // 2
+    for layer in range(LAYERS):
+        lanes = []
+        for number in range(3):
+            at = (layer * 3 + number) * tall
+            lanes.append(sum(hold[slot, at : at + tall, :].astype(F32) for slot in range(hold.shape[0])))
+        total = jnp.concatenate(lanes, 1)
+        v = jnp.concatenate([total[each:, 0:GROUP], total[each:, GROUP : 2 * GROUP]], 0)
+        for b in range(4):
+            span = slice(b * rows, (b + 1) * rows)
+            blocks[layer, b, :, 0 : 2 * GROUP] = total[span]
+            blocks[layer, b, :, 2 * GROUP : 3 * GROUP] = v[span]
+    for place, out in enumerate(outs):
+        for layer in range(LAYERS):
+            out[layer] = blocks[layer, place ^ scal[0]]
 
 
 BIT = {"x": 4, "y": 8, "a": 1, "b": 2}
@@ -966,42 +1010,121 @@
             row_at += blocks * rows
 
 
-def settle_kernel(spans, scal, *refs):
-    pieces, (mine, theirs), (hold, sems) = refs[:-4], refs[-4:-2], refs[-2:]
-    sizes = [sum(blocks) for blocks in spans[1]]
-    each = (len(pieces) - 1) // len(sizes)
-    sources = []
-    for part, size in enumerate(sizes):
-        sources += [piece.at[0] for piece in pieces[part * each : (part + 1) * each]]
-        sources.append(pieces[-1].at[0, sum(sizes[:part]) : sum(sizes[: part + 1]), :])
-    each += 1
-    copies = []
-    for number, source in enumerate(sources):
-        copy = pltpu.make_async_copy(source, hold.at[number, 0 : source.shape[0], :], sems.at[number])
-        copy.start()
-        copies.append(copy)
-    for copy in copies:
-        copy.wait()
+def settle_kernel(layout, blocks, scal, *refs):
+    pieces, (mine, theirs, hold, sems) = refs[:-4], refs[-4:]
+    bring(layout, pieces, hold, sems)
     core = scal[2]
+    row = at = 0
+    for rows in blocks:
+        half = rows // 2
+        total = hold[0, row : row + rows, :].astype(F32)
+        for slot in range(1, hold.shape[0]):
+            total = total + hold[slot, row : row + rows, :].astype(F32)
+        low, high = total[0:half], total[half:rows]
+        mine[at : at + half, :] = jnp.where(core == 0, low, high)
+        theirs[at : at + half, :] = jnp.where(core == 0, high, low)
+        row += rows
+        at += half
+
+
+def add_kernel(layout, rows, *refs):
+    outs, (hold, sems) = refs[-2 - len(rows) : -2], refs[-2:]
+    bring(layout, refs[: -2 - len(rows)], hold, sems)
+    depth = {}
+    for _, _, slot, target, count in layout:
+        depth[target] = (max(slot, depth.get(target, (0, 0))[0]), count)
     at = 0
-    for part, blocks in enumerate(spans[1]):
-        row = 0
-        for rows in blocks:
-            half = rows // 2
-            total = hold[part * each, row : row + rows, :].astype(F32)
-            for number in range(1, each):
-                total = total + hold[part * each + number, row : row + rows, :].astype(F32)
-            low, high = total[0:half], total[half:rows]
-            mine[at : at + half, :] = jnp.where(core == 0, low, high)
-            theirs[at : at + half, :] = jnp.where(core == 0, high, low)
-            row += rows
-            at += half
+    for out, size in zip(outs, rows):
+        for target in sorted(depth):
+            if at <= target < at + size:
+                last, count = depth[target]
+                total = sum(hold[slot, target : target + count, :].astype(F32) for slot in range(last + 1))
+                out[target - at : target - at + count, :] = total.astype(BF)
+        at += size
+
+
+def plain_add_kernel(left, right, out):
+    out[...] = left[...] + right[...]
+
+
+DMOD = 12 * WIDTH
+SMALL = 2 * 6912 + WIDTH
+SMALL_AT = {"triple": (0, 2304), "output": (2304, 3072), "expand": (3072, 6144), "shrink": (6144, 6912)}
+
+
+def pack_kernel(first0, vec0, first1, vec1, mask, out):
+    for layer, (first, vec) in enumerate(((first0, vec0), (first1, vec1))):
+        at = layer * 6 * WIDTH
+        out[:, at : at + 1536] = first[:, 0:1536]
+        out[:, at + 1536 : at + 2304] = vec[:, 2304:3072]
+        out[:, at + 2304 : at + 3840] = vec[:, 768:2304]
+        out[:, at + 3840 : at + 4608] = vec[:, 0:768]
+        at = DMOD + layer * 6912
+        out[:, at : at + 2304] = first[:, 1536:3840]
+        out[:, at + 2304 : at + 3072] = vec[:, 6912:7680]
+        out[:, at + 3072 : at + 6144] = vec[:, 3840:6912]
+        out[:, at + 6144 : at + 6912] = vec[:, 3072:3840]
+    out[:, DMOD + 2 * 6912 :] = mask[...]
+
+
+def join_kernel(own, got, condition, adaptive_any, out, condition_grad, adaptive, sems):
+    (copy,) = fetch([(adaptive_any, adaptive)], sems)
+    total = own[...] + got[...]
+    out[:, 0:DMOD] = total[:, 0:DMOD]
+    out[:, DMOD : DMOD + 128] = condition[...]
+    out[:, DMOD + 128 :] = total[:, DMOD:]
+    copy.wait()
+    grad = jnp.zeros((8, 128), F32)
+    for layer in range(LAYERS):
+        at = layer * 6 * WIDTH
+        grad = grad + dot_nt(three_rows(total[:, at : at + 6 * WIDTH]), adaptive[layer])
+    condition_grad[...] = column_sum(grad)
+
+
+def spread_kernel(own, got, out):
+    rows = own.shape[1] - SMALL
+    out[:, 0:rows] = own[:, 0:rows]
+    out[:, rows : 2 * rows] = got[:, 0:rows]
+    out[:, 2 * rows :] = own[:, rows:] + got[:, rows:]
+
+
+def small_kernel(scal, own, got, adaptive_w, adaptive_b, triple_b, output_b, expand_b, shrink_b, mask_sum):
+    index = scal[4]
+    each = DMOD + 128
+    rows = own.shape[1] - SMALL
+    share = adaptive_w.shape[1]
+    number = lax.broadcasted_iota(jnp.int32, (8, 128), 0)
+    lane = lax.broadcasted_iota(jnp.int32, (8, 128), 1)
+    pick = (lane == index * share + number) & (number < share)
+    totals = [jnp.zeros((8, 6 * WIDTH), F32), jnp.zeros((8, 6 * WIDTH), F32)]
+    sums = [jnp.zeros((1, 6 * WIDTH), F32), jnp.zeros((1, 6 * WIDTH), F32)]
+    for source in (own, got):
+        for at in range(0, rows, each):
+            column = jnp.sum(jnp.where(pick, source[:, at + DMOD : at + each], 0.0), 1, keepdims=True)
+            for layer in range(LAYERS):
+                low = at + layer * 6 * WIDTH
+                row = source[:, low : low + 6 * WIDTH]
+                totals[layer] = totals[layer] + column * row
+                sums[layer] = sums[layer] + row
+    summed = own[:, rows:] + got[:, rows:]
+
+    def cut(row):
+        size = row.shape[1] // 32
+        return pltpu.roll(row, lax.rem(row.shape[1] - index * size, row.shape[1]), 1)[:, 0:size]
+
+    for layer in range(LAYERS):
+        adaptive_w[layer] = totals[layer][0:share]
+        adaptive_b[layer : layer + 1, :] = cut(sums[layer])
+        for out, (low, high) in zip((triple_b, output_b, expand_b, shrink_b), SMALL_AT.values()):
+            at = layer * 6912
+            out[layer : layer + 1, :] = cut(summed[:, at + low : at + high])
+    mask_sum[...] = cut(summed[:, 2 * 6912 :])
 
 
 def finish_kernel(plans, scal, *refs):
     pairs = 2 * len(plans)
-    groups = refs[pairs : pairs + 4 * LAYERS]
-    outs, hold = refs[pairs + 4 * LAYERS : -1], refs[-1]
+    groups = refs[pairs : pairs + 4]
+    outs, hold = refs[pairs + 4 : -1], refs[-1]
     core = scal[2]
     for bucket, plan in enumerate(plans):
         mine, got = refs[2 * bucket : 2 * bucket + 2]
@@ -1015,7 +1138,7 @@
             at += rows
     for layer in range(LAYERS):
         for place in range(4):
-            hold[place] = groups[layer * 4 + place][...]
+            hold[place] = groups[place][layer]
         for group in range(4):
             block = hold[group ^ scal[0]]
             for number in range(3):
@@ -1027,23 +1150,43 @@
     return jax.ShapeDtypeStruct(shape, dtype)
 
 
+class Outs(list):
+    token = None
+
+
 def call(kernel, specs, outs, scratch, micros, name, limit, after=()):
     count, extra = len(specs), len(after)
 
     def body(*refs):
-        kernel(*refs[:count], *refs[count + extra :])
+        mark = refs[count + extra + len(outs)]
+        mark[...] = jnp.zeros(mark.shape, F32)
+        kernel(*refs[:count], *refs[count + extra : count + extra + len(outs)], *refs[count + extra + len(outs) + 1 :])
 
     made = pl.pallas_call(
         body,
         in_specs=specs + [ANY] * extra,
-        out_specs=[VM] * len(outs),
-        out_shape=outs,
+        out_specs=[VM] * (len(outs) + 1),
+        out_shape=outs + [shaped(8, 128)],
         scratch_shapes=scratch,
         compiler_params=pltpu.CompilerParams(vmem_limit_bytes=limit * MEBI),
         cost_estimate=pl.CostEstimate(flops=int(micros * 1e9), bytes_accessed=int(micros * 1e6), transcendentals=0),
         name=name,
     )
-    return lambda *operands: made(*operands, *after)
+
+    def run(*operands):
+        operands = [
+            pltpu.with_memory_space_constraint(operand, pltpu.HBM) if spec is HBM or spec is HV else operand
+            for operand, spec in zip(operands, specs)
+        ]
+        marks = [
+            mark if mark.shape == (8, 128) else pltpu.with_memory_space_constraint(mark, pltpu.HBM) for mark in after
+        ]
+        results = made(*operands, *marks)
+        found = Outs(results[:-1])
+        found.token = results[-1]
+        return found
+
+    return run
 
 
 def swap(values, axis, bit):
@@ -1055,69 +1198,148 @@
     return [chunks[0]] + [swap(chunks[place], "blk", place) for place in (1, 2, 3)]
 
 
-class Bucket:
-    def __init__(self, sends, keeps, orders):
-        self.orders = orders
-        self.sent = list(sends)
-        self.held = [[keep, swap(send, *STEP[order[0]])] for keep, send, order in zip(keeps, sends, orders)]
-        self.depth = 1
-        self.size = 8
-
-    def advance(self):
-        half = self.size // 2
-        self.sent = [
-            sum(piece[half : self.size].astype(F32) for piece in held).astype(BF) for held in self.held
-        ]
-        if half == 1:
-            self.sent = [jnp.concatenate(self.sent, 1)]
-            self.last = swap(self.sent[0], *STEP[self.orders[0][-1]])
-        else:
-            for held, out, order in zip(self.held, self.sent, self.orders):
-                held.append(swap(out, *STEP[order[self.depth]]))
-        self.size = half
-        self.depth += 1
-
-
-def weight_bucket(scal, own, far, mine, got, products, orders, after=()):
+def shaped_like(values):
+    return shaped(*values.shape, dtype=values.dtype)
+
+
+class Part:
+    def __init__(self, keep, got, rows, order):
+        self.views = [(keep, 0), (got, 0)]
+        self.rows = rows
+        self.order = order
+
+    def halve(self):
+        self.rows //= 2
+
+
+def exchange(parts, cost, after=()):
+    groups = {}
+    for part in parts:
+        groups.setdefault(part.order[0], []).append(part)
+        part.order = part.order[1:]
+    groups = list(groups.items())
+    ordered, rows = [], []
+    for _, group in groups:
+        for part in group:
+            part.halve()
+        ordered += group
+        rows.append(sum(part.rows for part in group))
+    arrays, layout, total = collect(ordered, True)
+    slots = max(slot for _, _, slot, _, _ in layout) + 1
+    outs = call(
+        functools.partial(add_kernel, layout, rows),
+        [HBM] * len(arrays),
+        [shaped(count, 128, dtype=BF) for count in rows],
+        [pltpu.VMEM((slots, total, 128), BF), pltpu.SemaphoreType.DMA((len(layout),))],
+        cost,
+        "add",
+        16,
+        after,
+    )(*arrays)
+    for (axis, group), out in zip(groups, outs):
+        got = swap(out, *STEP[axis])
+        at = 0
+        for part in group:
+            part.views.append((got, at))
+            at += part.rows
+    return [outs.token]
+
+
+def weight_parts(scal, own, far, mine, got, products, orders, after=()):
     count = len(orders)
-    shapes = []
+    shapes, rows = [], []
     for part in range(count):
-        rows = sum(dealt[part] * (high - low) // 16 for low, high, _, dealt in products)
-        shapes.append(shaped(8, rows, 128, dtype=BF))
+        rows.append(sum(dealt[part] * (high - low) // 16 for low, high, _, dealt in products))
+        shapes.append(shaped(8, rows[-1], 128, dtype=BF))
     outs = call(
         functools.partial(weights_kernel, products, orders),
-        [SM] + [VM] * 4,
+        [SM] + [HV] * 4,
         shapes * 2,
         [pltpu.VMEM((high - low, max(dealt) * 128), BF) for low, high, _, dealt in products],
-        0.1,
+        300,
         "mlp_weights",
-        28,
+        26,
         after,
     )(scal, own, far, mine, got)
-    return Bucket(outs[:count], outs[count:], orders)
-
-
-def settle(bucket, scal, products):
-    count = len(bucket.orders)
-    spans = []
-    for part in range(count):
-        blocks = []
+    flat = [out.reshape(-1, 128) for out in outs]
+    parts = [
+        Part(flat[count + number], swap(flat[number], *STEP[order[0]]), 8 * rows[number], order[1:])
+        for number, order in enumerate(orders)
+    ]
+    return parts, [outs.token]
+
+
+def triple_part(scal, h_rows, stacked, after=()):
+    rows = WIDTH // 8 * 3 // 2 * 3
+    outs = call(
+        triple_kernel,
+        [SM] + [HV] * 5,
+        [shaped(4 * rows, 128, dtype=BF)] * 2,
+        [pltpu.VMEM((8, rows, 128), BF)],
+        300,
+        "triple_weights",
+        20,
+        after,
+    )(scal, *h_rows, stacked)
+    return Part(outs[0], swap(outs[1], "dp", 1), 4 * rows, "ab"), [outs.token]
+
+
+def collect(parts, upper=False):
+    arrays, layout, at = [], [], 0
+    for part in parts:
+        for slot, (array, first) in enumerate(part.views):
+            first = first + part.rows if upper else first
+            known = [number for number, other in enumerate(arrays) if other is array]
+            if not known:
+                arrays.append(array)
+                known = [len(arrays) - 1]
+            layout.append((known[0], first, slot, at, part.rows))
+        at += part.rows
+    return arrays, layout, at
+
+
+def blocks_of(products):
+    blocks = []
+    for part in range(len(products[0][3])):
         for low, high, _, dealt in products:
             blocks += [(high - low) // 16] * dealt[part]
-        spans.append(blocks)
-    rows = sum(sum(blocks) for blocks in spans) // 2
-    pieces = [piece for held in bucket.held for piece in held] + [bucket.last]
-    number = len(pieces) - 1 + count
-    mine, theirs = call(
-        functools.partial(settle_kernel, (bucket.orders, spans)),
-        [SM] + [ANY] * len(pieces),
-        [shaped(rows, 128)] * 2,
-        [pltpu.VMEM((number, max(sum(blocks) for blocks in spans), 128), BF), pltpu.SemaphoreType.DMA((number,))],
-        0.1,
+    return blocks
+
+
+def settle(parts, scal, products, cost, after=()):
+    arrays, layout, rows = collect(parts)
+    slots = max(slot for _, _, slot, _, _ in layout) + 1
+    outs = call(
+        functools.partial(settle_kernel, layout, blocks_of(products)),
+        [SM] + [HBM] * len(arrays),
+        [shaped(rows // 2, 128)] * 2,
+        [pltpu.VMEM((slots, rows, 128), BF), pltpu.SemaphoreType.DMA((len(layout),))],
+        cost,
         "settle",
         10,
-    )(scal, *pieces)
-    return mine, swap(theirs, "dp", 1)
+        after,
+    )(scal, *arrays)
+    return *outs, outs.token
+
+
+def triple_settle(parts, scal, after=()):
+    arrays, layout, rows = collect(parts)
+    slots = max(slot for _, _, slot, _, _ in layout) + 1
+    blocks = call(
+        functools.partial(triple_settle_kernel, layout),
+        [SM] + [HBM] * len(arrays),
+        [shaped(LAYERS, WIDTH // 32, 3 * GROUP)] * 4,
+        [
+            pltpu.VMEM((slots, rows, 128), BF),
+            pltpu.VMEM((LAYERS, 4, WIDTH // 32, 3 * GROUP), F32),
+            pltpu.SemaphoreType.DMA((len(layout),)),
+        ],
+        0.1,
+        "triple_settle",
+        8,
+        after,
+    )(scal, *arrays)
+    return swap_chunks(blocks), [blocks.token]
 
 
 def plan_of(products, names):
@@ -1129,40 +1351,12 @@
     return plan
 
 
-class Triple:
-    def __init__(self, scal, h_rows, stacked, after=()):
-        self.scal = scal
-        shape = (WIDTH // 8 * 3 // 2, 2 * GROUP)
-        keep, theirs = call(
-            triple_kernel,
-            [SM] + [VM] * 5,
-            [shaped(4, *shape, dtype=BF)] * 2,
-            [pltpu.VMEM((8, *shape), BF)],
-            0.1,
-            "triple_weights",
-            20,
-            after,
-        )(scal, *h_rows, stacked)
-        self.sent = [theirs]
-        self.held = [keep, swap(theirs, "dp", 1)]
-        self.steps = [(2, 4, "a"), (1, 2, "b")]
-
-    def advance(self):
-        low, high, name = self.steps.pop(0)
-        self.sent = [sum(piece[low:high].astype(F32) for piece in self.held).astype(BF)]
-        self.held.append(swap(self.sent[0], *STEP[name]))
-
-    def settle(self):
-        blocks = call(
-            triple_settle_kernel,
-            [SM] + [VM] * 4,
-            [shaped(WIDTH // 32, 3 * GROUP)] * 4,
-            [pltpu.VMEM((4, WIDTH // 32, 3 * GROUP), F32)],
-            0.1,
-            "triple_settle",
-            8,
-        )(self.scal, *self.held)
-        return swap_chunks(blocks)
+def rotary_tables(start, rows):
+    position = (start[:, None] + jnp.arange(rows, dtype=jnp.int32)[None, :]).astype(F32)
+    lane = jnp.arange(128, dtype=jnp.int32)
+    frequency = jnp.exp((lane % 32).astype(F32) * (-2.0 * math.log(10000.0) / HEAD_DIM))
+    angles = position[:, :, None] * frequency
+    return jnp.cos(angles), jnp.sin(angles) * jnp.where(lane % 64 < 32, -1.0, 1.0)
 
 
 def local_fast(
@@ -1172,18 +1366,11 @@
     rows = inputs.shape[1]
     hidden = expand_weight.shape[2]
     blk, dp = lax.axis_index("blk"), lax.axis_index("dp")
-    core = dp % 2
-    scal = jnp.stack([blk, dp // 2, core, prefix[0]]).astype(jnp.int32)
-    start = (blk ^ jnp.arange(4, dtype=jnp.int32)) * rows
-    position = (start[:, None] + jnp.arange(rows, dtype=jnp.int32)[None, :]).astype(F32)
-    lane = jnp.arange(128, dtype=jnp.int32)
-    frequency = jnp.exp((lane % 32).astype(F32) * (-2.0 * math.log(10000.0) / HEAD_DIM))
-    angles = position[:, :, None] * frequency
-    cosine = jnp.cos(angles)
-    sine = jnp.sin(angles) * jnp.where(lane % 64 < 32, -1.0, 1.0)
-    biases = jnp.concatenate(
-        [part.astype(F32) for part in (triple_bias, output_bias, expand_bias, shrink_bias)], 1
-    )[:, None, :]
+    scal = jnp.stack([blk, dp // 2, dp % 2, prefix[0], blk * 8 + dp]).astype(jnp.int32)
+    starts = (blk ^ jnp.arange(4, dtype=jnp.int32)) * rows
+    cosine, sine = rotary_tables(starts[:1], rows)
+    cosines, sines = rotary_tables(starts, rows)
+
     f_square = shaped(rows, WIDTH)
     b_square = shaped(rows, WIDTH, dtype=BF)
     b_tall = shaped(rows, hidden, dtype=BF)
@@ -1192,28 +1379,29 @@
     o_chunk = shaped(rows // 2, 2 * GROUP, dtype=BF)
     c_hold = pltpu.VMEM((4, packed, 2 * GROUP), BF)
     o_hold = pltpu.VMEM((4, rows // 2, 2 * GROUP), BF)
+    adaptive_hold = pltpu.VMEM((condition.shape[1], 6 * WIDTH), BF)
     triple_hold = pltpu.VMEM((WIDTH, 3 * WIDTH), BF)
     output_hold = pltpu.VMEM((WIDTH, WIDTH), BF)
     expand_hold = pltpu.VMEM((WIDTH, hidden), BF)
     shrink_hold = pltpu.VMEM((hidden, WIDTH), BF)
-
     h_both = shaped(2, WIDTH // 2, rows, dtype=BF)
     half_width = hidden // 2 + WIDTH
     tall = hidden + 2 * WIDTH
-
-    def far(values):
-        return swap(values, "dp", 1)
-
-    x0, mod, h_rows, c0, c1, c2, c3 = call(
+    mod_row = shaped(1, 6 * WIDTH)
+
+    x0, mod0, h_rows, *chunks = call(
         first_kernel,
-        [SM] + [VM] * 8 + [HBM],
-        [f_square, shaped(LAYERS, 1, 6 * WIDTH), h_both] + [chunk] * 4,
-        [triple_hold, c_hold, pltpu.SemaphoreType.DMA((1,))],
+        [SM] + [VM] * 3 + [HBM] * 6,
+        [f_square, mod_row, h_both] + [chunk] * 4,
+        [
+            pltpu.VMEM(inputs.shape, BF), pltpu.VMEM(condition.shape, F32), pltpu.VMEM(adaptive_bias.shape, BF),
+            pltpu.VMEM(triple_bias.shape, BF), adaptive_hold, triple_hold, c_hold, pltpu.SemaphoreType.DMA((6,)),
+        ],
         300,
         "qkv_first",
         24,
     )(
-        scal, inputs, mask_embed[None], condition, adaptive_weight, adaptive_bias[:, None, :], biases, cosine, sine,
+        scal, mask_embed[None], cosine, sine, inputs, condition, adaptive_bias, triple_bias, adaptive_weight,
         triple_weight,
     )
 
@@ -1221,11 +1409,12 @@
         return call(
             attend_kernel,
             [VM] * 4,
-            [o_chunk] * 4 + [shaped(4, 8, rows), shaped(4, GROUP, rows)],
+            [o_chunk] * 4 + [shaped(4, 8, rows), shaped(4, rows, GROUP)],
             [
+                pltpu.VMEM((4, GROUP, rows), F32),
                 pltpu.VMEM((4, rows, GROUP), BF),
                 pltpu.VMEM((4 * rows, GROUP), BF),
-                pltpu.VMEM((GROUP, 4 * rows), BF),
+                pltpu.VMEM((3, HEAD_DIM + 16, 4 * rows), BF),
             ],
             300,
             "attend",
@@ -1234,11 +1423,15 @@
         )(*chunks)
 
     def attend_back(chunks, given, lse, turned, after):
+        stack = shaped(4, packed, 2 * GROUP, dtype=BF)
         return call(
             attend_back_kernel,
-            [VM] * 12,
-            [chunk] * 4 + [shaped(4, packed, 2 * GROUP, dtype=BF)],
+            [SM, VM] + [HV] * 6 + [HBM] * 2,
+            [stack],
             [
+                pltpu.VMEM((4, rows, 128), F32),
+                pltpu.VMEM((4, rows, 128), F32),
+                pltpu.SemaphoreType.DMA((2,)),
                 pltpu.VMEM((3, 4 * rows, GROUP), BF),
                 pltpu.VMEM((3, 4 * rows, GROUP), BF),
                 pltpu.VMEM((4, rows, GROUP), BF),
@@ -1254,7 +1447,7 @@
             "attend_back",
             24,
             after,
-        )(*chunks, *given, lse, turned, cosine, sine)
+        )(scal, given, *chunks, lse, turned, cosines, sines)
 
     def far(values):
         return swap(values, "dp", 1)
@@ -1263,107 +1456,156 @@
         near = swap(both, "blk", 1)
         return [both, near, swap(both, "blk", 2), swap(near, "blk", 2)]
 
-    chunks0 = swap_chunks([c0, c1, c2, c3])
+    chunks0 = swap_chunks(chunks)
     h_rows0 = gather_rows(h_rows)
     *o_chunks, lse0, ot0 = attend(chunks0, ())
     o_chunks = swap_chunks(o_chunks)
-    aout0, m0, turned0, slope0, f0, x1, h_rows, c0, c1, c2, c3 = call(
+    aout0, m0, turned0, slope0, f0, x1, mod1, h_rows, *chunks = call(
         middle_kernel,
-        [SM] + [VM] * 9 + [HBM] * 4,
-        [b_square, f_square, shaped(tall, rows, dtype=BF), b_tall, b_square, f_square, h_both] + [chunk] * 4,
-        [output_hold, expand_hold, shrink_hold, triple_hold, o_hold, pltpu.VMEM((rows, WIDTH), BF), c_hold]
-        + [pltpu.SemaphoreType.DMA((4,))],
+        [SM] + [HV] + [VM] * 13 + [HBM] * 5,
+        [b_square, f_square, shaped(tall, rows, dtype=BF), b_tall, b_square, f_square, mod_row, h_both] + [chunk] * 4,
+        [output_hold, expand_hold, shrink_hold, triple_hold, adaptive_hold, o_hold, pltpu.VMEM((rows, WIDTH), BF)]
+        + [c_hold, pltpu.SemaphoreType.DMA((5,))],
         300,
         "mlp_qkv",
-        36,
+        34,
         h_rows0[1:3],
-    )(scal, x0, mod, biases, cosine, sine, *o_chunks, output_weight, expand_weight, shrink_weight, triple_weight)
+    )(
+        scal, x0, mod0, condition, adaptive_bias, output_bias, expand_bias, shrink_bias, triple_bias, cosine, sine,
+        *o_chunks, output_weight, expand_weight, shrink_weight, triple_weight, adaptive_weight,
+    )
     turned0_far = far(turned0)
-    chunks1 = swap_chunks([c0, c1, c2, c3])
+    chunks1 = swap_chunks(chunks)
     h_rows1 = gather_rows(h_rows)
-    *o_chunks, lse1, ot1 = attend(chunks1, h_rows0[3:])
+    *o_chunks, lse1, ot1 = attend(chunks1, [*h_rows0[3:], cosines, sines])
     o_chunks = swap_chunks(o_chunks)
     outputs, aout1, m1, turned1, slope1, f1 = call(
         ahead_kernel,
-        [SM] + [VM] * 7 + [HBM] * 3,
+        [SM] + [HV] + [VM] * 8 + [HBM] * 3,
         [shaped(1, rows, WIDTH, dtype=BF), b_square, f_square, shaped(tall, rows, dtype=BF), b_tall, b_square],
         [output_hold, expand_hold, shrink_hold, o_hold, pltpu.VMEM((rows, WIDTH), BF), pltpu.SemaphoreType.DMA((3,))],
         300,
         "mlp_ahead",
-        32,
+        28,
         [*h_rows1[1:3], turned0_far],
-    )(scal, x1, mod, biases, *o_chunks, output_weight, expand_weight, shrink_weight)
+    )(
+        scal, x1, mod1, output_bias, expand_bias, shrink_bias, *o_chunks, output_weight, expand_weight, shrink_weight
+    )
     turned1_far = far(turned1)
-    back_outs = [o_chunk] * 4 + [f_square, shaped(1, 7680)]
-    mine1, theirs1, *given, dm1, vec1 = call(
+    back_outs = [shaped(4, rows // 2, 2 * GROUP, dtype=BF), f_square, shaped(1, 7680)]
+    mine1, theirs1, given, dm1, vec1 = call(
         turn_kernel,
-        [SM] + [VM] * 6 + [HBM] * 3,
+        [SM] + [VM] * 5 + [HBM] * 4,
         [shaped(rows, half_width, dtype=BF)] * 2 + back_outs,
-        [output_hold, expand_hold, shrink_hold, o_hold, pltpu.VMEM((2, rows, half_width), BF)]
-        + [pltpu.SemaphoreType.DMA((3,))],
+        [output_hold, expand_hold, shrink_hold, pltpu.VMEM(cotangent.shape, BF)]
+        + [pltpu.VMEM((2, rows, half_width), BF), pltpu.SemaphoreType.DMA((4,))],
         300,
         "mlp_turn",
-        32,
+        28,
         h_rows1[3:],
-    )(scal, cotangent, mod, m1, f1, slope1, aout1, output_weight, expand_weight, shrink_weight)
-    given = swap_chunks(given)
+    )(scal, mod1, m1, f1, slope1, aout1, cotangent, output_weight, expand_weight, shrink_weight)
+
+    def exchange_blocks(stack):
+        return lax.all_to_all(stack, "blk", 0, 0)
+
     products = (
-        (hidden, hidden + WIDTH, 0, (7, 5)),
-        (0, hidden, hidden // 2, (1, 2)),
-        (hidden + WIDTH, tall, hidden // 2 + WIDTH // 2, (2, 1)),
-    )
-    bucket1 = weight_bucket(scal, turned1, turned1_far, mine1, far(theirs1), products, ("axyb", "yaxb"))
-    *grads, stacked = attend_back(chunks1, given, lse1, ot1, bucket1.sent[:1])
-    grads = swap_chunks(grads)
-    triple1 = Triple(scal, h_rows1, stacked)
-    bucket1.advance()
-    mine0, theirs0, first1, *given, dm0, vec0 = call(
+        (hidden, hidden + WIDTH, 0, (4, 4, 4)),
+        (0, hidden, hidden // 2, (1, 1, 1)),
+        (hidden + WIDTH, tall, hidden // 2 + WIDTH // 2, (1, 1, 1)),
+    )
+    orders = ("axyb", "xyba", "yaxb")
+    given = exchange_blocks(given)
+    parts1, sent = weight_parts(scal, turned1, turned1_far, mine1, far(theirs1), products, orders)
+    outs = attend_back(chunks1, given, lse1, ot1, sent)
+    stacked = outs[0]
+    grads = exchange_blocks(stacked)
+    sent = exchange(parts1, 0.1, [outs.token])
+    triple1, sent = triple_part(scal, h_rows1, stacked, sent)
+    outs = call(
         back_kernel,
-        [SM] + [VM] * 11 + [HBM] * 4,
+        [SM] + [HV] * 2 + [VM] * 3 + [HV] * 4 + [HBM] * 4,
         [shaped(rows, half_width, dtype=BF)] * 2 + [shaped(1, 3840)] + back_outs,
-        [triple_hold, output_hold, expand_hold, shrink_hold, c_hold, pltpu.VMEM((rows, 3 * WIDTH), BF), o_hold]
+        [triple_hold, output_hold, expand_hold, shrink_hold, pltpu.VMEM((rows, 3 * WIDTH), BF)]
         + [pltpu.VMEM((2, rows, half_width), BF), pltpu.SemaphoreType.DMA((4,))],
         300,
         "qkv_mlp_back",
-        36,
-        bucket1.sent + triple1.sent,
+        32,
+        sent,
     )(
-        scal, x1, dm1, mod, *grads, m0, f0, slope0, aout0, triple_weight, output_weight, expand_weight, shrink_weight
-    )
-    given = swap_chunks(given)
-    bucket1.advance()
-    bucket0 = weight_bucket(
-        scal, turned0, turned0_far, mine0, far(theirs0), products, ("ayxb", "xayb")
-    )
-    *grads, stacked = attend_back(chunks0, given, lse0, ot0, bucket0.sent[:1] + bucket1.sent)
-    grads = swap_chunks(grads)
-    triple0 = Triple(scal, h_rows0, stacked)
-    triple1.advance()
-    bucket0.advance()
-    bucket1.advance()
+        scal, x1, dm1, mod1, mod0, grads, m0, f0, slope0, aout0, triple_weight, output_weight, expand_weight,
+        shrink_weight,
+    )
+    mine0, theirs0, first1, given, dm0, vec0 = outs
+    given = exchange_blocks(given)
+    sent = exchange([*parts1, triple1], 300, [outs.token])
+    parts0, sent = weight_parts(scal, turned0, turned0_far, mine0, far(theirs0), products, orders, sent)
+    sent = exchange([*parts1, triple1], 0.1, sent)
+    outs = attend_back(chunks0, given, lse0, ot0, sent)
+    stacked = outs[0]
+    grads = exchange_blocks(stacked)
+    sent = exchange(parts0, 0.1, [outs.token])
+    triple0, sent = triple_part(scal, h_rows0, stacked, sent)
     first0, input_grad, mask_term = call(
         last_kernel,
-        [SM] + [VM] * 7 + [HBM],
+        [SM] + [HV] * 2 + [VM] * 2 + [HBM],
         [shaped(1, 3840), shaped(1, rows, WIDTH), shaped(1, WIDTH)],
-        [triple_hold, c_hold, pltpu.VMEM((rows, 3 * WIDTH), BF), pltpu.SemaphoreType.DMA((1,))],
+        [triple_hold, pltpu.VMEM((rows, 3 * WIDTH), BF), pltpu.SemaphoreType.DMA((1,))],
         300,
         "qkv_back",
         24,
-        [*triple0.sent, *triple1.sent, *bucket0.sent, *bucket1.sent],
-    )(scal, x0, dm0, mod, *grads, triple_weight)
-    triple0.advance()
-    triple0.advance()
-    bucket0.advance()
-    bucket0.advance()
-    triple1.advance()
-    parts = [*settle(bucket1, scal, products), *settle(bucket0, scal, products)]
+        sent,
+    )(scal, x0, dm0, mod0, grads, triple_weight)
+
+    def spread(own, got, cost, after=()):
+        wide = shaped(1, 2 * own.shape[1] - SMALL)
+        return call(spread_kernel, [VM] * 2, [wide], [], cost, "spread", 8, after)(own, got)
+
+    outs = call(pack_kernel, [VM] * 5, [shaped(1, DMOD + SMALL)], [], 0.1, "pack", 8)(
+        first0, vec0, first1, vec1, mask_term
+    )
+    small = outs[0]
+    near = swap(small, "blk", 1)
+    sent = exchange([*parts0, triple0], 300, [outs.token])
+    (summed,) = call(plain_add_kernel, [VM] * 2, [shaped_like(small)], [], 300, "plain_add", 8, sent)(small, near)
+    outs = call(
+        join_kernel,
+        [VM] * 3 + [HBM],
+        [shaped(1, DMOD + 128 + SMALL), shaped(1, 128)],
+        [pltpu.VMEM(adaptive_weight.shape, BF), pltpu.SemaphoreType.DMA((1,))],
+        0.1,
+        "join",
+        12,
+    )(summed, swap(summed, "blk", 2), condition, adaptive_weight)
+    wide, condition_grad = outs
+    got = far(wide)
+    sent = exchange([*parts0, triple0], 300, [outs.token])
+    (wide,) = spread(wide, got, 300, sent)
+    outs = spread(wide, swap(wide, *STEP["a"]), 0.1)
+    wide = outs[0]
+    got = swap(wide, *STEP["b"])
+    blocks, cut = triple_settle([triple0, triple1], scal, [outs.token])
+    outs = call(
+        small_kernel,
+        [SM] + [VM] * 2,
+        [shaped(LAYERS, condition.shape[1] // 32, 6 * WIDTH), shaped(LAYERS, 6 * WIDTH // 32)]
+        + [shaped(LAYERS, (high - low) // 32) for low, high in SMALL_AT.values()]
+        + [shaped(1, WIDTH // 32)],
+        [],
+        300,
+        "small",
+        10,
+        cut,
+    )(scal, wide, got)
+    small_grads = list(outs)
+    own1, theirs1, early = settle(parts1, scal, products, 0.1, cut)
+    own0, theirs0, _ = settle(parts0, scal, products, 0.1, [early, outs.token, *blocks[1:]])
     plans = (
         plan_of(products, ((2, 1), (3, 1), (1, 1))),
         plan_of(products, ((2, 0), (3, 0), (1, 0))),
     )
     weight_grads = call(
         functools.partial(finish_kernel, plans),
-        [SM] + [VM] * 12,
+        [SM] + [VM] * 8,
         [
             shaped(LAYERS, WIDTH // 32, 3 * WIDTH),
             shaped(LAYERS, WIDTH // 32, WIDTH),
@@ -1374,65 +1616,22 @@
         0.1,
         "finish",
         12,
-    )(scal, *parts, *triple0.settle(), *triple1.settle())
-
-    small = jnp.concatenate([first0, vec0, first1, vec1, mask_term], 1)
-    small = small + swap(small, "blk", 1)
-    small = small + swap(small, "blk", 2)
-    dmods, sums = [], []
-    for layer in range(LAYERS):
-        first = small[:, layer * 11520 : layer * 11520 + 3840]
-        vec = small[:, layer * 11520 + 3840 : (layer + 1) * 11520]
-        dmods += [first[:, 0:1536], vec[:, 2304:3072], vec[:, 768:2304], vec[:, 0:768]]
-        sums += [first[:, 1536:3840], vec[:, 6912:7680], vec[:, 3840:6912], vec[:, 3072:3840]]
-    dmod = jnp.concatenate(dmods, 1)
-    gathered = jnp.concatenate([dmod, condition], 1)
-    total = jnp.concatenate(sums + [small[:, 2 * 11520 :]], 1)
-    condition_grad = sum(
-        lax.dot_general(
-            dmod[:, layer * 6 * WIDTH : (layer + 1) * 6 * WIDTH],
-            adaptive_weight[layer].astype(F32),
-            (((1,), (1,)), ((), ())),
-            precision=HIGHEST,
-        )
-        for layer in range(LAYERS)
-    )
-    for bit in (1, 2, 4):
-        gathered = jnp.concatenate([gathered, swap(gathered, "dp", bit)], 0)
-        total = total + swap(total, "dp", bit)
-    index = blk * 8 + dp
-    share_rows = condition.shape[1] // 32
-    near = lax.dynamic_slice_in_dim(gathered[:, 12 * WIDTH :], index * share_rows, share_rows, 1)
-    gathered = gathered[:, : 12 * WIDTH]
-    adaptive_w = jnp.sum(near[:, :, None] * gathered[:, None, :], 0)
-    adaptive_w = jnp.stack([adaptive_w[:, : 6 * WIDTH], adaptive_w[:, 6 * WIDTH :]], 0)
-    adaptive_all = jnp.sum(gathered, 0)
-
-    def cut(values):
-        size = values.shape[0] // 32
-        return lax.dynamic_slice_in_dim(values, index * size, size, 0)
-
-    adaptive_b = jnp.stack([cut(adaptive_all[: 6 * WIDTH]), cut(adaptive_all[6 * WIDTH :])], 0)
-    total = total[0]
-    bias_grads = []
-    for low, high in BIAS_AT.values():
-        bias_grads.append(jnp.stack([cut(total[low:high]), cut(total[6912 + low : 6912 + high])], 0))
-    mask_sum = cut(total[2 * 6912 :])
+    )(scal, own1, far(theirs1), own0, far(theirs0), *blocks)
     return (
         outputs,
         input_grad,
         condition_grad,
-        mask_sum,
-        adaptive_w,
-        adaptive_b,
+        small_grads[6][0],
+        small_grads[0],
+        small_grads[1],
         weight_grads[0],
-        bias_grads[0],
+        small_grads[2],
         weight_grads[1],
-        bias_grads[1],
+        small_grads[3],
         weight_grads[2],
-        bias_grads[2],
+        small_grads[4],
         weight_grads[3],
-        bias_grads[3],
+        small_grads[5],
     )
 
 

time: 362 us -> 352 us (0.972)
  Pallas kernels: 119 us -> 169 us
  other arithmetic: 36.5 us -> 3.7 us
  waiting for transfers between devices: 103 us -> 79.4 us
    pallas_call x19 -> x30, Pallas kernels: 119 us -> 169 us  [run(): results = made(*operands, *marks)]
    ppermute x70 -> x58, waiting for transfers between devices: 103 us -> 75.6 us  [swap(): return lax.ppermute(values, axis, [(i, i ^ bit) for i in range(size)])]
    convert_element_type x17 -> x2, other arithmetic: 24.6 us -> 0.11 us  [rotary_tables(): (start[:, None] + jnp.arange(rows, dtype=jnp.int32)[None, :]).astype(F32)]
    all_to_all x0 -> x4, starting transfers between devices: none -> 17 us  [exchange_blocks(): return lax.all_to_all(stack, 'blk', 0, 0)]
    ppermute x70 -> x58, starting transfers between devices: 75 us -> 58.7 us  [swap(): return lax.ppermute(values, axis, [(i, i ^ bit) for i in range(size)])]
    unnamed x171 -> x100, local copies, waits for them, and re-layouts: 12.3 us -> 16.2 us
    all_to_all x0 -> x4, waiting for transfers between devices: none -> 3.74 us  [exchange_blocks(): return lax.all_to_all(stack, 'blk', 0, 0)]
    another operation x7 -> x0, other arithmetic: 3.64 us -> none  [the longest x4 2.28 us: local_fast(): jnp.stack([cut(total[low:high]), cut(total[6912 + low:6912 + high])], 0)]
  transfers between devices with their start and end apart: 70 -> 62, of which waited for: 25 -> 22; matrix products, arithmetic and copies ran while one was open for 11% -> 1% of each run, Pallas kernels for 32% -> 43%
where the time goes in v3:
time: 352 us; the launch traced here: 347 us
  Pallas kernels  169 us (48%)
  waiting for transfers between devices  79.4 us (23%)
  starting transfers between devices  75.7 us (22%)
  local copies, waits for them, and re-layouts  17 us (5%)
  other arithmetic  3.7 us (1%)
    pallas_call x30, Pallas kernels, run(): results = made(*operands, *marks)  169 us
    ppermute x58, waiting for transfers between devices, swap(): return lax.ppermute(values, axis, [(i, i ^ bit) for i in range(size)])  75.6 us
    ppermute x58, starting transfers between devices, swap(): return lax.ppermute(values, axis, [(i, i ^ bit) for i in range(size)])  58.7 us
    all_to_all x4, starting transfers between devices, exchange_blocks(): return lax.all_to_all(stack, 'blk', 0, 0)  17 us
    unnamed x100, local copies, waits for them, and re-layouts  16.2 us
  transfers between devices with their start and end apart: 62, of which 22 were waited for; matrix products, arithmetic and copies ran while one was open for 1% of the time, Pallas kernels for 43%

profile of v3, /device:TPU:0, one launch (start us, length us, event | category | flops | bytes accessed | tf_op | source)
XLA Modules:
  0.0 346.7 jit_solution(9460159301795638504)
XLA Ops:
  2.8 6.0 %qkv_first.1 = (f32[256,768]{1,0:T(8,128)S(1)}, f32[1,4608]{1,0:T(1,128)S(1)}, bf16[2,384,256]{2,1,0:T(8,128)(2,1)}, bf16[384,384]{1,0:T(8,128)(2,1)S(1)}, bf16[...) custom-call(s32[5]{0:T(128)S(1)} %stack.19.refs_0_, ...), custom_call_target="tpu_custom_call" | custom-call | flops 299999985664 | bytes 300000000 | tf_op jit(solution)/shard_map/qkv_first/pallas_call | solution.py:1184
  8.8 3.0 collective-permute-start
  13.3 2.0 collective-permute-start.7
  16.8 2.8 collective-permute-done.refs_1_.refs_3_
  19.6 8.4 %collective-permute-done.1.refs_2_.refs_4_ = bf16[384,384]{1,0:T(8,128)(2,1)S(1)} collective-permute-done((bf16[384,384]{1,0:T(8,128)(2,1)S(1)}, bf16[384,384]{1,0:T(8,128)(2,1)S(1)}, u32[]{:S(2)}, u32[]{:S(2)}) %collective-permute-start.1) | collective-permute-done | bytes 294944 | tf_op jit(solution)/shard_map/ppermute | solution.py:1194
  28.1 6.6 %attend.2 = (bf16[128,384]{1,0:T(8,128)(2,1)S(1)}, bf16[128,384]{1,0:T(8,128)(2,1)S(1)}, bf16[128,384]{1,0:T(8,128)(2,1)S(1)}, bf16[128,384]{1,0:T(8,128)(2,1)S(...) custom-call(bf16[384,384]{1,0:T(8,128)(2,1)S(1)} %get-tuple-element.147.refs_0_.refs_2_, ...), custom_call_target="tpu_custom_call" | custom-call | flops 299999985664 | bytes 300000000 | tf_op jit(solution)/shard_map/attend/pallas_call | solution.py:1184
  41.9 2.0 collective-permute-done.5.refs_14_
  44.0 11.6 %mlp_qkv.1 = (bf16[256,768]{1,0:T(8,128)(2,1)S(1)}, f32[256,768]{1,0:T(8,128)S(1)}, bf16[4608,256]{1,0:T(8,128)(2,1)}, bf16[256,3072]{1,0:T(8,128)(2,1)S(1)}, bf...) custom-call(s32[5]{0:T(128)S(1)} %stack.19.refs_0_, ...), custom_call_target="tpu_custom_call" | custom-call | flops 299999985664 | bytes 300000000 | tf_op jit(solution)/shard_map/mlp_qkv/pallas_call | solution.py:1184
  60.2 3.0 fusion
  66.0 4.1 %collective-permute-done.9.refs_2_.refs_4_ = bf16[384,384]{1,0:T(8,128)(2,1)S(1)} collective-permute-done((bf16[384,384]{1,0:T(8,128)(2,1)S(1)}, bf16[384,384]{1,0:T(8,128)(2,1)S(1)}, u32[]{:S(2)}, u32[]{:S(2)}) %collective-permute-start.9) | collective-permute-done | bytes 294944 | tf_op jit(solution)/shard_map/ppermute | solution.py:1194
  71.8 7.6 %collective-permute-done.11.refs_4_ = bf16[2,384,256]{2,1,0:T(8,128)(2,1)S(1)} collective-permute-done((bf16[2,384,256]{2,1,0:T(8,128)(2,1)}, bf16[2,384,256]{2,1,0:T(8,128)(2,1)S(1)}, u32[]{:S(2)}, u32[]{:S(2)}) %collective-permute-start.11) | collective-permute-done | bytes 393248 | tf_op jit(solution)/shard_map/ppermute | solution.py:1194
  80.2 6.6 %attend.3 = (bf16[128,384]{1,0:T(8,128)(2,1)S(1)}, bf16[128,384]{1,0:T(8,128)(2,1)S(1)}, bf16[128,384]{1,0:T(8,128)(2,1)S(1)}, bf16[128,384]{1,0:T(8,128)(2,1)S(...) custom-call(bf16[384,384]{1,0:T(8,128)(2,1)S(1)} %get-tuple-element.158.refs_0_.refs_2_, ...), custom_call_target="tpu_custom_call" | custom-call | flops 299999985664 | bytes 300000000 | tf_op jit(solution)/shard_map/attend/pallas_call | solution.py:1184
  89.4 2.6 collective-permute-start.14
  95.0 10.1 %mlp_ahead.1 = (bf16[1,256,768]{2,1,0:T(8,128)(2,1)}, bf16[256,768]{1,0:T(8,128)(2,1)S(1)}, f32[256,768]{1,0:T(8,128)S(1)}, bf16[4608,256]{1,0:T(8,128)(2,1)}, b...) custom-call(s32[5]{0:T(128)S(1)} %stack.19.refs_0_, f32[256,768]{1,0:T(8,128)} %copy-done.27, ...), custom_call_target="tpu_custom_call" | custom-call | flops 299999985664 | bytes 300000000 | tf_op jit(solution)/shard_map/mlp_ahead/pallas_call | solution.py:1184
  105.3 20.7 %mlp_turn.1 = (bf16[256,2304]{1,0:T(8,128)(2,1)S(1)}, bf16[256,2304]{1,0:T(8,128)(2,1)S(1)}, bf16[4,128,384]{2,1,0:T(8,128)(2,1)}, f32[256,768]{1,0:T(8,128)S(1)...) custom-call(s32[5]{0:T(128)S(1)} %stack.19.refs_0_, f32[1,4608]{1,0:T(1,128)S(1)} %get-tuple-element.157.refs_2_.refs_1_.refs_3_, ...), custom_call_target="tpu_custom_call" | custom-call | flops 299999985664 | bytes 300000000 | tf_op jit(solution)/shard_map/mlp_turn/pallas_call | solution.py:1184
  128.4 4.1 %all-to-all-start = ((bf16[4,128,384]{2,1,0:T(8,128)(2,1)}), bf16[4,128,384]{2,1,0:T(8,128)(2,1)}, u32[]{:S(2)}, u32[]{:S(2)}) async-start(bf16[4,128,384]{2,1,0:T(8,128)(2,1)} %get-tuple-element.174), calls=%async_computation | async-start | bytes 786432 | tf_op jit(solution)/shard_map/all_to_all | solution.py:1509
  133.5 9.2 %mlp_weights.2 = (bf16[8,432,128]{2,1,0:T(8,128)(2,1)}, bf16[8,432,128]{2,1,0:T(8,128)(2,1)}, bf16[8,432,128]{2,1,0:T(8,128)(2,1)}, bf16[8,432,128]{2,1,0:T(8,12...) custom-call(s32[5]{0:T(128)S(1)} %stack.19.refs_0_, ...), custom_call_target="tpu_custom_call" | custom-call | flops 299999985664 | bytes 300000000 | tf_op jit(solution)/shard_map/mlp_weights/pallas_call | solution.py:1184
  150.7 13.3 %attend_back.2 = (bf16[4,384,384]{2,1,0:T(8,128)(2,1)}, f32[8,128]{1,0:T(8,128)S(1)}) custom-call(s32[5]{0:T(128)S(1)} %stack.19.refs_0_, bf16[4,128,384]{2,1,0:T(8,128)(2,1)} %all-to-all-done.refs_1_, bf16[384,384]{1,0:T(8,128)(2,1)} %copy-done.33, bf16[384,384]{1,0:T(8,128)(2,1)} %copy-done.13, bf16[384,384]{1,0:T(8,128)(2,1)} %copy-done.14, ...), custom_call_target="tpu_custom_call" | custom-call | flops 299999985664 | bytes 300000000 | tf_op jit(solution)/shard_map/attend_back/pallas_call | solution.py:1184
  163.9 4.3 %all-to-all-start.1 = ((bf16[4,384,384]{2,1,0:T(8,128)(2,1)}), bf16[4,384,384]{2,1,0:T(8,128)(2,1)}, u32[]{:S(2)}, u32[]{:S(2)}) async-start(bf16[4,384,384]{2,1,0:T(8,128)(2,1)} %get-tuple-element.181.refs_5_), calls=%async_computation.1 | async-start | bytes 2359296 | tf_op jit(solution)/shard_map/all_to_all | solution.py:1509
  168.8 7.0 %collective-permute-done.23.refs_5_.refs_7_.refs_12_ = bf16[3456,128]{1,0:T(8,128)(2,1)} collective-permute-done((bf16[3456,128]{1,0:T(8,128)(2,1)}, bf16[3456,128]{1,0:T(8,128)(2,1)}, u32[]{:S(2)}, u32[]{:S(2)}) %collective-permute-start.23) | collective-permute-done | bytes 884768 | tf_op jit(solution)/shard_map/ppermute | solution.py:1194
  175.8 2.9 add.96
  178.7 4.1 %triple_weights.2 = (bf16[1728,128]{1,0:T(8,128)(2,1)S(1)}, bf16[1728,128]{1,0:T(8,128)(2,1)}, f32[8,128]{1,0:T(8,128)S(1)}) custom-call(s32[5]{0:T(128)S(1)} %stack.19.refs_0_, bf16[2,384,256]{2,1,0:T(8,128)(2,1)} %get-tuple-element.166.refs_1_, bf16[2,384,256]{2,1,0:T(8,128)(2,1)} %collective-permute-done.15.refs_13_.refs_2_, ...), custom_call_target="tpu_custom_call" | custom-call | flops 299999985664 | bytes 300000000 | tf_op jit(solution)/shard_map/triple_weights/pallas_call | solution.py:1184
  183.7 3.0 collective-permute-start.25
  187.0 12.4 %qkv_mlp_back.1 = (bf16[256,2304]{1,0:T(8,128)(2,1)S(1)}, bf16[256,2304]{1,0:T(8,128)(2,1)}, f32[1,3840]{1,0:T(1,128)S(1)}, bf16[4,128,384]{2,1,0:T(8,128)(2,1)}...) custom-call(s32[5]{0:T(128)S(1)} %stack.19.refs_0_, f32[256,768]{1,0:T(8,128)} %copy-done.27, ...), custom_call_target="tpu_custom_call" | custom-call | flops 299999985664 | bytes 300000000 | tf_op jit(solution)/shard_map/qkv_mlp_back/pallas_call | solution.py:1184
  201.3 4.3 %all-to-all-start.2 = ((bf16[4,128,384]{2,1,0:T(8,128)(2,1)}), bf16[4,128,384]{2,1,0:T(8,128)(2,1)}, u32[]{:S(2)}, u32[]{:S(2)}) async-start(bf16[4,128,384]{2,1,0:T(8,128)(2,1)} %get-tuple-element.196), calls=%async_computation.2 | async-start | bytes 786432 | tf_op jit(solution)/shard_map/all_to_all | solution.py:1509
  205.7 2.8 add.97
  208.5 2.0 collective-permute-start.28
  213.7 2.6 collective-permute-start.31
  216.3 9.2 %mlp_weights.3 = (bf16[8,432,128]{2,1,0:T(8,128)(2,1)}, bf16[8,432,128]{2,1,0:T(8,128)(2,1)}, bf16[8,432,128]{2,1,0:T(8,128)(2,1)}, bf16[8,432,128]{2,1,0:T(8,12...) custom-call(s32[5]{0:T(128)S(1)} %stack.19.refs_0_, ...), custom_call_target="tpu_custom_call" | custom-call | flops 299999985664 | bytes 300000000 | tf_op jit(solution)/shard_map/mlp_weights/pallas_call | solution.py:1184
  229.3 2.5 add.98
  231.8 13.1 %attend_back.3 = (bf16[4,384,384]{2,1,0:T(8,128)(2,1)}, f32[8,128]{1,0:T(8,128)S(1)}) custom-call(s32[5]{0:T(128)S(1)} %stack.19.refs_0_, bf16[4,128,384]{2,1,0:T(8,128)(2,1)} %all-to-all-done.2.refs_1_, bf16[384,384]{1,0:T(8,128)(2,1)} %copy-done.34, bf16[384,384]{1,0:T(8,128)(2,1)} %copy-done.10, bf16[384,384]{1,0:T(8,128)(2,1)} %copy-done.11, ...), custom_call_target="tpu_custom_call" | custom-call | flops 299999985664 | bytes 300000000 | tf_op jit(solution)/shard_map/attend_back/pallas_call | solution.py:1184
  245.0 4.3 %all-to-all-start.3 = ((bf16[4,384,384]{2,1,0:T(8,128)(2,1)}), bf16[4,384,384]{2,1,0:T(8,128)(2,1)}, u32[]{:S(2)}, u32[]{:S(2)}) async-start(bf16[4,384,384]{2,1,0:T(8,128)(2,1)} %get-tuple-element.214.refs_5_), calls=%async_computation.3 | async-start | bytes 2359296 | tf_op jit(solution)/shard_map/all_to_all | solution.py:1509
  249.9 2.9 add.99
  252.8 4.0 %triple_weights.3 = (bf16[1728,128]{1,0:T(8,128)(2,1)S(1)}, bf16[1728,128]{1,0:T(8,128)(2,1)}, f32[8,128]{1,0:T(8,128)S(1)}) custom-call(s32[5]{0:T(128)S(1)} %stack.19.refs_0_, bf16[2,384,256]{2,1,0:T(8,128)(2,1)} %get-tuple-element.155.refs_1_, bf16[2,384,256]{2,1,0:T(8,128)(2,1)} %collective-permute-done.6.refs_20_.refs_2_, ...), custom_call_target="tpu_custom_call" | custom-call | flops 299999985664 | bytes 300000000 | tf_op jit(solution)/shard_map/triple_weights/pallas_call | solution.py:1184
  262.1 3.7 %all-to-all-done.3.refs_4_ = bf16[4,384,384]{2,1,0:T(8,128)(2,1)} async-done(((bf16[4,384,384]{2,1,0:T(8,128)(2,1)}), bf16[4,384,384]{2,1,0:T(8,128)(2,1)}, u32[]{:S(2)}, u32[]{:S(2)}) %all-to-all-start.3) | async-done | bytes 1179680 | tf_op jit(solution)/shard_map/all_to_all | solution.py:1509
  265.8 6.1 %qkv_back.1 = (f32[1,3840]{1,0:T(1,128)S(1)}, f32[1,256,768]{2,1,0:T(8,128)}, f32[1,768]{1,0:T(1,128)S(1)}, f32[8,128]{1,0:T(8,128)}) custom-call(s32[5]{0:T(128)S(1)} %stack.19.refs_0_, f32[256,768]{1,0:T(8,128)} %copy-done.30, f32[256,768]{1,0:T(8,128)} %copy-done.28, f32[1,4608]{1,0:T(1,128)S(1)} %copy-done.38, ...), custom_call_target="tpu_custom_call" | custom-call | flops 299999985664 | bytes 300000000 | tf_op jit(solution)/shard_map/qkv_back/pallas_call | solution.py:1184
  273.8 2.8 add.100
  283.1 4.0 %collective-permute-done.41.refs_1_ = f32[1,23808]{1,0:T(1,128)S(1)} collective-permute-done((f32[1,23808]{1,0:T(1,128)S(1)}, f32[1,23808]{1,0:T(1,128)S(1)}, u32[]{:S(2)}, u32[]{:S(2)}) %collective-permute-start.41) | collective-permute-done | bytes 95264 | tf_op jit(solution)/shard_map/ppermute | solution.py:1194
  287.1 2.6 collective-permute-start.50
  289.7 2.9 join.1
  292.7 14.7 %collective-permute-done.46.refs_14_.refs_9_ = bf16[864,128]{1,0:T(8,128)(2,1)} collective-permute-done((bf16[864,128]{1,0:T(8,128)(2,1)}, bf16[864,128]{1,0:T(8,128)(2,1)}, u32[]{:S(2)}, u32[]{:S(2)}) %collective-permute-start.46) | collective-permute-done | bytes 221216 | tf_op jit(solution)/shard_map/ppermute | solution.py:1194
  307.4 2.5 add.101
  311.6 14.6 %collective-permute-done.47.refs_1_ = f32[1,33280]{1,0:T(1,128)S(1)} collective-permute-done((f32[1,33280]{1,0:T(1,128)S(1)}, f32[1,33280]{1,0:T(1,128)S(1)}, u32[]{:S(2)}, u32[]{:S(2)}) %collective-permute-start.47) | collective-permute-done | bytes 133152 | tf_op jit(solution)/shard_map/ppermute | solution.py:1194
  326.3 2.0 collective-permute-start.53
  328.4 2.7 triple_settle.1
  334.6 3.1 settle.2
  339.4 2.7 settle.3
  344.0 2.4 finish.1
  (214 shorter events, 72.2 us)
Async XLA Ops:
  8.8 10.8 %collective-permute-start = (bf16[384,384]{1,0:T(8,128)(2,1)S(1)}, bf16[384,384]{1,0:T(8,128)(2,1)S(1)}, u32[]{:S(2)}, u32[]{:S(2)}) collective-permute-start(bf16[384,384]{1,0:T(8,128)(2,1)S(1)} %get-tuple-element.148), channel_id=1, source_target_pairs={{0,8},{8,0},{16,24},{24,16},{1,9},{9,1},{17,25},{25,17},{2,10},{10... | collective-permute-start | bytes 884744 | tf_op jit(solution)/shard_map/ppermute | solution.py:1194
  11.8 16.3 %collective-permute-start.1 = (bf16[384,384]{1,0:T(8,128)(2,1)S(1)}, bf16[384,384]{1,0:T(8,128)(2,1)S(1)}, u32[]{:S(2)}, u32[]{:S(2)}) collective-permute-start(bf16[384,384]{1,0:T(8,128)(2,1)S(1)} %get-tuple-element.149), channel_id=1, source_target_pairs={{0,16},{8,24},{16,0},{24,8},{1,17},{9,25},{17,1},{25,9},{2,18},{10... | collective-permute-start | bytes 884744 | tf_op jit(solution)/shard_map/ppermute | solution.py:1194
  13.3 14.7 %collective-permute-start.2 = (bf16[384,384]{1,0:T(8,128)(2,1)S(1)}, bf16[384,384]{1,0:T(8,128)(2,1)S(1)}, u32[]{:S(2)}, u32[]{:S(2)}) collective-permute-start(bf16[384,384]{1,0:T(8,128)(2,1)S(1)} %get-tuple-element.150), channel_id=1, source_target_pairs={{0,24},{8,16},{16,8},{24,0},{1,25},{9,17},{17,9},{25,1},{2,26},{10... | collective-permute-start | bytes 884744 | tf_op jit(solution)/shard_map/ppermute | solution.py:1194
  13.3 26.5 %collective-permute-start.7 = (bf16[2,384,256]{2,1,0:T(8,128)(2,1)}, bf16[2,384,256]{2,1,0:T(8,128)(2,1)}, u32[]{:S(2)}, u32[]{:S(2)}) collective-permute-start(bf16[2,384,256]{2,1,0:T(8,128)(2,1)} %get-tuple-element.155.refs_1_), channel_id=1, source_target_pairs={{0,16},{8,24},{16,0},{24,8},{1,17},{9,25},{17,1},{25,9},{2,18},{10... | collective-permute-start | bytes 1179656 | tf_op jit(solution)/shard_map/ppermute | solution.py:1194
  15.3 24.5 %collective-permute-start.6 = (bf16[2,384,256]{2,1,0:T(8,128)(2,1)}, bf16[2,384,256]{2,1,0:T(8,128)(2,1)}, u32[]{:S(2)}, u32[]{:S(2)}) collective-permute-start(bf16[2,384,256]{2,1,0:T(8,128)(2,1)} %get-tuple-element.155.refs_1_), channel_id=1, source_target_pairs={{0,8},{8,0},{16,24},{24,16},{1,9},{9,1},{17,25},{25,17},{2,10},{10... | collective-permute-start | bytes 1179656 | tf_op jit(solution)/shard_map/ppermute | solution.py:1194
  55.7 9.6 %collective-permute-start.8 = (bf16[384,384]{1,0:T(8,128)(2,1)S(1)}, bf16[384,384]{1,0:T(8,128)(2,1)S(1)}, u32[]{:S(2)}, u32[]{:S(2)}) collective-permute-start(bf16[384,384]{1,0:T(8,128)(2,1)S(1)} %get-tuple-element.159), channel_id=1, source_target_pairs={{0,8},{8,0},{16,24},{24,16},{1,9},{9,1},{17,25},{25,17},{2,10},{10... | collective-permute-start | bytes 884744 | tf_op jit(solution)/shard_map/ppermute | solution.py:1194
  57.3 12.9 %collective-permute-start.9 = (bf16[384,384]{1,0:T(8,128)(2,1)S(1)}, bf16[384,384]{1,0:T(8,128)(2,1)S(1)}, u32[]{:S(2)}, u32[]{:S(2)}) collective-permute-start(bf16[384,384]{1,0:T(8,128)(2,1)S(1)} %get-tuple-element.160), channel_id=1, source_target_pairs={{0,16},{8,24},{16,0},{24,8},{1,17},{9,25},{17,1},{25,9},{2,18},{10... | collective-permute-start | bytes 884744 | tf_op jit(solution)/shard_map/ppermute | solution.py:1194
  57.8 14.1 %collective-permute-start.10 = (bf16[384,384]{1,0:T(8,128)(2,1)S(1)}, bf16[384,384]{1,0:T(8,128)(2,1)S(1)}, u32[]{:S(2)}, u32[]{:S(2)}) collective-permute-start(bf16[384,384]{1,0:T(8,128)(2,1)S(1)} %get-tuple-element.161), channel_id=1, source_target_pairs={{0,24},{8,16},{16,8},{24,0},{1,25},{9,17},{17,9},{25,1},{2,26},{10... | collective-permute-start | bytes 884744 | tf_op jit(solution)/shard_map/ppermute | solution.py:1194
  59.3 20.2 %collective-permute-start.11 = (bf16[2,384,256]{2,1,0:T(8,128)(2,1)}, bf16[2,384,256]{2,1,0:T(8,128)(2,1)S(1)}, u32[]{:S(2)}, u32[]{:S(2)}) collective-permute-start(bf16[2,384,256]{2,1,0:T(8,128)(2,1)} %collective-permute-done.6.refs_20_.refs_2_), channel_id=1, source_target_pairs={{0,16},{8,24},{16,0},{24,8},{1,17},{9,25},{17,1},{25,9},{2,18},{10... | collective-permute-start | bytes 1179656 | tf_op jit(solution)/shard_map/ppermute | solution.py:1194
  63.3 26.1 %collective-permute-start.16 = (bf16[2,384,256]{2,1,0:T(8,128)(2,1)}, bf16[2,384,256]{2,1,0:T(8,128)(2,1)}, u32[]{:S(2)}, u32[]{:S(2)}) collective-permute-start(bf16[2,384,256]{2,1,0:T(8,128)(2,1)} %get-tuple-element.166.refs_1_), channel_id=1, source_target_pairs={{0,16},{8,24},{16,0},{24,8},{1,17},{9,25},{17,1},{25,9},{2,18},{10... | collective-permute-start | bytes 1179656 | tf_op jit(solution)/shard_map/ppermute | solution.py:1194
  65.4 26.6 %collective-permute-start.15 = (bf16[2,384,256]{2,1,0:T(8,128)(2,1)}, bf16[2,384,256]{2,1,0:T(8,128)(2,1)}, u32[]{:S(2)}, u32[]{:S(2)}) collective-permute-start(bf16[2,384,256]{2,1,0:T(8,128)(2,1)} %get-tuple-element.166.refs_1_), channel_id=1, source_target_pairs={{0,8},{8,0},{16,24},{24,16},{1,9},{9,1},{17,25},{25,17},{2,10},{10... | collective-permute-start | bytes 1179656 | tf_op jit(solution)/shard_map/ppermute | solution.py:1194
  70.2 24.9 %collective-permute-start.17 = (bf16[4608,256]{1,0:T(8,128)(2,1)}, bf16[4608,256]{1,0:T(8,128)(2,1)}, u32[]{:S(2)}, u32[]{:S(2)}) collective-permute-start(bf16[4608,256]{1,0:T(8,128)(2,1)} %get-tuple-element.167.refs_1_), channel_id=1, source_target_pairs={{0,1},{1,0},{2,3},{3,2},{4,5},{5,4},{6,7},{7,6},{8,9},{9,8},{10,11... | collective-permute-start | bytes 7077896 | tf_op jit(solution)/shard_map/ppermute | solution.py:1194
  92.0 13.2 %collective-permute-start.18 = (bf16[2,384,256]{2,1,0:T(8,128)(2,1)}, bf16[2,384,256]{2,1,0:T(8,128)(2,1)}, u32[]{:S(2)}, u32[]{:S(2)}) collective-permute-start(bf16[2,384,256]{2,1,0:T(8,128)(2,1)} %collective-permute-done.15.refs_13_.refs_2_), channel_id=1, source_target_pairs={{0,16},{8,24},{16,0},{24,8},{1,17},{9,25},{17,1},{25,9},{2,18},{10... | collective-permute-start | bytes 1179656 | tf_op jit(solution)/shard_map/ppermute | solution.py:1194
  105.2 27.4 %collective-permute-start.19 = (bf16[4608,256]{1,0:T(8,128)(2,1)}, bf16[4608,256]{1,0:T(8,128)(2,1)}, u32[]{:S(2)}, u32[]{:S(2)}) collective-permute-start(bf16[4608,256]{1,0:T(8,128)(2,1)} %get-tuple-element.177.refs_1_), channel_id=1, source_target_pairs={{0,1},{1,0},{2,3},{3,2},{4,5},{5,4},{6,7},{7,6},{8,9},{9,8},{10,11... | collective-permute-start | bytes 7077896 | tf_op jit(solution)/shard_map/ppermute | solution.py:1194
  128.4 22.3 %all-to-all-start = ((bf16[4,128,384]{2,1,0:T(8,128)(2,1)}), bf16[4,128,384]{2,1,0:T(8,128)(2,1)}, u32[]{:S(2)}, u32[]{:S(2)}) async-start(bf16[4,128,384]{2,1,0:T(8,128)(2,1)} %get-tuple-element.174), calls=%async_computation | async-start | bytes 786432 | tf_op jit(solution)/shard_map/all_to_all | solution.py:1509
  145.6 22.7 %collective-permute-start.21 = (bf16[3456,128]{1,0:T(8,128)(2,1)}, bf16[3456,128]{1,0:T(8,128)(2,1)}, u32[]{:S(2)}, u32[]{:S(2)}) collective-permute-start(bf16[3456,128]{1,0:T(8,128)(2,1)} %bitcast.6), channel_id=1, source_target_pairs={{0,2},{1,3},{2,0},{3,1},{4,6},{5,7},{6,4},{7,5},{8,10},{9,11},{10,... | collective-permute-start | bytes 2654216 | tf_op jit(solution)/shard_map/ppermute | solution.py:1194
  147.2 21.6 %collective-permute-start.22 = (bf16[3456,128]{1,0:T(8,128)(2,1)}, bf16[3456,128]{1,0:T(8,128)(2,1)}, u32[]{:S(2)}, u32[]{:S(2)}) collective-permute-start(bf16[3456,128]{1,0:T(8,128)(2,1)} %bitcast.8), channel_id=1, source_target_pairs={{0,8},{8,0},{16,24},{24,16},{1,9},{9,1},{17,25},{25,17},{2,10},{10... | collective-permute-start | bytes 2654216 | tf_op jit(solution)/shard_map/ppermute | solution.py:1194
  149.2 26.7 %collective-permute-start.23 = (bf16[3456,128]{1,0:T(8,128)(2,1)}, bf16[3456,128]{1,0:T(8,128)(2,1)}, u32[]{:S(2)}, u32[]{:S(2)}) collective-permute-start(bf16[3456,128]{1,0:T(8,128)(2,1)} %bitcast.10), channel_id=1, source_target_pairs={{0,16},{8,24},{16,0},{24,8},{1,17},{9,25},{17,1},{25,9},{2,18},{10... | collective-permute-start | bytes 2654216 | tf_op jit(solution)/shard_map/ppermute | solution.py:1194
  163.9 23.0 %all-to-all-start.1 = ((bf16[4,384,384]{2,1,0:T(8,128)(2,1)}), bf16[4,384,384]{2,1,0:T(8,128)(2,1)}, u32[]{:S(2)}, u32[]{:S(2)}) async-start(bf16[4,384,384]{2,1,0:T(8,128)(2,1)} %get-tuple-element.181.refs_5_), calls=%async_computation.1 | async-start | bytes 2359296 | tf_op jit(solution)/shard_map/all_to_all | solution.py:1509
  183.6 22.0 %collective-permute-start.27 = (bf16[1728,128]{1,0:T(8,128)(2,1)}, bf16[1728,128]{1,0:T(8,128)(2,1)}, u32[]{:S(2)}, u32[]{:S(2)}) collective-permute-start(bf16[1728,128]{1,0:T(8,128)(2,1)} %get-tuple-element.203), channel_id=1, source_target_pairs={{0,1},{1,0},{2,3},{3,2},{4,5},{5,4},{6,7},{7,6},{8,9},{9,8},{10,11... | collective-permute-start | bytes 1327112 | tf_op jit(solution)/shard_map/ppermute | solution.py:1194
  183.6 22.0 %collective-permute-start.24 = (bf16[1728,128]{1,0:T(8,128)(2,1)}, bf16[1728,128]{1,0:T(8,128)(2,1)}, u32[]{:S(2)}, u32[]{:S(2)}) collective-permute-start(bf16[1728,128]{1,0:T(8,128)(2,1)} %get-tuple-element.199), channel_id=1, source_target_pairs={{0,8},{8,0},{16,24},{24,16},{1,9},{9,1},{17,25},{25,17},{2,10},{10... | collective-permute-start | bytes 1327112 | tf_op jit(solution)/shard_map/ppermute | solution.py:1194
  183.7 22.0 %collective-permute-start.25 = (bf16[1728,128]{1,0:T(8,128)(2,1)}, bf16[1728,128]{1,0:T(8,128)(2,1)}, u32[]{:S(2)}, u32[]{:S(2)}) collective-permute-start(bf16[1728,128]{1,0:T(8,128)(2,1)} %get-tuple-element.200), channel_id=1, source_target_pairs={{0,16},{8,24},{16,0},{24,8},{1,17},{9,25},{17,1},{25,9},{2,18},{10... | collective-permute-start | bytes 1327112 | tf_op jit(solution)/shard_map/ppermute | solution.py:1194
  186.6 19.0 %collective-permute-start.26 = (bf16[1728,128]{1,0:T(8,128)(2,1)}, bf16[1728,128]{1,0:T(8,128)(2,1)}, u32[]{:S(2)}, u32[]{:S(2)}) collective-permute-start(bf16[1728,128]{1,0:T(8,128)(2,1)} %get-tuple-element.201), channel_id=1, source_target_pairs={{0,2},{1,3},{2,0},{3,1},{4,6},{5,7},{6,4},{7,5},{8,10},{9,11},{10,... | collective-permute-start | bytes 1327112 | tf_op jit(solution)/shard_map/ppermute | solution.py:1194
  201.3 30.6 %all-to-all-start.2 = ((bf16[4,128,384]{2,1,0:T(8,128)(2,1)}), bf16[4,128,384]{2,1,0:T(8,128)(2,1)}, u32[]{:S(2)}, u32[]{:S(2)}) async-start(bf16[4,128,384]{2,1,0:T(8,128)(2,1)} %get-tuple-element.196), calls=%async_computation.2 | async-start | bytes 786432 | tf_op jit(solution)/shard_map/all_to_all | solution.py:1509
  205.6 10.7 %collective-permute-start.32 = (bf16[256,2304]{1,0:T(8,128)(2,1)}, bf16[256,2304]{1,0:T(8,128)(2,1)}, u32[]{:S(2)}, u32[]{:S(2)}) collective-permute-start(bf16[256,2304]{1,0:T(8,128)(2,1)} %get-tuple-element.210), channel_id=1, source_target_pairs={{0,1},{1,0},{2,3},{3,2},{4,5},{5,4},{6,7},{7,6},{8,9},{9,8},{10,11... | collective-permute-start | bytes 3538952 | tf_op jit(solution)/shard_map/ppermute | solution.py:1194
  208.5 20.1 %collective-permute-start.28 = (bf16[864,128]{1,0:T(8,128)(2,1)}, bf16[864,128]{1,0:T(8,128)(2,1)}, u32[]{:S(2)}, u32[]{:S(2)}) collective-permute-start(bf16[864,128]{1,0:T(8,128)(2,1)} %get-tuple-element.205), channel_id=1, source_target_pairs={{0,16},{8,24},{16,0},{24,8},{1,17},{9,25},{17,1},{25,9},{2,18},{10... | collective-permute-start | bytes 663560 | tf_op jit(solution)/shard_map/ppermute | solution.py:1194
  210.5 18.7 %collective-permute-start.29 = (bf16[864,128]{1,0:T(8,128)(2,1)}, bf16[864,128]{1,0:T(8,128)(2,1)}, u32[]{:S(2)}, u32[]{:S(2)}) collective-permute-start(bf16[864,128]{1,0:T(8,128)(2,1)} %get-tuple-element.206), channel_id=1, source_target_pairs={{0,8},{8,0},{16,24},{24,16},{1,9},{9,1},{17,25},{25,17},{2,10},{10... | collective-permute-start | bytes 663560 | tf_op jit(solution)/shard_map/ppermute | solution.py:1194
  212.0 17.3 %collective-permute-start.30 = (bf16[864,128]{1,0:T(8,128)(2,1)}, bf16[864,128]{1,0:T(8,128)(2,1)}, u32[]{:S(2)}, u32[]{:S(2)}) collective-permute-start(bf16[864,128]{1,0:T(8,128)(2,1)} %get-tuple-element.207), channel_id=1, source_target_pairs={{0,2},{1,3},{2,0},{3,1},{4,6},{5,7},{6,4},{7,5},{8,10},{9,11},{10,... | collective-permute-start | bytes 663560 | tf_op jit(solution)/shard_map/ppermute | solution.py:1194
  213.7 15.7 %collective-permute-start.31 = (bf16[864,128]{1,0:T(8,128)(2,1)}, bf16[864,128]{1,0:T(8,128)(2,1)}, u32[]{:S(2)}, u32[]{:S(2)}) collective-permute-start(bf16[864,128]{1,0:T(8,128)(2,1)} %get-tuple-element.208), channel_id=1, source_target_pairs={{0,4},{1,5},{2,6},{3,7},{4,0},{5,1},{6,2},{7,3},{8,12},{9,13},{10,... | collective-permute-start | bytes 663560 | tf_op jit(solution)/shard_map/ppermute | solution.py:1194
  228.2 21.2 %collective-permute-start.33 = (bf16[3456,128]{1,0:T(8,128)(2,1)}, bf16[3456,128]{1,0:T(8,128)(2,1)}, u32[]{:S(2)}, u32[]{:S(2)}) collective-permute-start(bf16[3456,128]{1,0:T(8,128)(2,1)} %bitcast.12), channel_id=1, source_target_pairs={{0,2},{1,3},{2,0},{3,1},{4,6},{5,7},{6,4},{7,5},{8,10},{9,11},{10,... | collective-permute-start | bytes 2654216 | tf_op jit(solution)/shard_map/ppermute | solution.py:1194
  228.6 20.9 %collective-permute-start.34 = (bf16[3456,128]{1,0:T(8,128)(2,1)}, bf16[3456,128]{1,0:T(8,128)(2,1)}, u32[]{:S(2)}, u32[]{:S(2)}) collective-permute-start(bf16[3456,128]{1,0:T(8,128)(2,1)} %bitcast.14), channel_id=1, source_target_pairs={{0,8},{8,0},{16,24},{24,16},{1,9},{9,1},{17,25},{25,17},{2,10},{10... | collective-permute-start | bytes 2654216 | tf_op jit(solution)/shard_map/ppermute | solution.py:1194
  229.2 20.7 %collective-permute-start.35 = (bf16[3456,128]{1,0:T(8,128)(2,1)}, bf16[3456,128]{1,0:T(8,128)(2,1)}, u32[]{:S(2)}, u32[]{:S(2)}) collective-permute-start(bf16[3456,128]{1,0:T(8,128)(2,1)} %bitcast.16), channel_id=1, source_target_pairs={{0,16},{8,24},{16,0},{24,8},{1,17},{9,25},{17,1},{25,9},{2,18},{10... | collective-permute-start | bytes 2654216 | tf_op jit(solution)/shard_map/ppermute | solution.py:1194
  245.0 20.8 %all-to-all-start.3 = ((bf16[4,384,384]{2,1,0:T(8,128)(2,1)}), bf16[4,384,384]{2,1,0:T(8,128)(2,1)}, u32[]{:S(2)}, u32[]{:S(2)}) async-start(bf16[4,384,384]{2,1,0:T(8,128)(2,1)} %get-tuple-element.214.refs_5_), calls=%async_computation.3 | async-start | bytes 2359296 | tf_op jit(solution)/shard_map/all_to_all | solution.py:1509
  257.6 15.8 %collective-permute-start.40 = (bf16[1728,128]{1,0:T(8,128)(2,1)}, bf16[1728,128]{1,0:T(8,128)(2,1)}, u32[]{:S(2)}, u32[]{:S(2)}) collective-permute-start(bf16[1728,128]{1,0:T(8,128)(2,1)} %get-tuple-element.235), channel_id=1, source_target_pairs={{0,1},{1,0},{2,3},{3,2},{4,5},{5,4},{6,7},{7,6},{8,9},{9,8},{10,11... | collective-permute-start | bytes 1327112 | tf_op jit(solution)/shard_map/ppermute | solution.py:1194
  257.6 16.2 %collective-permute-start.37 = (bf16[1728,128]{1,0:T(8,128)(2,1)}, bf16[1728,128]{1,0:T(8,128)(2,1)}, u32[]{:S(2)}, u32[]{:S(2)}) collective-permute-start(bf16[1728,128]{1,0:T(8,128)(2,1)} %get-tuple-element.231), channel_id=1, source_target_pairs={{0,8},{8,0},{16,24},{24,16},{1,9},{9,1},{17,25},{25,17},{2,10},{10... | collective-permute-start | bytes 1327112 | tf_op jit(solution)/shard_map/ppermute | solution.py:1194
  259.1 14.8 %collective-permute-start.38 = (bf16[1728,128]{1,0:T(8,128)(2,1)}, bf16[1728,128]{1,0:T(8,128)(2,1)}, u32[]{:S(2)}, u32[]{:S(2)}) collective-permute-start(bf16[1728,128]{1,0:T(8,128)(2,1)} %get-tuple-element.232), channel_id=1, source_target_pairs={{0,16},{8,24},{16,0},{24,8},{1,17},{9,25},{17,1},{25,9},{2,18},{10... | collective-permute-start | bytes 1327112 | tf_op jit(solution)/shard_map/ppermute | solution.py:1194
  260.5 13.4 %collective-permute-start.39 = (bf16[1728,128]{1,0:T(8,128)(2,1)}, bf16[1728,128]{1,0:T(8,128)(2,1)}, u32[]{:S(2)}, u32[]{:S(2)}) collective-permute-start(bf16[1728,128]{1,0:T(8,128)(2,1)} %get-tuple-element.233), channel_id=1, source_target_pairs={{0,2},{1,3},{2,0},{3,1},{4,6},{5,7},{6,4},{7,5},{8,10},{9,11},{10,... | collective-permute-start | bytes 1327112 | tf_op jit(solution)/shard_map/ppermute | solution.py:1194
  272.6 8.4 %collective-permute-start.36 = (f32[1,23808]{1,0:T(1,128)}, f32[1,23808]{1,0:T(1,128)}, u32[]{:S(2)}, u32[]{:S(2)}) collective-permute-start(f32[1,23808]{1,0:T(1,128)} %get-tuple-element.230.refs_0_), channel_id=1, source_target_pairs={{0,8},{8,0},{16,24},{24,16},{1,9},{9,1},{17,25},{25,17},{2,10},{10... | collective-permute-start | bytes 285704 | tf_op jit(solution)/shard_map/ppermute | solution.py:1194
  276.7 15.9 %collective-permute-start.43 = (bf16[864,128]{1,0:T(8,128)(2,1)}, bf16[864,128]{1,0:T(8,128)(2,1)}, u32[]{:S(2)}, u32[]{:S(2)}) collective-permute-start(bf16[864,128]{1,0:T(8,128)(2,1)} %get-tuple-element.241), channel_id=1, source_target_pairs={{0,16},{8,24},{16,0},{24,8},{1,17},{9,25},{17,1},{25,9},{2,18},{10... | collective-permute-start | bytes 663560 | tf_op jit(solution)/shard_map/ppermute | solution.py:1194
  278.5 14.2 %collective-permute-start.44 = (bf16[864,128]{1,0:T(8,128)(2,1)}, bf16[864,128]{1,0:T(8,128)(2,1)}, u32[]{:S(2)}, u32[]{:S(2)}) collective-permute-start(bf16[864,128]{1,0:T(8,128)(2,1)} %get-tuple-element.242), channel_id=1, source_target_pairs={{0,8},{8,0},{16,24},{24,16},{1,9},{9,1},{17,25},{25,17},{2,10},{10... | collective-permute-start | bytes 663560 | tf_op jit(solution)/shard_map/ppermute | solution.py:1194
  279.0 13.7 %collective-permute-start.45 = (bf16[864,128]{1,0:T(8,128)(2,1)}, bf16[864,128]{1,0:T(8,128)(2,1)}, u32[]{:S(2)}, u32[]{:S(2)}) collective-permute-start(bf16[864,128]{1,0:T(8,128)(2,1)} %get-tuple-element.243), channel_id=1, source_target_pairs={{0,2},{1,3},{2,0},{3,1},{4,6},{5,7},{6,4},{7,5},{8,10},{9,11},{10,... | collective-permute-start | bytes 663560 | tf_op jit(solution)/shard_map/ppermute | solution.py:1194
  280.6 26.8 %collective-permute-start.46 = (bf16[864,128]{1,0:T(8,128)(2,1)}, bf16[864,128]{1,0:T(8,128)(2,1)}, u32[]{:S(2)}, u32[]{:S(2)}) collective-permute-start(bf16[864,128]{1,0:T(8,128)(2,1)} %get-tuple-element.244), channel_id=1, source_target_pairs={{0,4},{1,5},{2,6},{3,7},{4,0},{5,1},{6,2},{7,3},{8,12},{9,13},{10,... | collective-permute-start | bytes 663560 | tf_op jit(solution)/shard_map/ppermute | solution.py:1194
  287.1 41.2 %collective-permute-start.50 = (bf16[1296,128]{1,0:T(8,128)(2,1)}, bf16[1296,128]{1,0:T(8,128)(2,1)}, u32[]{:S(2)}, u32[]{:S(2)}) collective-permute-start(bf16[1296,128]{1,0:T(8,128)(2,1)} %get-tuple-element.250), channel_id=1, source_target_pairs={{0,4},{1,5},{2,6},{3,7},{4,0},{5,1},{6,2},{7,3},{8,12},{9,13},{10,... | collective-permute-start | bytes 995336 | tf_op jit(solution)/shard_map/ppermute | solution.py:1194
  292.6 17.4 %collective-permute-start.42 = (f32[1,23936]{1,0:T(1,128)}, f32[1,23936]{1,0:T(1,128)}, u32[]{:S(2)}, u32[]{:S(2)}) collective-permute-start(f32[1,23936]{1,0:T(1,128)} %get-tuple-element.240.refs_0_), channel_id=1, source_target_pairs={{0,1},{1,0},{2,3},{3,2},{4,5},{5,4},{6,7},{7,6},{8,9},{9,8},{10,11... | collective-permute-start | bytes 287240 | tf_op jit(solution)/shard_map/ppermute | solution.py:1194
  310.0 18.4 %collective-permute-start.49 = (bf16[1296,128]{1,0:T(8,128)(2,1)}, bf16[1296,128]{1,0:T(8,128)(2,1)}, u32[]{:S(2)}, u32[]{:S(2)}) collective-permute-start(bf16[1296,128]{1,0:T(8,128)(2,1)} %get-tuple-element.249), channel_id=1, source_target_pairs={{0,4},{1,5},{2,6},{3,7},{4,0},{5,1},{6,2},{7,3},{8,12},{9,13},{10,... | collective-permute-start | bytes 995336 | tf_op jit(solution)/shard_map/ppermute | solution.py:1194
  311.6 14.6 %collective-permute-start.47 = (f32[1,33280]{1,0:T(1,128)S(1)}, f32[1,33280]{1,0:T(1,128)S(1)}, u32[]{:S(2)}, u32[]{:S(2)}) collective-permute-start(f32[1,33280]{1,0:T(1,128)S(1)} %get-tuple-element.247.refs_0_), channel_id=1, source_target_pairs={{0,2},{1,3},{2,0},{3,1},{4,6},{5,7},{6,4},{7,5},{8,10},{9,11},{10,... | collective-permute-start | bytes 399368 | tf_op jit(solution)/shard_map/ppermute | solution.py:1194
  326.2 11.5 %collective-permute-start.48 = (f32[1,51968]{1,0:T(1,128)S(1)}, f32[1,51968]{1,0:T(1,128)S(1)}, u32[]{:S(2)}, u32[]{:S(2)}) collective-permute-start(f32[1,51968]{1,0:T(1,128)S(1)} %get-tuple-element.248.refs_1_), channel_id=1, source_target_pairs={{0,4},{1,5},{2,6},{3,7},{4,0},{5,1},{6,2},{7,3},{8,12},{9,13},{10,... | collective-permute-start | bytes 623624 | tf_op jit(solution)/shard_map/ppermute | solution.py:1194
  326.3 13.0 %collective-permute-start.53 = (bf16[432,128]{1,0:T(8,128)(2,1)}, bf16[432,128]{1,0:T(8,128)(2,1)}, u32[]{:S(2)}, u32[]{:S(2)}) collective-permute-start(bf16[432,128]{1,0:T(8,128)(2,1)} %get-tuple-element.259), channel_id=1, source_target_pairs={{0,2},{1,3},{2,0},{3,1},{4,6},{5,7},{6,4},{7,5},{8,10},{9,11},{10,... | collective-permute-start | bytes 331784 | tf_op jit(solution)/shard_map/ppermute | solution.py:1194
  (64 other events, 678.0 us)
